TPU v7x, 32 devices: a whole 2x2x4 slice. The times are simulated.
32 devices in a mesh: replica: 4 (over y, x), fsdp: 8 (over z, core).
Axes of the slice: x: 2, y: 2, z: 4, core: 2. Of those that a mesh axis runs over, the one named last changes fastest.
Arguments:
- tokens: bfloat16 [32768, 1280], P(('replica', 'fsdp')), may hold values from -6 to 6
- lengths: int32 [32], P(('replica', 'fsdp')), may hold values from 256 to 1024, as said below
- cotangent: bfloat16 [32768, 1280], P(('replica', 'fsdp')), may hold values from -6 to 6
- query_weight: bfloat16 [1280, 1280], P('fsdp'), may hold values from -0.15625 to 0.15625
- key_weight: bfloat16 [1280, 1280], P('fsdp'), may hold values from -0.15625 to 0.15625
- value_weight: bfloat16 [1280, 1280], P('fsdp'), may hold values from -0.15625 to 0.15625
- output_weight: bfloat16 [1280, 1280], P('fsdp'), may hold values from -1.25 to 1.25
- up_weight: bfloat16 [1280, 1280], P('fsdp'), may hold values from -0.15625 to 0.15625
- down_weight: bfloat16 [1280, 1280], P('fsdp'), may hold values from -0.15625 to 0.15625
- attn_gain: bfloat16 [1280], P('fsdp'), may hold values from 0.099609375 to 1.8984375
- mlp_gain: bfloat16 [1280], P('fsdp'), may hold values from 0.099609375 to 1.8984375
- up_bias: bfloat16 [1280], P('fsdp'), may hold values from -3 to 3
- down_bias: bfloat16 [1280], P('fsdp'), may hold values from -1.796875 to 1.796875
- query_scale: bfloat16 [80], replicated, may hold values from 0.5 to 2
Outputs:
- output: bfloat16 [32768, 1280], P(('replica', 'fsdp'))
- input_grad: bfloat16 [32768, 1280], P(('replica', 'fsdp'))
- query_grad: float32 [1280, 1280], P('fsdp')
- key_grad: float32 [1280, 1280], P('fsdp')
- value_grad: float32 [1280, 1280], P('fsdp')
- output_grad: float32 [1280, 1280], P('fsdp')
- up_grad: float32 [1280, 1280], P('fsdp')
- down_grad: float32 [1280, 1280], P('fsdp')
- attn_gain_grad: float32 [1280], P('fsdp')
- mlp_gain_grad: float32 [1280], P('fsdp')
- up_bias_grad: float32 [1280], P('fsdp')
- down_bias_grad: float32 [1280], P('fsdp')
- scale_grad: float32 [80], replicated
Inputs may be any that keep to these rules, and one draw needn't show every extreme that they name: `lengths`: valid tokens of each slot; some slot has exactly 1024 and some exactly 256.
All inputs are finite; a program needn't handle non-finite values.
Results may differ from a plain program's by a relative error of at most 0.017.
Values may be sent and summed in bfloat16 or wider, within the bound.
No kernel may reach another device: no remote copies, remote signals or barrier semaphores. Data moves between devices by JAX's collectives and lax.ppermute only.
A program may use at most 384 MiB of HBM per device.

v0:
```python
import functools
import math

import jax
import jax.numpy as jnp
from jax import lax
from jax.experimental import pallas as pl
from jax.experimental.pallas import tpu as pltpu
from jax.sharding import PartitionSpec as P

D = 1280
HEADS = 16
HD = 80
FF = 1280
SEQ = 1024
EPS = 1e-06
LOG2E = math.log2(math.e)
NEG = -1e30
LANES = 128
BLOCK = 256
GROUP = 8
HALF = GROUP * HD
TRIPLE = 3 * HALF
VMEM_LIMIT = 58 << 20
SHORT = 40

bf16 = jnp.bfloat16
f32 = jnp.float32


def rms_parts(v):
    inverse = lax.rsqrt(jnp.mean(v * v, axis=-1, keepdims=True) + EPS)
    return (v * inverse, inverse)


def rms_back(grad_n, normed, inverse):
    return inverse * (grad_n - normed * jnp.mean(grad_n * normed, axis=-1, keepdims=True))


def nt(a, b):
    return lax.dot_general(a, b, (((1,), (1,)), ((), ())), preferred_element_type=f32)


def nn(a, b):
    return lax.dot_general(a, b, (((1,), (0,)), ((), ())), preferred_element_type=f32)


def tn(a, b):
    return lax.dot_general(a, b, (((0,), (0,)), ((), ())), preferred_element_type=f32)


def widen(v):
    return jnp.pad(v, ((0, 0), (0, LANES - HD)))


def split3(v):
    a = v.astype(bf16).astype(f32)
    b = (v - a).astype(bf16).astype(f32)
    c = (v - a - b).astype(bf16).astype(f32)
    return a, b, c


def extra_lanes(lane, base, extra):
    out = jnp.zeros_like(base)
    for place, value in reversed(list(enumerate(extra))):
        out = jnp.where(lane == HD + place, value, out)
    return jnp.where(lane < HD, base, out)


def forward_kernel(heads, len_ref, qkv_ref, o_ref, qa_ref, ka_ref, va_ref):
    length = len_ref[0]
    lane = lax.broadcasted_iota(jnp.int32, (SEQ, LANES), 1)
    row = lax.broadcasted_iota(jnp.int32, (SEQ, LANES), 0)
    mask = jnp.where(row < length, 0.0, NEG)
    k_pad = jnp.where(lane == HD, mask, jnp.where((lane > HD) & (lane < HD + 4), 1.0, 0.0)).astype(bf16)
    v_pad = jnp.where((lane >= HD) & (lane < HD + 3), 1.0, 0.0).astype(bf16)
    q_pad = jnp.where(lane == HD, 1.0, 0.0).astype(bf16)
    in_head = lane < HD
    block_lane = lane[:BLOCK]
    block_row = lax.broadcasted_iota(jnp.int32, (LANES, BLOCK), 0)
    causal = lax.broadcasted_iota(jnp.int32, (BLOCK, BLOCK), 0) <= lax.broadcasted_iota(
        jnp.int32, (BLOCK, BLOCK), 1
    )
    blocks = SEQ // BLOCK

    def prepare(h):
        for n, (ref, pad) in enumerate(((qa_ref, q_pad), (ka_ref, k_pad), (va_ref, v_pad))):
            at = n * HALF + h * HD
            ref[h] = jnp.where(in_head, widen(qkv_ref[:, at : at + HD]), pad)

    def scores(h, i):
        return nt(ka_ref[h, : (i + 1) * BLOCK, :], qa_ref[h, i * BLOCK : (i + 1) * BLOCK, :])

    def attend(h, i, st):
        before = i * BLOCK
        diagonal = jnp.where(causal, st[before:], NEG)
        top = jnp.max(diagonal, axis=0, keepdims=True)
        if i:
            top = jnp.maximum(top, jnp.max(st[:before], axis=0, keepdims=True))
        p = jnp.exp2(diagonal - top).astype(bf16)
        if i:
            p = jnp.concatenate([jnp.exp2(st[:before] - top).astype(bf16), p], axis=0)
        return tn(va_ref[h, : before + BLOCK, :], p), top

    def finish(h, i, ot, top):
        rows = slice(i * BLOCK, (i + 1) * BLOCK)
        total = ot[HD : HD + 1]
        a, b, c = split3(-(top + jnp.log2(total)))
        scaled = jnp.where(block_row < HD, ot / total, 0.0)
        for place, value in ((1, a), (2, b), (3, c)):
            scaled = jnp.where(block_row == HD + place, value, scaled)
        o = scaled.T
        o_ref[rows, h * HD : (h + 1) * HD] = o[:, :HD].astype(bf16)
        qa_ref[h, rows, :] = jnp.where(block_lane <= HD, qa_ref[h, rows, :].astype(f32), o).astype(bf16)

    for h in range(heads):
        prepare(h)
    scored, done = [], []
    for h, i in [(h, i) for h in range(heads) for i in range(blocks)] + [(None, None)] * 2:
        if h is not None:
            scored.append((h, i, scores(h, i)))
        if len(scored) > 1 or (h is None and scored):
            hh, ii, st = scored.pop(0)
            done.append((hh, ii, *attend(hh, ii, st)))
        if len(done) > 1 or (h is None and not scored and done):
            finish(*done.pop(0))
    while done:
        finish(*done.pop(0))


def attend_forward(half, lengths, qkv, before=None):
    wide = pl.BlockSpec((GROUP, SEQ, LANES), lambda g: (0, 0, 0))
    kept = [] if before is None else [before]

    def kernel(len_ref, qkv_ref, *refs):
        forward_kernel(GROUP, len_ref, qkv_ref, *refs[len(kept) :])

    return pl.pallas_call(
        kernel,
        grid=(1,),
        in_specs=[pl.BlockSpec(memory_space=pltpu.SMEM), pl.BlockSpec((SEQ, TRIPLE), lambda g: (0, 0))]
        + [pl.BlockSpec(memory_space=pl.ANY)] * len(kept),
        out_specs=[pl.BlockSpec((SEQ, HALF), lambda g: (0, half)), wide, wide, wide],
        out_shape=[jax.ShapeDtypeStruct((SEQ, D), bf16)]
        + [jax.ShapeDtypeStruct((GROUP, SEQ, LANES), bf16)] * 3,
        input_output_aliases={2: 0} if kept else {},
        compiler_params=pltpu.CompilerParams(vmem_limit_bytes=VMEM_LIMIT),
        cost_estimate=pl.CostEstimate(
            flops=GROUP * SEQ * SEQ * 1200 // SHORT, bytes_accessed=0, transcendentals=0
        ),
        name="attend_forward",
    )(lengths, qkv, *kept)


def backward_kernel(
    heads, fac_ref, qa_ref, ka_ref, va_ref, o_ref, g_ref, d_ref, sg_ref, dqs, gs
):
    lane = lax.broadcasted_iota(jnp.int32, (SEQ, LANES), 1)
    causal = lax.broadcasted_iota(jnp.int32, (BLOCK, BLOCK), 0) <= lax.broadcasted_iota(
        jnp.int32, (BLOCK, BLOCK), 1
    )
    fac = fac_ref[0:1, :]
    blocks = SEQ // BLOCK

    @pl.when(pl.program_id(0) == 0)
    def _():
        sg_ref[...] = jnp.zeros_like(sg_ref)

    sums = []

    def prepare(h):
        own = slice(h * HD, (h + 1) * HD)
        g = widen(g_ref[:, own]).astype(f32)
        o = widen(o_ref[:, own]).astype(f32)
        delta = jnp.sum(g * o, axis=1, keepdims=True)
        gs[h] = extra_lanes(lane, g, split3(-delta)).astype(bf16)

    def products(h, j):
        js = slice(j * BLOCK, (j + 1) * BLOCK)
        return nt(ka_ref[h, js, :], qa_ref[h, j * BLOCK :, :]), nt(va_ref[h, js, :], gs[h, j * BLOCK :, :])

    def middle(j, st, dpt):
        p = jnp.exp2(st)
        diagonal = jnp.where(causal, p[:, :BLOCK], 0.0)
        p = jnp.concatenate([diagonal, p[:, BLOCK:]], axis=1) if j < blocks - 1 else diagonal
        return (p * dpt).astype(bf16), p.astype(bf16)

    def finish(h, j, ds, p):
        own, dk, dv = (slice(n * HALF + h * HD, n * HALF + (h + 1) * HD) for n in range(3))
        js = slice(j * BLOCK, (j + 1) * BLOCK)
        d_ref[js, dv] = nn(p, gs[h, j * BLOCK :, :])[:, :HD].astype(bf16)
        d_ref[js, dk] = (nn(ds, qa_ref[h, j * BLOCK :, :])[:, :HD] * (1.0 / LOG2E)).astype(bf16)
        dqt = tn(ka_ref[h, js, :], ds)
        if j == 0:
            dqs[h % 2] = dqt
        else:
            dqs[h % 2, :, j * BLOCK :] += dqt
        if j == blocks - 1:
            dq = dqs[h % 2].T.astype(bf16).astype(f32)
            sums.append(jnp.sum(dq * qa_ref[h].astype(f32), axis=0, keepdims=True))
            d_ref[:, own] = (dq * fac)[:, :HD].astype(bf16)

    for h in range(heads):
        prepare(h)
    waiting = []
    for h, j in [(h, j) for h in range(heads) for j in range(blocks)]:
        waiting.append((h, j, *products(h, j)))
        if len(waiting) > 1:
            hh, jj, st, dpt = waiting.pop(0)
            finish(hh, jj, *middle(jj, st, dpt))
    hh, jj, st, dpt = waiting.pop(0)
    finish(hh, jj, *middle(jj, st, dpt))
    sg_ref[0:1, :] += sum(sums)


def attend_backward(half, fac, qa, ka, va, o, g):
    part = pl.BlockSpec((SEQ, HALF), lambda g: (0, half))
    wide = pl.BlockSpec((GROUP, SEQ, LANES), lambda g: (0, 0, 0))
    full = pl.BlockSpec((8, LANES), lambda g: (0, 0))
    return pl.pallas_call(
        functools.partial(backward_kernel, GROUP),
        grid=(1,),
        in_specs=[full, wide, wide, wide, part, part],
        out_specs=[pl.BlockSpec((SEQ, TRIPLE), lambda g: (0, 0)), full],
        out_shape=[jax.ShapeDtypeStruct((SEQ, TRIPLE), bf16), jax.ShapeDtypeStruct((8, LANES), f32)],
        scratch_shapes=[pltpu.VMEM((2, LANES, SEQ), f32), pltpu.VMEM((GROUP, SEQ, LANES), bf16)],
        compiler_params=pltpu.CompilerParams(vmem_limit_bytes=VMEM_LIMIT),
        cost_estimate=pl.CostEstimate(
            flops=GROUP * SEQ * SEQ * 2400 // SHORT, bytes_accessed=0, transcendentals=0
        ),
        name="attend_backward",
    )(fac, qa, ka, va, o, g)


class Grid:
    def __init__(self, mesh_shape):
        self.copies, self.owners = mesh_shape["replica"], mesh_shape["fsdp"]
        self.planes = self.owners // 2
        self.rows = D // self.owners

    @property
    def pieced(self):
        return self.copies == 4 and self.owners == 8

    def place(self):
        me, copy = lax.axis_index("fsdp"), lax.axis_index("replica")
        return copy // 2, copy % 2, me // 2, me % 2

    def along_z(self, v, step):
        n = self.planes
        pairs = [(i, (i // 2 + step) % n * 2 + i % 2) for i in range(self.owners)]
        return lax.ppermute(v, "fsdp", pairs)

    def other_core(self, v):
        return lax.ppermute(v, "fsdp", [(i, i ^ 1) for i in range(self.owners)])

    def across(self, v, code):
        return lax.ppermute(v, "replica", [(i, i ^ code) for i in range(self.copies)])


def kernel_call(kernel, name, operands, outs, scratch=(), flops=0, nbytes=0, **more):
    return pl.pallas_call(
        kernel,
        out_shape=outs,
        scratch_shapes=scratch,
        compiler_params=pltpu.CompilerParams(vmem_limit_bytes=VMEM_LIMIT),
        cost_estimate=pl.CostEstimate(flops=flops // SHORT, bytes_accessed=nbytes // SHORT, transcendentals=0),
        name=name,
        **more,
    )(*operands)


def piece_copies(planes, quarter, place_ref, refs, buf, sem):
    y, x, z, core = (place_ref[i] for i in range(4))
    groups = []
    for s, (source, c) in enumerate(((refs[:5], core), (refs[5:10], 1 - core))):
        block, *pieces = source
        home = 2 * z + c
        groups.append((home, [pltpu.make_async_copy(block, buf.at[home], sem.at[s, 0, 0])]))
        for d in range(1, planes):
            owner = 2 * lax.rem(z - d + planes, planes) + c
            copies = []
            for code, piece in enumerate(pieces):
                py = 1 - y if code >= 2 else y
                px = 1 - x if code % 2 else x
                at = pl.multiple_of((2 * py + px) * quarter, 16)
                copies.append(
                    pltpu.make_async_copy(piece.at[d - 1], buf.at[owner, pl.ds(at, quarter), :], sem.at[s, d, code])
                )
            groups.append((owner, copies))
    return groups


def project_kernel(planes, rows, quarter, first, place_ref, scale_ref, x_ref, *refs):
    outs, scratch = refs[10 : 10 + (5 if first else 2)], refs[10 + (5 if first else 2) :]
    qkv_ref, whole_ref = outs[:2]
    buf, sem_in, sem_out = scratch[:3]
    groups = piece_copies(planes, quarter, place_ref, refs, buf, sem_in)
    for _, copies in groups:
        for copy in copies:
            copy.start()
    if first:
        held = scratch[3]
        for at in range(0, SEQ, BLOCK):
            held[at : at + BLOCK, :] = rms_parts(x_ref[at : at + BLOCK, :].astype(f32))[0]
    written = []
    for g, (owner, copies) in enumerate(groups):
        for copy in copies:
            copy.wait()
        at = pl.multiple_of(owner * rows, 16)
        for t in range(3):
            copy = pltpu.make_async_copy(
                buf.at[owner, pl.ds(t * rows, rows), :],
                whole_ref.at[pl.ds(at, rows), pl.ds(t * HALF, HALF)],
                sem_out.at[g, t],
            )
            copy.start()
            written.append(copy)
    if first:
        vec_ref, attn_in, left_ref = outs[2:5]
        vec_ref[...] = buf[:, 3 * rows : 3 * rows + 16, :]
        gain = jnp.concatenate([buf[b, 3 * rows : 3 * rows + 16, :rows][0:1] for b in range(2 * planes)], axis=1)
        gain = gain.astype(f32)
        for at in range(0, SEQ, BLOCK):
            attn_in[at : at + BLOCK, :] = (held[at : at + BLOCK, :] * gain).astype(bf16)
    else:
        attn_in = x_ref
    for t in range(3):
        weight = buf[:, t * rows : (t + 1) * rows, :].reshape(D, HALF)
        result = nn(attn_in[...], weight)
        qkv_ref[:, t * HALF : (t + 1) * HALF] = (result * scale_ref[0:1, :] if t == 0 else result).astype(bf16)
    if first:
        left_ref[...] = attn_in[...].T
    for copy in written:
        copy.wait()


def project(grid, place, scale, x, pieces, first):
    total = pieces[0].shape[0]
    vmem, hbm = pl.BlockSpec(memory_space=pltpu.VMEM), pl.BlockSpec(memory_space=pl.ANY)
    outs = [jax.ShapeDtypeStruct((SEQ, TRIPLE), bf16), jax.ShapeDtypeStruct((D, TRIPLE), bf16)]
    scratch = [
        pltpu.VMEM((grid.owners, total, HALF), bf16),
        pltpu.SemaphoreType.DMA((2, grid.planes, 4)),
        pltpu.SemaphoreType.DMA((grid.owners, 3)),
    ]
    if first:
        outs += [
            jax.ShapeDtypeStruct((grid.owners, 16, HALF), bf16),
            jax.ShapeDtypeStruct((SEQ, D), bf16),
            jax.ShapeDtypeStruct((D, SEQ), bf16),
        ]
        scratch.append(pltpu.VMEM((SEQ, D), f32))
    return kernel_call(
        functools.partial(project_kernel, grid.planes, grid.rows, total // 4, first),
        "project",
        (place, scale, x, *pieces),
        outs,
        scratch=scratch,
        flops=2 * SEQ * D * TRIPLE,
        nbytes=4 * D * TRIPLE + 2 * SEQ * (D + TRIPLE),
        in_specs=[pl.BlockSpec(memory_space=pltpu.SMEM), vmem, vmem] + [hbm] * 10,
        out_specs=[vmem, hbm] + [vmem] * 3 * first,
    )


def cut_kernel(rows, place_ref, *refs):
    weights, vec_ref = refs[:6], refs[6]
    chunks, pieces = refs[7:10], refs[10:13]
    for half in range(2):
        for t in range(3):
            chunks[half][t * rows : (t + 1) * rows, :] = weights[t][:, half * HALF : (half + 1) * HALF]
        chunks[half][3 * rows :, :] = vec_ref[...]
    for t in range(6):
        w, half = 3 + t // 2, t % 2
        chunks[2][t * rows : (t + 1) * rows, :] = weights[w][:, half * HALF : (half + 1) * HALF]
    copy = 2 * place_ref[0] + place_ref[1]
    for chunk, piece in zip(chunks, pieces, strict=True):
        quarter = piece.shape[0]
        piece[...] = chunk[pl.ds(pl.multiple_of(copy * quarter, 16), quarter), :]


def cut(grid, place, weights, vectors):
    rows = [512, 512, 6 * grid.rows]
    vec = jnp.pad(vectors.reshape(1, HALF), ((0, 512 - 3 * grid.rows - 1), (0, 0)))
    out = kernel_call(
        functools.partial(cut_kernel, grid.rows),
        "cut",
        (place, *weights, vec),
        [jax.ShapeDtypeStruct((n, HALF), bf16) for n in rows]
        + [jax.ShapeDtypeStruct((n // 4, HALF), bf16) for n in rows],
        nbytes=12 * grid.rows * D * 2,
        in_specs=[pl.BlockSpec(memory_space=pltpu.SMEM)] + [pl.BlockSpec(memory_space=pltpu.VMEM)] * 7,
    )
    return out[:3], out[3:]


def chunk_across(grid, along):
    return [along] + [grid.across(along, code) for code in (1, 2, 3)]


def both_cores(grid, own):
    return own + [grid.other_core(v) for v in own]


def in_blocks():
    return [slice(at, at + BLOCK) for at in range(0, SEQ, BLOCK)]


def mlp_forward_kernel(planes, rows, quarter, place_ref, gain_ref, bias_ref, *refs):
    attended_ref, token_ref, grad_ref = refs[10:13]
    weights, (hidden_ref, mlp_in_ref, pre_ref, act_ref, down_grad_ref) = refs[13:16], refs[16:21]
    buf, attended, token, grad, hidden, mlp_in, pre, act, down_grad, sem_in, sem_out, sem = refs[21:]
    loads = [
        pltpu.make_async_copy(source, target, sem.at[n])
        for n, (source, target) in enumerate(((attended_ref, attended), (token_ref, token), (grad_ref, grad)))
    ]
    groups = piece_copies(planes, quarter, place_ref, refs, buf, sem_in)
    for _, copies in groups:
        for copy in copies:
            copy.start()
    for load in loads:
        load.start()
    written = []

    def keep(source, target, n):
        copy = pltpu.make_async_copy(source, target, sem.at[n])
        copy.start()
        written.append(copy)

    for g, (owner, copies) in enumerate(groups):
        for copy in copies:
            copy.wait()
        at = pl.multiple_of(owner * rows, 16)
        for t in range(6):
            copy = pltpu.make_async_copy(
                buf.at[owner, pl.ds(t * rows, rows), :],
                weights[t // 2].at[pl.ds(at, rows), pl.ds(t % 2 * HALF, HALF)],
                sem_out.at[g, t],
            )
            copy.start()
            written.append(copy)
    for load in loads:
        load.wait()

    def tile(t):
        return buf[:, t * rows : (t + 1) * rows, :].reshape(D, HALF)

    halves = (slice(0, HALF), slice(HALF, D))
    for h, across in enumerate(halves):
        hidden[:, across] = token[:, across].astype(f32) + nn(attended[...], tile(h))
    keep(hidden, hidden_ref, 3)
    for at in in_blocks():
        mlp_in[at, :] = (rms_parts(hidden[at, :])[0] * gain_ref[0:1, :]).astype(bf16)
    keep(mlp_in, mlp_in_ref, 4)
    for h, across in enumerate(halves):
        value = nn(mlp_in[...], tile(2 + h)) + bias_ref[0:1, across]
        pre[:, across] = value
        act[:, across] = (value * jax.nn.sigmoid(value)).astype(bf16)
    keep(pre, pre_ref, 5)
    keep(act, act_ref, 6)
    down_grad[...] = tn(act[...], grad[...]).astype(bf16)
    keep(down_grad, down_grad_ref, 7)
    for copy in written:
        copy.wait()


def mlp_forward(grid, place, gain, bias, pieces, attended, tokens, grad_out_low):
    total = pieces[0].shape[0]
    vmem, hbm = pl.BlockSpec(memory_space=pltpu.VMEM), pl.BlockSpec(memory_space=pl.ANY)
    low, high, square = ((SEQ, D), bf16), ((SEQ, D), f32), ((D, D), bf16)
    outs = [square] * 3 + [high, low, high, low, square]
    return kernel_call(
        functools.partial(mlp_forward_kernel, grid.planes, grid.rows, total // 4),
        "mlp_forward",
        (place, row_of(gain), row_of(bias), *pieces, attended, tokens, grad_out_low),
        [jax.ShapeDtypeStruct(*o) for o in outs],
        scratch=[
            pltpu.VMEM((grid.owners, total, HALF), bf16),
            *[pltpu.VMEM(*v) for v in (low, low, low, high, low, high, low, square)],
            pltpu.SemaphoreType.DMA((2, grid.planes, 4)),
            pltpu.SemaphoreType.DMA((grid.owners, 6)),
            pltpu.SemaphoreType.DMA((8,)),
        ],
        flops=6 * SEQ * D * D,
        nbytes=16 * D * D + 22 * SEQ * D,
        in_specs=[pl.BlockSpec(memory_space=pltpu.SMEM), vmem, vmem] + [hbm] * 13,
        out_specs=[hbm] * 8,
    )


def row_of(v):
    return jnp.broadcast_to(v[None], (8, v.shape[0]))


def mlp_backward_kernel(gain_ref, *refs):
    grad_ref, down_ref, pre_ref, mlp_in_ref, up_ref, hidden_ref, output_ref, attended_ref = refs[:8]
    up_grad_ref, grad_hidden_ref, grad_att_ref, output_grad_ref, sums_ref = refs[8:13]
    grad, down, wide, mlp_in, up, hidden, output, attended, grad_pre, grad_proj, first, second, sem = refs[13:]
    loads = {}
    for n, (name, source, target) in enumerate(
        (
            ("grad", grad_ref, grad),
            ("down", down_ref, down),
            ("pre", pre_ref, wide),
            ("mlp_in", mlp_in_ref, mlp_in),
            ("up", up_ref, up),
            ("hidden", hidden_ref, hidden),
            ("output", output_ref, output),
            ("attended", attended_ref, attended),
        )
    ):
        loads[name] = pltpu.make_async_copy(source, target, sem.at[n])
        loads[name].start()
    written = []

    def keep(source, target):
        copy = pltpu.make_async_copy(source, target, sem.at[8 + len(written)])
        copy.start()
        written.append(copy)

    for name in ("grad", "down", "pre"):
        loads[name].wait()
    sums = jnp.zeros((1, D), f32)
    for at in in_blocks():
        pre = wide[at, :]
        sigma = jax.nn.sigmoid(pre)
        value = (nt(grad[at, :], down[...]) * (sigma * (1.0 + pre * (1.0 - sigma)))).astype(bf16)
        grad_pre[at, :] = value
        sums = sums + jnp.sum(value.astype(f32), axis=0, keepdims=True)
    sums_ref[...] = jnp.zeros_like(sums_ref)
    sums_ref[0:1, :] = sums
    sums_ref[1:2, :] = jnp.sum(grad[...].astype(f32), axis=0, keepdims=True)
    for name in ("mlp_in", "up", "hidden"):
        loads[name].wait()
    first[...] = tn(mlp_in[...], grad_pre[...]).astype(bf16)
    keep(first, up_grad_ref)
    for at in in_blocks():
        normed, inverse = rms_parts(hidden[at, :])
        back = rms_back(nt(grad_pre[at, :], up[...]) * gain_ref[0:1, :], normed, inverse)
        value = grad[at, :].astype(f32) + back
        wide[at, :] = value
        grad_proj[at, :] = value.astype(bf16)
    keep(wide, grad_hidden_ref)
    for name in ("output", "attended"):
        loads[name].wait()
    for at in in_blocks():
        mlp_in[at, :] = nt(grad_proj[at, :], output[...]).astype(bf16)
    keep(mlp_in, grad_att_ref)
    second[...] = tn(attended[...], grad_proj[...]).astype(bf16)
    keep(second, output_grad_ref)
    for copy in written:
        copy.wait()


def mlp_backward(gain, grad_out_low, w_down, pre, mlp_in, w_up, hidden1, w_out, attended):
    hbm = pl.BlockSpec(memory_space=pl.ANY)
    low, high, square = ((SEQ, D), bf16), ((SEQ, D), f32), ((D, D), bf16)
    up_grad, grad_hidden, grad_att, output_grad, sums = kernel_call(
        mlp_backward_kernel,
        "mlp_backward",
        (row_of(gain), grad_out_low, w_down, pre, mlp_in, w_up, hidden1, w_out, attended),
        [jax.ShapeDtypeStruct(*o) for o in (square, high, low, square, ((8, D), f32))],
        scratch=[
            *[pltpu.VMEM(*v) for v in (low, square, high, low, square, high, square, low, low, low, square, square)],
            pltpu.SemaphoreType.DMA((12,)),
        ],
        flops=10 * SEQ * D * D,
        nbytes=10 * D * D + 26 * SEQ * D,
        in_specs=[pl.BlockSpec(memory_space=pltpu.VMEM)] + [hbm] * 8,
        out_specs=[hbm] * 4 + [pl.BlockSpec(memory_space=pltpu.VMEM)],
    )
    return up_grad, output_grad, grad_hidden, grad_att, sums[0], sums[1]


def weight_grad_kernel(planes, rows, place_ref, left_ref, right_ref, vec_ref, mine, theirs, left, right, stage, sem_in, sem_out):
    core = place_ref[3]
    loads = [pltpu.make_async_copy(left_ref, left, sem_in.at[3])]
    for w in range(3):
        part = pl.ds(w * HALF, HALF)
        loads.append(pltpu.make_async_copy(right_ref.at[:, part], right.at[:, part], sem_in.at[w]))
    for load in loads:
        load.start()
    written = []

    def send(w, source, size, c, whole, z):
        copy = pltpu.make_async_copy(source, whole.at[z, pl.ds(w * rows, size), :], sem_out.at[w, c, z])
        copy.start()
        written.append(copy)

    sides = ((1, theirs), (0, mine))
    owner = {(c, z): 2 * z + (1 - core if c else core) for c in range(2) for z in range(planes)}
    for c, whole in sides:
        for z in range(planes):
            send(3, vec_ref.at[owner[c, z]], 32, c, whole, z)
    loads[0].wait()
    for w in range(3):
        loads[1 + w].wait()
        stage[w] = nn(left[...], right[:, w * HALF : (w + 1) * HALF]).astype(bf16)
        for c, whole in sides:
            for z in range(planes):
                at = pl.multiple_of(owner[c, z] * rows, 16)
                send(w, stage.at[w, pl.ds(at, rows), :], rows, c, whole, z)
    for copy in written:
        copy.wait()


def weight_grads(grid, place, left, right, vectors):
    rows = jnp.stack(vectors, axis=1).astype(bf16)
    rows = jnp.pad(rows, ((0, 0), (0, 32 - len(vectors)), (0, HALF - grid.rows)))
    shape = jax.ShapeDtypeStruct((grid.planes, 512, HALF), bf16)
    hbm = pl.BlockSpec(memory_space=pl.ANY)
    return kernel_call(
        functools.partial(weight_grad_kernel, grid.planes, grid.rows),
        "weight_grads",
        (place, left, right, rows),
        [shape, shape],
        scratch=[
            pltpu.VMEM((D, SEQ), bf16),
            pltpu.VMEM((SEQ, TRIPLE), bf16),
            pltpu.VMEM((3, D, HALF), bf16),
            pltpu.SemaphoreType.DMA((4,)),
            pltpu.SemaphoreType.DMA((4, 2, grid.planes)),
        ],
        flops=2 * SEQ * D * TRIPLE,
        nbytes=(SEQ * D + (SEQ + D) * TRIPLE) * 2,
        in_specs=[pl.BlockSpec(memory_space=pltpu.SMEM), hbm, hbm, pl.BlockSpec(memory_space=pltpu.VMEM)],
        out_specs=[hbm, hbm],
    )


def added(a, b):
    return (a.astype(f32) + b.astype(f32)).astype(bf16)


def fold_cores_kernel(place_ref, a_ref, b_ref, send_low, keep_low, send_high, keep_high):
    y, x = place_ref[0], place_ref[1]
    for p in range(2):
        send_low[0, p] = added(a_ref[0, p, 1 - x, 0], b_ref[0, p, 1 - x, 0])
        keep_low[0, p] = added(a_ref[0, p, x, 0], b_ref[0, p, x, 0])
        send_high[0, p] = added(a_ref[0, 1 - y, p, 1], b_ref[0, 1 - y, p, 1])
        keep_high[0, p] = added(a_ref[0, y, p, 1], b_ref[0, y, p, 1])


def fold_cores(grid, place, a, b):
    n, columns = grid.planes, a.shape[2]
    split = (n, 2, 2, 2, 64, columns)
    block = pl.BlockSpec((1, *split[1:]), lambda i: (i, 0, 0, 0, 0, 0))
    out = pl.BlockSpec((1, 2, 64, columns), lambda i: (i, 0, 0, 0))
    return kernel_call(
        fold_cores_kernel,
        "fold_cores",
        (place, a.reshape(split), b.reshape(split)),
        [jax.ShapeDtypeStruct((n, 2, 64, columns), bf16)] * 4,
        nbytes=a.size * 6,
        grid=(n,),
        in_specs=[pl.BlockSpec(memory_space=pltpu.SMEM), block, block],
        out_specs=[out] * 4,
    )


def fold_first_kernel(place_ref, low_a, low_b, high_a, high_b, send_low, keep_low, send_high, keep_high):
    y, x = place_ref[0], place_ref[1]
    send_low[0] = added(low_a[0, 1 - y], low_b[0, 1 - y])
    keep_low[0] = added(low_a[0, y], low_b[0, y])
    send_high[0] = added(high_a[0, 1 - x], high_b[0, 1 - x])
    keep_high[0] = added(high_a[0, x], high_b[0, x])


def fold_first(grid, place, *parts):
    n, columns = grid.planes, parts[0].shape[3]
    block = pl.BlockSpec((1, 2, 64, columns), lambda i: (i, 0, 0, 0))
    out = pl.BlockSpec((1, 64, columns), lambda i: (i, 0, 0))
    return kernel_call(
        fold_first_kernel,
        "fold_first",
        (place, *parts),
        [jax.ShapeDtypeStruct((n, 64, columns), bf16)] * 4,
        nbytes=parts[0].size * 12,
        grid=(n,),
        in_specs=[pl.BlockSpec(memory_space=pltpu.SMEM)] + [block] * 4,
        out_specs=[out] * 4,
    )


def fold_second_kernel(planes, place_ref, low_a, low_b, high_a, high_b, *outs):
    z = place_ref[2]
    for s in range(planes):
        at = lax.rem(z + s, planes)
        outs[s][0] = added(low_a[at], low_b[at])
        outs[s][1] = added(high_a[at], high_b[at])


def fold_second(grid, place, *parts):
    n, columns = grid.planes, parts[0].shape[2]
    return kernel_call(
        functools.partial(fold_second_kernel, n),
        "fold_second",
        (place, *parts),
        [jax.ShapeDtypeStruct((2, 64, columns), bf16)] * n,
        nbytes=parts[0].size * 12,
        in_specs=[pl.BlockSpec(memory_space=pltpu.SMEM)] + [pl.BlockSpec(memory_space=pltpu.VMEM)] * 4,
    )


def fold_planes_kernel(*refs):
    *parts, out = refs
    total = parts[0][...].astype(f32)
    for part in parts[1:]:
        total = total + part[...].astype(f32)
    out[...] = total.astype(bf16)


def fold_planes(grid, *parts):
    return kernel_call(
        fold_planes_kernel,
        "fold_planes",
        parts,
        jax.ShapeDtypeStruct(parts[0].shape, bf16),
        nbytes=parts[0].size * 10,
    )


def finish_kernel(units, rows, place_ref, *refs):
    me = 2 * place_ref[0] + place_ref[1]
    parts, outs, stage = refs[: 4 * units], refs[4 * units : -1], refs[-1]
    columns = parts[0].shape[2]
    for u in range(units):
        across = slice(u * columns, (u + 1) * columns)
        for r in range(4):
            for code in range(4):

                @pl.when(me == r ^ code)
                def _(r=r, code=code, u=u, across=across):
                    for h in range(2):
                        at = 128 * r + 64 * h
                        stage[at : at + 64, across] = parts[4 * u + code][h].astype(f32)

    for w in range(3):
        outs[w][...] = stage[w * rows : (w + 1) * rows, :]
    outs[3][...] = stage[3 * rows :, :]


def finish(grid, place, units):
    columns = units[0][0].shape[2] * len(units)
    parts = [part for unit in units for part in unit]
    return kernel_call(
        functools.partial(finish_kernel, len(units), grid.rows),
        "finish",
        (place, *parts),
        [jax.ShapeDtypeStruct((grid.rows, columns), f32)] * 3
        + [jax.ShapeDtypeStruct((512 - 3 * grid.rows, columns), f32)],
        scratch=[pltpu.VMEM((512, columns), f32)],
        nbytes=512 * columns * 6,
        in_specs=[pl.BlockSpec(memory_space=pltpu.SMEM)]
        + [pl.BlockSpec(memory_space=pltpu.VMEM)] * len(parts),
    )


def input_grad_kernel(x_ref, gain_ref, hidden_ref, grad_a, grad_b, weight_a, weight_b, out):
    total = nt(grad_a[...], weight_a[...]) + nt(grad_b[...], weight_b[...])
    normed, inverse = rms_parts(x_ref[...].astype(f32))
    out[...] = (hidden_ref[...] + rms_back(total * gain_ref[0:1, :], normed, inverse)).astype(bf16)


def input_grad_of(tokens, gain, grad_hidden, grads, weights):
    count, block = tokens.shape[0], BLOCK
    rows = pl.BlockSpec((block, D), lambda i: (i, 0))
    return kernel_call(
        input_grad_kernel,
        "input_grad",
        (tokens, jnp.broadcast_to(gain[None], (8, D)), grad_hidden, *grads, *weights),
        jax.ShapeDtypeStruct((count, D), bf16),
        flops=6 * count * D * D,
        nbytes=6 * D * D + 14 * count * D,
        grid=(count // block,),
        in_specs=[rows, pl.BlockSpec((8, D), lambda i: (0, 0)), rows]
        + [pl.BlockSpec((block, TRIPLE), lambda i: (i, 0))] * 2
        + [pl.BlockSpec((D, TRIPLE), lambda i: (0, 0))] * 2,
        out_specs=rows,
    )


def after(value, *first):
    return lax.optimization_barrier((value, first))[0]


def shards(
    grid,
    tokens,
    lengths,
    cotangent,
    query_weight,
    key_weight,
    value_weight,
    output_weight,
    up_weight,
    down_weight,
    attn_gain,
    mlp_gain,
    up_bias,
    down_bias,
    query_scale,
):
    assert lengths.shape[0] == 1 and tokens.shape[0] == SEQ
    vectors = jnp.concatenate([attn_gain, mlp_gain, up_bias, down_bias])
    y, x, z, core = grid.place()
    place = jnp.stack([y, x, z, core]).astype(jnp.int32)
    xin = tokens.astype(f32)
    factor = query_scale.astype(f32) * (1.0 / jnp.sqrt(f32(HD)))
    scale_half = row_of(jnp.tile(factor * LOG2E, GROUP))
    valid = (jnp.arange(SEQ, dtype=jnp.int32) < lengths[0]).reshape(-1, 1)
    grad_out_low = jnp.where(valid, cotangent, jnp.zeros_like(cotangent))
    if grid.pieced:
        weights = (query_weight, key_weight, value_weight, output_weight, up_weight, down_weight)
        chunks, cuts = cut(grid, place, weights, vectors)
        planes = range(1, grid.planes)
        z1 = [grid.along_z(cuts[0], d) for d in planes]
        z2 = [grid.along_z(after(cuts[1], *z1), d) for d in planes]
        across1 = chunk_across(grid, jnp.stack(z1))
        across2 = chunk_across(grid, jnp.stack(after(z2, *z1)))
        z3 = [grid.along_z(after(cuts[2], *z2), d) for d in planes]
        qkv_a, wa, vecs, attn_in, left = project(
            grid, place, scale_half, tokens, both_cores(grid, [chunks[0], *across1]), True
        )
        vecs = vecs[:, 0].reshape(grid.owners, 4, grid.rows)
        qkv_a, z3 = after((qkv_a, z3), wa)
        attended, *kept_a = attend_forward(0, lengths, qkv_a)
        across3 = chunk_across(grid, jnp.stack(z3))
        pieces2 = both_cores(grid, [chunks[1], *after(across2, qkv_a)])
        qkv_b, wb = project(grid, place, scale_half, after(attn_in, attended), pieces2, False)
        attended, *kept_b = attend_forward(1, lengths, qkv_b, attended)
        pieces3 = both_cores(grid, [chunks[2], *after(across3, attended)])
        gain_m, bias_up = (vecs[:, i].reshape(D).astype(f32) for i in (1, 2))
        wo, w_up, w_down, hidden1, mlp_in, pre, act, down_grad = mlp_forward(
            grid, place, gain_m, bias_up, pieces3, attended, tokens, grad_out_low
        )
    else:
        wq, wk, wv, wo, w_up, w_down = (
            lax.all_gather(w, "fsdp", axis=0, tiled=True)
            for w in (query_weight, key_weight, value_weight, output_weight, up_weight, down_weight)
        )
        wa = jnp.concatenate([w[:, :HALF] for w in (wq, wk, wv)], axis=1)
        wb = jnp.concatenate([w[:, HALF:] for w in (wq, wk, wv)], axis=1)
        vecs = lax.all_gather(vectors, "fsdp", axis=0).reshape(grid.owners, 4, grid.rows)
        attn_in = (rms_parts(xin)[0] * vecs[:, 0].reshape(D).astype(f32)).astype(bf16)
        left = attn_in.T
        scale_row = jnp.concatenate([scale_half[0], jnp.ones((2 * HALF,), f32)])
        attended, *kept_a = attend_forward(0, lengths, (nn(attn_in, wa) * scale_row).astype(bf16))
        attended, *kept_b = attend_forward(1, lengths, (nn(attn_in, wb) * scale_row).astype(bf16), attended)
        gain_m, bias_up = (vecs[:, i].reshape(D).astype(f32) for i in (1, 2))
        hidden1 = xin + nn(attended, wo)
        mlp_in = (rms_parts(hidden1)[0] * gain_m).astype(bf16)
        pre = nn(mlp_in, w_up) + bias_up
        act = (pre * jax.nn.sigmoid(pre)).astype(bf16)
        down_grad = tn(act, grad_out_low).astype(bf16)
    kept = (kept_a, kept_b)
    gain_a, bias_down = (vecs[:, i].reshape(D).astype(f32) for i in (0, 3))

    fac_row = jnp.broadcast_to(jnp.pad(factor, (0, LANES - HD))[None], (8, LANES))
    owned = (grid.owners, grid.rows)

    def scattered(grad):
        return lax.psum_scatter(grad, "fsdp", scatter_dimension=0, tiled=True)

    part_down = scattered(down_grad)
    up_grad, output_grad, grad_hidden, grad_att, up_bias_grad, down_bias_grad = mlp_backward(
        gain_m, grad_out_low, w_down, pre, mlp_in, w_up, hidden1, wo, attended
    )
    part_up, part_o = scattered(up_grad), scattered(output_grad)

    back_a, scale_a = attend_backward(0, fac_row, *kept[0], attended, grad_att)
    if grid.pieced:
        mine_a, theirs_a = weight_grads(
            grid, place, left, back_a, [up_bias_grad.reshape(owned), down_bias_grad.reshape(owned)]
        )
        recv_a = grid.other_core(theirs_a)
        a1 = fold_cores(grid, place, mine_a, recv_a)
        ra1 = (grid.across(a1[0], 1), grid.across(a1[2], 2))
        grad_att = after(grad_att, a1[0])
    back_b, scale_b = attend_backward(1, fac_row, *kept[1], attended, grad_att)
    scale_part = (scale_a + scale_b)[0, :HD] / (query_scale.astype(f32) * LOG2E)

    if grid.pieced:
        scale_rows = jnp.broadcast_to(jnp.pad(scale_part, (0, grid.rows - HD))[None], owned)
        mine_b, theirs_b = weight_grads(grid, place, left, after(back_b, *ra1), [scale_rows])
        recv_b = grid.other_core(theirs_b)
        a2 = fold_first(grid, place, a1[1], after(ra1[0], mine_b), a1[3], ra1[1])
        ra2 = (grid.across(a2[0], 2), grid.across(a2[2], 1))
        b1 = fold_cores(grid, place, mine_b, after(recv_b, a2[0]))
        rb1 = (grid.across(b1[0], 1), grid.across(b1[2], 2))
        late = jnp.concatenate(after([part_o, part_up, part_down], b1[0]))
        summed = lax.psum(late, "replica").astype(f32)
        input_grad = input_grad_of(tokens, gain_a, after(grad_hidden, b1[0], late), (back_a, back_b), (wa, wb))
        a3 = fold_second(grid, place, a2[1], after(ra2[0], input_grad), a2[3], ra2[1])
        ra3 = [grid.along_z(a3[s], s) for s in range(1, grid.planes)]
        b2 = fold_first(grid, place, b1[1], after(rb1[0], a3[0]), b1[3], rb1[1])
        rb2 = (grid.across(b2[0], 2), grid.across(b2[2], 1))
        act = after(act, b2[0])
        out_f = (hidden1 + nn(act, w_down) + bias_down).astype(bf16)
        a4 = fold_planes(grid, a3[0], *after(ra3, out_f))
        a5 = [a4] + [grid.across(a4, code) for code in (1, 2, 3)]
        b3 = fold_second(grid, place, b2[1], after(rb2[0], a4), b2[3], rb2[1])
        rb3 = [grid.along_z(b3[s], s) for s in range(1, grid.planes)]
        b4 = fold_planes(grid, b3[0], *after(rb3, summed))
        b5 = [b4] + [grid.across(b4, code) for code in (1, 2, 3)]
        g_q, g_k, g_v, tail = finish(grid, place, [a5, b5])
        g_o, g_up, g_down = (summed[i * grid.rows : (i + 1) * grid.rows] for i in range(3))
        g_up_bias, g_down_bias = tail[0, : grid.rows], tail[1, : grid.rows]
        scale_grad = tail[0, HALF : HALF + HD]
    else:
        out_f = (hidden1 + nn(act, w_down) + bias_down).astype(bf16)
        input_grad = input_grad_of(tokens, gain_a, grad_hidden, (back_a, back_b), (wa, wb))
        joined = [
            jnp.concatenate([g[:, w * HALF : (w + 1) * HALF] for g in (back_a, back_b)], axis=1) for w in range(3)
        ]
        g_o, g_up, g_down, g_q, g_k, g_v, g_up_bias, g_down_bias = (
            lax.psum(g.astype(f32), "replica")
            for g in (
                part_o,
                part_up,
                part_down,
                *[scattered(tn(attn_in, g).astype(bf16)) for g in joined],
                scattered(up_bias_grad),
                scattered(down_bias_grad),
            )
        )
        scale_grad = lax.psum(scale_part, ("replica", "fsdp"))

    def weighed(*pairs):
        return sum(jnp.sum(w.astype(f32) * g, axis=1) for w, g in pairs)

    g_attn_gain = weighed((query_weight, g_q), (key_weight, g_k), (value_weight, g_v)) / attn_gain.astype(f32)
    g_mlp_gain = weighed((up_weight, g_up)) / mlp_gain.astype(f32)
    sums = (g_q, g_k, g_v, g_o, g_up, g_down, g_attn_gain, g_mlp_gain, g_up_bias, g_down_bias)
    return (out_f, input_grad, *sums, scale_grad)


def solution(mesh):
    split = P(("replica", "fsdp"), None)
    rows = P("fsdp", None)
    part = P("fsdp")
    return jax.shard_map(
        functools.partial(shards, Grid(mesh.shape)),
        mesh=mesh,
        in_specs=(split, P(("replica", "fsdp")), split, *[rows] * 6, *[part] * 4, P()),
        out_specs=(split, split, *[rows] * 6, *[part] * 4, P()),
        check_vma=False,
    )
```

profile of v0, /device:TPU:0, one launch (start us, length us, event | category | flops | bytes accessed | tf_op | source)
XLA Modules:
  0.0 406.1 jit_solution(1974388321235287423)
XLA Ops:
  9.3 3.4 cut.1
  12.7 5.0 %collective-permute-start.2 = (bf16[128,640]{1,0:T(8,128)(2,1)}, bf16[128,640]{1,0:T(8,128)(2,1)S(1)}, u32[]{:S(2)}, u32[]{:S(2)}) collective-permute-start(bf16[128,640]{1,0:T(8,128)(2,1)} %get-tuple-element.120), channel_id=1, source_target_pairs={{0,6},{1,7},{2,0},{3,1},{4,2},{5,3},{6,4},{7,5},{8,14},{9,15},{10,... | collective-permute-start | bytes 491528 | tf_op jit(solution)/shard_map/ppermute | solution.py:252
  18.7 3.9 collective-permute-done.2
  22.7 9.1 %collective-permute-done.1 = bf16[128,640]{1,0:T(8,128)(2,1)S(1)} collective-permute-done((bf16[128,640]{1,0:T(8,128)(2,1)}, bf16[128,640]{1,0:T(8,128)(2,1)S(1)}, u32[]{:S(2)}, u32[]{:S(2)}) %collective-permute-start.1) | collective-permute-done | bytes 163872 | tf_op jit(solution)/shard_map/ppermute | solution.py:252
  32.9 1.7 collective-permute-start.12
  34.6 2.0 collective-permute-start.11
  36.7 2.5 collective-permute-start.5
  39.2 9.7 %collective-permute-done.12 = bf16[128,640]{1,0:T(8,128)(2,1)S(1)} collective-permute-done((bf16[128,640]{1,0:T(8,128)(2,1)}, bf16[128,640]{1,0:T(8,128)(2,1)S(1)}, u32[]{:S(2)}, u32[]{:S(2)}) %collective-permute-start.12) | collective-permute-done | bytes 163872 | tf_op jit(solution)/shard_map/ppermute | solution.py:252
  49.0 1.5 collective-permute-start.4
  50.5 1.5 collective-permute-start.3
  52.9 4.1 %collective-permute-done.16 = bf16[240,640]{1,0:T(8,128)(2,1)S(1)} collective-permute-done((bf16[240,640]{1,0:T(8,128)(2,1)}, bf16[240,640]{1,0:T(8,128)(2,1)S(1)}, u32[]{:S(2)}, u32[]{:S(2)}) %collective-permute-start.16) | collective-permute-done | bytes 307232 | tf_op jit(solution)/shard_map/ppermute | solution.py:252
  57.0 13.7 %collective-permute-done.15 = bf16[240,640]{1,0:T(8,128)(2,1)S(1)} collective-permute-done((bf16[240,640]{1,0:T(8,128)(2,1)}, bf16[240,640]{1,0:T(8,128)(2,1)S(1)}, u32[]{:S(2)}, u32[]{:S(2)}) %collective-permute-start.15) | collective-permute-done | bytes 307232 | tf_op jit(solution)/shard_map/ppermute | solution.py:252
  72.5 2.4 collective-permute-start.22
  77.7 16.3 %project.2 = (bf16[1024,1920]{1,0:T(8,128)(2,1)}, bf16[1280,1920]{1,0:T(8,128)(2,1)}, bf16[8,16,640]{2,1,0:T(8,128)(2,1)}, bf16[1024,1280]{1,0:T(8,128)(2,1)}, bf16[1280,1024]{1,0:T(8,128)(2,1)}) custom-call(s32[4]{0:T(128)} %pad_add_fusion.place_ref, f32[8,640]{1,0:T(8,128)} %broadcast_in_dim.23.scale_ref, bf16[1024,1280]{1,0:T(8,128)(2,1)} %x_ref.3, ...), custom_call_target="tpu_custom_call" | custom-call | flops 125829120 | bytes 409600 | tf_op jit(solution)/shard_map/project/pallas_call | solution.py:262
  94.1 3.3 collective-permute-done.21.refs_3_
  99.1 1.7 collective-permute-start.19
  100.8 1.3 collective-permute-start.18
  103.1 1.6 collective-permute-done.26.refs_8_
  105.5 12.7 %attend_forward.2 = (bf16[1024,1280]{1,0:T(8,128)(2,1)}, bf16[8,1024,128]{2,1,0:T(8,128)(2,1)}, bf16[8,1024,128]{2,1,0:T(8,128)(2,1)}, bf16[8,1024,128]{2,1,0:T(8,128)(2,1)}) custom-call(s32[1]{0:T(128)} %copy.34.len_ref, bf16[1024,1920]{1,0:T(8,128)(2,1)} %get-tuple-element.133.qkv_ref), custom_call_target="tpu_custom_call" | custom-call | flops 251658240 | tf_op jit(solution)/shard_map/attend_forward/pallas_call | solution.py:138
  119.1 14.1 %project.3 = (bf16[1024,1920]{1,0:T(8,128)(2,1)}, bf16[1280,1920]{1,0:T(8,128)(2,1)}) custom-call(s32[4]{0:T(128)} %pad_add_fusion.place_ref, f32[8,640]{1,0:T(8,128)} %broadcast_in_dim.23.scale_ref, bf16[1024,1280]{1,0:T(8,128)(2,1)} %get-tuple-element.135.x_ref, bf16[512,640]{1,0:T(8,128)(2,1)} %get-tuple-element.136.refs_0_, ...), custom_call_target="tpu_custom_call" | custom-call | flops 125829120 | bytes 409600 | tf_op jit(solution)/shard_map/project/pallas_call | solution.py:262
  133.2 12.5 %attend_forward.3 = (bf16[1024,1280]{1,0:T(8,128)(2,1)}, bf16[8,1024,128]{2,1,0:T(8,128)(2,1)}, bf16[8,1024,128]{2,1,0:T(8,128)(2,1)}, bf16[8,1024,128]{2,1,0:T(8,128)(2,1)}) custom-call(s32[1]{0:T(128)} %copy.34.len_ref, bf16[1024,1920]{1,0:T(8,128)(2,1)} %get-tuple-element.144.qkv_ref, ...), custom_call_target="tpu_custom_call", output_to_operand_aliasing={{0}: (2, {})} | custom-call | flops 251658240 | tf_op jit(solution)/shard_map/attend_forward/pallas_call | solution.py:138
  146.9 1.7 broadcast_select_fusion.refs_12_.refs_0_
  150.0 1.3 collective-permute-done.31.refs_8_
  151.3 1.3 collective-permute-done.32.refs_9_
  153.8 25.3 %mlp_forward.1 = (bf16[1280,1280]{1,0:T(8,128)(2,1)}, bf16[1280,1280]{1,0:T(8,128)(2,1)}, bf16[1280,1280]{1,0:T(8,128)(2,1)}, f32[1024,1280]{1,0:T(8,128)}, bf16...) custom-call(s32[4]{0:T(128)} %pad_add_fusion.place_ref, ...), custom_call_target="tpu_custom_call" | custom-call | flops 251658240 | bytes 1376256 | tf_op jit(solution)/shard_map/mlp_forward/pallas_call | solution.py:262
  179.2 28.6 %mlp_backward.1 = (bf16[1280,1280]{1,0:T(8,128)(2,1)}, f32[1024,1280]{1,0:T(8,128)}, bf16[1024,1280]{1,0:T(8,128)(2,1)}, bf16[1280,1280]{1,0:T(8,128)(2,1)}, f32[8,1280]{1,0:T(8,128)}) custom-call(f32[8,1280]{1,0:T(8,128)} %broadcast_in_dim.24.gain_ref, bf16[1024,1280]{1,0:T(8,128)(2,1)} %broadcast_select_fusion.refs_12_.refs_0_, ...), custom_call_target="tpu_custom_call" | custom-call | flops 419430400 | bytes 1261568 | tf_op jit(solution)/shard_map/mlp_backward/pallas_call | solution.py:262
  209.5 20.4 %attend_backward.2 = (bf16[1024,1920]{1,0:T(8,128)(2,1)}, f32[8,128]{1,0:T(8,128)}) custom-call(f32[8,128]{1,0:T(8,128)} %broadcast_in_dim.28.fac_ref, bf16[8,1024,128]{2,1,0:T(8,128)(2,1)} %get-tuple-element.162.qa_ref, bf16[8,1024,128]{2,1,0:T(8,128)(2,1)} %get-tuple-element.163.ka_ref, bf16[8,1024,128]{2,1,0:T(8,128)(2,1)} %get-tuple-element.164.va_ref, ...), custom_call_target="tpu_custom_call" | custom-call | flops 503316480 | tf_op jit(solution)/shard_map/attend_backward/pallas_call | solution.py:220
  230.7 12.7 %weight_grads.2 = (bf16[4,512,640]{2,1,0:T(8,128)(2,1)}, bf16[4,512,640]{2,1,0:T(8,128)(2,1)}) custom-call(s32[4]{0:T(128)} %pad_add_fusion.place_ref, bf16[1280,1024]{1,0:T(8,128)(2,1)} %get-tuple-element.152.left_ref, bf16[1024,1920]{1,0:T(8,128)(2,1)} %get-tuple-element.165.right_ref.grad_a, bf16[8,32,640]{2,1,0:T(8,128)(2,1)} %fusion.5.vec_ref), custom_call_target="tpu_custom_call" | custom-call | flops 125829120 | bytes 286720 | tf_op jit(solution)/shard_map/weight_grads/pallas_call | solution.py:262
  243.8 5.0 %collective-permute-done.33 = bf16[4,512,640]{2,1,0:T(8,128)(2,1)S(1)} collective-permute-done((bf16[4,512,640]{2,1,0:T(8,128)(2,1)}, bf16[4,512,640]{2,1,0:T(8,128)(2,1)S(1)}, u32[]{:S(2)}, u32[]{:S(2)}) %collective-permute-start.33) | collective-permute-done | bytes 2621472 | tf_op jit(solution)/shard_map/ppermute | solution.py:255
  248.7 1.4 copy-done.3
  250.2 4.7 %fold_cores.2 = (bf16[4,2,64,640]{3,2,1,0:T(8,128)(2,1)}, bf16[4,2,64,640]{3,2,1,0:T(8,128)(2,1)}, bf16[4,2,64,640]{3,2,1,0:T(8,128)(2,1)}, bf16[4,2,64,640]{3,2,1,0:T(8,128)(2,1)}) custom-call(s32[4]{0:T(128)} %pad_add_fusion.place_ref, bf16[4,2,2,2,64,640]{5,4,3,2,1,0:T(8,128)(2,1)} %bitcast.33, bf16[4,2,2,2,64,640]{5,4,3,2,1,0:T(8,128)(2,1)} %bitcast.34), custom_call_target="tpu_custom_call" | custom-call | bytes 196608 | tf_op jit(solution)/shard_map/fold_cores/pallas_call | solution.py:262
  254.9 1.2 collective-permute-start.35
  256.9 20.3 %attend_backward.3 = (bf16[1024,1920]{1,0:T(8,128)(2,1)}, f32[8,128]{1,0:T(8,128)}) custom-call(f32[8,128]{1,0:T(8,128)} %broadcast_in_dim.28.fac_ref, bf16[8,1024,128]{2,1,0:T(8,128)(2,1)} %get-tuple-element.153.qa_ref, bf16[8,1024,128]{2,1,0:T(8,128)(2,1)} %get-tuple-element.154.ka_ref, bf16[8,1024,128]{2,1,0:T(8,128)(2,1)} %get-tuple-element.155.va_ref, ...), custom_call_target="tpu_custom_call" | custom-call | flops 503316480 | tf_op jit(solution)/shard_map/attend_backward/pallas_call | solution.py:220
  278.8 12.7 %weight_grads.3 = (bf16[4,512,640]{2,1,0:T(8,128)(2,1)}, bf16[4,512,640]{2,1,0:T(8,128)(2,1)}) custom-call(s32[4]{0:T(128)} %pad_add_fusion.place_ref, bf16[1280,1024]{1,0:T(8,128)(2,1)} %get-tuple-element.152.left_ref, bf16[1024,1920]{1,0:T(8,128)(2,1)} %get-tuple-element.173.right_ref.grad_b, bf16[8,32,640]{2,1,0:T(8,128)(2,1)} %pad.28.vec_ref), custom_call_target="tpu_custom_call" | custom-call | flops 125829120 | bytes 286720 | tf_op jit(solution)/shard_map/weight_grads/pallas_call | solution.py:262
  293.0 3.8 fold_first.2
  296.8 1.3 collective-permute-start.39
  298.9 1.5 copy-done.2
  300.4 4.6 %fold_cores.3 = (bf16[4,2,64,640]{3,2,1,0:T(8,128)(2,1)}, bf16[4,2,64,640]{3,2,1,0:T(8,128)(2,1)}, bf16[4,2,64,640]{3,2,1,0:T(8,128)(2,1)}, bf16[4,2,64,640]{3,2,1,0:T(8,128)(2,1)}) custom-call(s32[4]{0:T(128)} %pad_add_fusion.place_ref, bf16[4,2,2,2,64,640]{5,4,3,2,1,0:T(8,128)(2,1)} %bitcast.31, bf16[4,2,2,2,64,640]{5,4,3,2,1,0:T(8,128)(2,1)} %bitcast.32), custom_call_target="tpu_custom_call" | custom-call | bytes 196608 | tf_op jit(solution)/shard_map/fold_cores/pallas_call | solution.py:262
  311.8 19.9 %input_grad.1 = bf16[1024,1280]{1,0:T(8,128)(2,1)} custom-call(bf16[1024,1280]{1,0:T(8,128)(2,1)} %x_ref.3, f32[8,1280]{1,0:T(8,128)} %broadcast_in_dim.29.gain_ref, f32[1024,1280]{1,0:T(8,128)} %get-tuple-element.193.hidden_ref, bf16[1024,1920]{1,0:T(8,128)(2,1)} %get-tuple-element.165.right_ref.grad_a, ...), custom_call_target="tpu_custom_call" | custom-call | flops 251658240 | bytes 704512 | tf_op jit(solution)/shard_map/input_grad/pallas_call | solution.py:262
  332.5 2.2 fold_second.2
  334.6 1.9 collective-permute-start.42
  336.6 1.9 collective-permute-start.43
  339.3 3.8 fold_first.3
  343.1 1.4 collective-permute-start.47
  345.3 7.9 %add_convert_fusion = bf16[1024,1280]{1,0:T(8,128)(2,1)} fusion(f32[1024,1280]{1,0:T(8,128)S(1)} %bitcast.30, bf16[1024,1280]{1,0:T(8,128)(2,1)} %get-tuple-element.203, bf16[1280,1280]{1,0:T(8,128)(2,1)} %get-tuple-element.156.refs_1_, f32[1280]{0:T(1024)} %reshape.89), kind=kOutput, calls=%fused_computation | convolution fusion | flops 3359375360 | bytes 13767680 | tf_op jit(solution)/shard_map/dot_general | solution.py:45
  353.9 1.9 fold_planes.2.refs_0_
  356.9 2.2 fold_second.3
  359.6 1.2 collective-permute-start.50
  360.8 2.9 collective-permute-start.51
  363.7 1.3 collective-permute-start.46
  365.1 1.3 collective-permute-start.45
  366.4 1.8 collective-permute-done.49.refs_1_
  369.3 3.0 collective-permute-done.50.refs_2_
  372.2 3.9 all-reduce.7.cloned.1.call-done
  376.2 1.9 fold_planes.3.refs_4_
  378.1 1.7 collective-permute-start.54
  379.8 1.4 collective-permute-start.53
  381.2 2.8 multiply_reduce_fusion
  385.2 3.4 collective-permute-done.53.refs_6_
  390.1 3.2 finish.1
  393.3 1.2 slice_bitcast_fusion
  394.5 1.3 fusion.11
  395.8 1.3 multiply_reduce_fusion.3
  397.1 1.6 multiply_reduce_fusion.1
  (237 shorter events, 40.1 us)
Async XLA Ops:
  7.2 69.4 %copy-start.52 = (bf16[80]{0:T(256)(128)(2,1)S(1)}, bf16[80]{0:T(256)(128)(2,1)}, u32[]{:S(2)}) copy-start(bf16[80]{0:T(256)(128)(2,1)} %param.27) | copy-start | bytes 484
  7.2 299.8 %reduce-scatter.8.cloned.1.call-start = ((), (), s32[]{:S(2)}) async-start(), calls=%async_computation.5 | async-start | bytes 3686400 | tf_op jit(solution)/shard_map/reduce_scatter | solution.py:864
  12.7 10.0 %collective-permute-start.2 = (bf16[128,640]{1,0:T(8,128)(2,1)}, bf16[128,640]{1,0:T(8,128)(2,1)S(1)}, u32[]{:S(2)}, u32[]{:S(2)}) collective-permute-start(bf16[128,640]{1,0:T(8,128)(2,1)} %get-tuple-element.120), channel_id=1, source_target_pairs={{0,6},{1,7},{2,0},{3,1},{4,2},{5,3},{6,4},{7,5},{8,14},{9,15},{10,... | collective-permute-start | bytes 491528 | tf_op jit(solution)/shard_map/ppermute | solution.py:252
  17.7 14.1 %collective-permute-start.1 = (bf16[128,640]{1,0:T(8,128)(2,1)}, bf16[128,640]{1,0:T(8,128)(2,1)S(1)}, u32[]{:S(2)}, u32[]{:S(2)}) collective-permute-start(bf16[128,640]{1,0:T(8,128)(2,1)} %get-tuple-element.120), channel_id=1, source_target_pairs={{0,4},{1,5},{2,6},{3,7},{4,0},{5,1},{6,2},{7,3},{8,12},{9,13},{10,... | collective-permute-start | bytes 491528 | tf_op jit(solution)/shard_map/ppermute | solution.py:252
  17.7 14.1 %collective-permute-start = (bf16[128,640]{1,0:T(8,128)(2,1)}, bf16[128,640]{1,0:T(8,128)(2,1)S(1)}, u32[]{:S(2)}, u32[]{:S(2)}) collective-permute-start(bf16[128,640]{1,0:T(8,128)(2,1)} %get-tuple-element.120), channel_id=1, source_target_pairs={{0,2},{1,3},{2,4},{3,5},{4,6},{5,7},{6,0},{7,1},{8,10},{9,11},{10,... | collective-permute-start | bytes 491528 | tf_op jit(solution)/shard_map/ppermute | solution.py:252
  31.8 7.4 %collective-permute-start.13 = (bf16[128,640]{1,0:T(8,128)(2,1)}, bf16[128,640]{1,0:T(8,128)(2,1)S(1)}, u32[]{:S(2)}, u32[]{:S(2)}) collective-permute-start(bf16[128,640]{1,0:T(8,128)(2,1)} %get-tuple-element.126), channel_id=1, source_target_pairs={{0,6},{1,7},{2,0},{3,1},{4,2},{5,3},{6,4},{7,5},{8,14},{9,15},{10,... | collective-permute-start | bytes 491528 | tf_op jit(solution)/shard_map/ppermute | solution.py:252
  32.9 16.1 %collective-permute-start.12 = (bf16[128,640]{1,0:T(8,128)(2,1)}, bf16[128,640]{1,0:T(8,128)(2,1)S(1)}, u32[]{:S(2)}, u32[]{:S(2)}) collective-permute-start(bf16[128,640]{1,0:T(8,128)(2,1)} %get-tuple-element.126), channel_id=1, source_target_pairs={{0,4},{1,5},{2,6},{3,7},{4,0},{5,1},{6,2},{7,3},{8,12},{9,13},{10,... | collective-permute-start | bytes 491528 | tf_op jit(solution)/shard_map/ppermute | solution.py:252
  34.6 14.3 %collective-permute-start.11 = (bf16[128,640]{1,0:T(8,128)(2,1)}, bf16[128,640]{1,0:T(8,128)(2,1)S(1)}, u32[]{:S(2)}, u32[]{:S(2)}) collective-permute-start(bf16[128,640]{1,0:T(8,128)(2,1)} %get-tuple-element.126), channel_id=1, source_target_pairs={{0,2},{1,3},{2,4},{3,5},{4,6},{5,7},{6,0},{7,1},{8,10},{9,11},{10,... | collective-permute-start | bytes 491528 | tf_op jit(solution)/shard_map/ppermute | solution.py:252
  36.7 41.0 %copy-start.6 = (bf16[3,128,640]{2,1,0:T(8,128)(2,1)}, bf16[3,128,640]{2,1,0:T(8,128)(2,1)S(1)}, u32[]{:S(2)}) copy-start(bf16[3,128,640]{2,1,0:T(8,128)(2,1)S(1)} %pad_maximum_fusion.1.refs_1_) | copy-start | bytes 1474564
  36.7 34.0 %collective-permute-start.5 = (bf16[3,128,640]{2,1,0:T(8,128)(2,1)S(1)}, bf16[3,128,640]{2,1,0:T(8,128)(2,1)S(1)}, u32[]{:S(2)}, u32[]{:S(2)}) collective-permute-start(bf16[3,128,640]{2,1,0:T(8,128)(2,1)S(1)} %pad_maximum_fusion.1.refs_1_), channel_id=1, source_target_pairs={{0,24},{8,16},{16,8},{24,0},{1,25},{9,17},{17,9},{25,1},{2,26},{10... | collective-permute-start | bytes 1474568 | tf_op jit(solution)/shard_map/ppermute | solution.py:258
  49.0 8.0 %collective-permute-start.16 = (bf16[240,640]{1,0:T(8,128)(2,1)}, bf16[240,640]{1,0:T(8,128)(2,1)S(1)}, u32[]{:S(2)}, u32[]{:S(2)}) collective-permute-start(bf16[240,640]{1,0:T(8,128)(2,1)} %get-tuple-element.127), channel_id=1, source_target_pairs={{0,6},{1,7},{2,0},{3,1},{4,2},{5,3},{6,4},{7,5},{8,14},{9,15},{10,... | collective-permute-start | bytes 921608 | tf_op jit(solution)/shard_map/ppermute | solution.py:252
  49.0 22.2 %collective-permute-start.4 = (bf16[3,128,640]{2,1,0:T(8,128)(2,1)S(1)}, bf16[3,128,640]{2,1,0:T(8,128)(2,1)S(1)}, u32[]{:S(2)}, u32[]{:S(2)}) collective-permute-start(bf16[3,128,640]{2,1,0:T(8,128)(2,1)S(1)} %pad_maximum_fusion.1.refs_1_), channel_id=1, source_target_pairs={{0,16},{8,24},{16,0},{24,8},{1,17},{9,25},{17,1},{25,9},{2,18},{10... | collective-permute-start | bytes 1474568 | tf_op jit(solution)/shard_map/ppermute | solution.py:258
  50.5 20.8 %collective-permute-start.3 = (bf16[3,128,640]{2,1,0:T(8,128)(2,1)S(1)}, bf16[3,128,640]{2,1,0:T(8,128)(2,1)S(1)}, u32[]{:S(2)}, u32[]{:S(2)}) collective-permute-start(bf16[3,128,640]{2,1,0:T(8,128)(2,1)S(1)} %pad_maximum_fusion.1.refs_1_), channel_id=1, source_target_pairs={{0,8},{8,0},{16,24},{24,16},{1,9},{9,1},{17,25},{25,17},{2,10},{10... | collective-permute-start | bytes 1474568 | tf_op jit(solution)/shard_map/ppermute | solution.py:258
  52.0 18.7 %collective-permute-start.15 = (bf16[240,640]{1,0:T(8,128)(2,1)}, bf16[240,640]{1,0:T(8,128)(2,1)S(1)}, u32[]{:S(2)}, u32[]{:S(2)}) collective-permute-start(bf16[240,640]{1,0:T(8,128)(2,1)} %get-tuple-element.127), channel_id=1, source_target_pairs={{0,4},{1,5},{2,6},{3,7},{4,0},{5,1},{6,2},{7,3},{8,12},{9,13},{10,... | collective-permute-start | bytes 921608 | tf_op jit(solution)/shard_map/ppermute | solution.py:252
  57.0 18.0 %collective-permute-start.6 = (bf16[512,640]{1,0:T(8,128)(2,1)}, bf16[512,640]{1,0:T(8,128)(2,1)S(1)}, u32[]{:S(2)}, u32[]{:S(2)}) collective-permute-start(bf16[512,640]{1,0:T(8,128)(2,1)} %get-tuple-element.119.refs_0_), channel_id=1, source_target_pairs={{0,1},{1,0},{2,3},{3,2},{4,5},{5,4},{6,7},{7,6},{8,9},{9,8},{10,11... | collective-permute-start | bytes 1966088 | tf_op jit(solution)/shard_map/ppermute | solution.py:255
  70.7 1.9 collective-permute-start.7
  70.7 4.8 %collective-permute-start.10 = (bf16[3,128,640]{2,1,0:T(8,128)(2,1)S(1)}, bf16[3,128,640]{2,1,0:T(8,128)(2,1)S(1)}, u32[]{:S(2)}, u32[]{:S(2)}) collective-permute-start(bf16[3,128,640]{2,1,0:T(8,128)(2,1)S(1)} %collective-permute-done.5.refs_4_), channel_id=1, source_target_pairs={{0,1},{1,0},{2,3},{3,2},{4,5},{5,4},{6,7},{7,6},{8,9},{9,8},{10,11... | collective-permute-start | bytes 1474568 | tf_op jit(solution)/shard_map/ppermute | solution.py:255
  71.2 4.8 %collective-permute-start.9 = (bf16[3,128,640]{2,1,0:T(8,128)(2,1)S(1)}, bf16[3,128,640]{2,1,0:T(8,128)(2,1)S(1)}, u32[]{:S(2)}, u32[]{:S(2)}) collective-permute-start(bf16[3,128,640]{2,1,0:T(8,128)(2,1)S(1)} %collective-permute-done.4.refs_3_), channel_id=1, source_target_pairs={{0,1},{1,0},{2,3},{3,2},{4,5},{5,4},{6,7},{7,6},{8,9},{9,8},{10,11... | collective-permute-start | bytes 1474568 | tf_op jit(solution)/shard_map/ppermute | solution.py:255
  71.3 4.9 %collective-permute-start.8 = (bf16[3,128,640]{2,1,0:T(8,128)(2,1)S(1)}, bf16[3,128,640]{2,1,0:T(8,128)(2,1)S(1)}, u32[]{:S(2)}, u32[]{:S(2)}) collective-permute-start(bf16[3,128,640]{2,1,0:T(8,128)(2,1)S(1)} %collective-permute-done.3.refs_2_), channel_id=1, source_target_pairs={{0,1},{1,0},{2,3},{3,2},{4,5},{5,4},{6,7},{7,6},{8,9},{9,8},{10,11... | collective-permute-start | bytes 1474568 | tf_op jit(solution)/shard_map/ppermute | solution.py:255
  72.5 21.5 %collective-permute-start.22 = (bf16[3,128,640]{2,1,0:T(8,128)(2,1)S(1)}, bf16[3,128,640]{2,1,0:T(8,128)(2,1)}, u32[]{:S(2)}, u32[]{:S(2)}) collective-permute-start(bf16[3,128,640]{2,1,0:T(8,128)(2,1)S(1)} %pad_maximum_fusion.2.refs_1_), channel_id=1, source_target_pairs={{0,24},{8,16},{16,8},{24,0},{1,25},{9,17},{17,9},{25,1},{2,26},{10... | collective-permute-start | bytes 1474568 | tf_op jit(solution)/shard_map/ppermute | solution.py:258
  75.0 22.3 %collective-permute-start.21 = (bf16[3,128,640]{2,1,0:T(8,128)(2,1)S(1)}, bf16[3,128,640]{2,1,0:T(8,128)(2,1)}, u32[]{:S(2)}, u32[]{:S(2)}) collective-permute-start(bf16[3,128,640]{2,1,0:T(8,128)(2,1)S(1)} %pad_maximum_fusion.2.refs_1_), channel_id=1, source_target_pairs={{0,16},{8,24},{16,0},{24,8},{1,17},{9,25},{17,1},{25,9},{2,18},{10... | collective-permute-start | bytes 1474568 | tf_op jit(solution)/shard_map/ppermute | solution.py:258
  75.5 21.9 %collective-permute-start.20 = (bf16[3,128,640]{2,1,0:T(8,128)(2,1)S(1)}, bf16[3,128,640]{2,1,0:T(8,128)(2,1)}, u32[]{:S(2)}, u32[]{:S(2)}) collective-permute-start(bf16[3,128,640]{2,1,0:T(8,128)(2,1)S(1)} %pad_maximum_fusion.2.refs_1_), channel_id=1, source_target_pairs={{0,8},{8,0},{16,24},{24,16},{1,9},{9,1},{17,25},{25,17},{2,10},{10... | collective-permute-start | bytes 1474568 | tf_op jit(solution)/shard_map/ppermute | solution.py:258
  76.1 26.0 %collective-permute-start.23 = (bf16[512,640]{1,0:T(8,128)(2,1)}, bf16[512,640]{1,0:T(8,128)(2,1)S(1)}, u32[]{:S(2)}, u32[]{:S(2)}) collective-permute-start(bf16[512,640]{1,0:T(8,128)(2,1)} %get-tuple-element.136.refs_0_), channel_id=1, source_target_pairs={{0,1},{1,0},{2,3},{3,2},{4,5},{5,4},{6,7},{7,6},{8,9},{9,8},{10,11... | collective-permute-start | bytes 1966088 | tf_op jit(solution)/shard_map/ppermute | solution.py:255
  76.2 17.9 %collective-permute-start.14 = (bf16[240,640]{1,0:T(8,128)(2,1)}, bf16[240,640]{1,0:T(8,128)(2,1)}, u32[]{:S(2)}, u32[]{:S(2)}) collective-permute-start(bf16[240,640]{1,0:T(8,128)(2,1)} %get-tuple-element.127), channel_id=1, source_target_pairs={{0,2},{1,3},{2,4},{3,5},{4,6},{5,7},{6,0},{7,1},{8,10},{9,11},{10,... | collective-permute-start | bytes 921608 | tf_op jit(solution)/shard_map/ppermute | solution.py:252
  97.4 5.2 %collective-permute-start.24 = (bf16[3,128,640]{2,1,0:T(8,128)(2,1)S(1)}, bf16[3,128,640]{2,1,0:T(8,128)(2,1)S(1)}, u32[]{:S(2)}, u32[]{:S(2)}) collective-permute-start(bf16[3,128,640]{2,1,0:T(8,128)(2,1)S(1)} %pad_maximum_fusion.2.refs_1_), channel_id=1, source_target_pairs={{0,1},{1,0},{2,3},{3,2},{4,5},{5,4},{6,7},{7,6},{8,9},{9,8},{10,11... | collective-permute-start | bytes 1474568 | tf_op jit(solution)/shard_map/ppermute | solution.py:255
  97.4 5.2 %collective-permute-start.25 = (bf16[3,128,640]{2,1,0:T(8,128)(2,1)}, bf16[3,128,640]{2,1,0:T(8,128)(2,1)S(1)}, u32[]{:S(2)}, u32[]{:S(2)}) collective-permute-start(bf16[3,128,640]{2,1,0:T(8,128)(2,1)} %collective-permute-done.20.refs_2_), channel_id=1, source_target_pairs={{0,1},{1,0},{2,3},{3,2},{4,5},{5,4},{6,7},{7,6},{8,9},{9,8},{10,11... | collective-permute-start | bytes 1474568 | tf_op jit(solution)/shard_map/ppermute | solution.py:255
  99.0 46.7 %copy-start = (bf16[3,240,640]{2,1,0:T(8,128)(2,1)}, bf16[3,240,640]{2,1,0:T(8,128)(2,1)S(1)}, u32[]{:S(2)}) copy-start(bf16[3,240,640]{2,1,0:T(8,128)(2,1)S(1)} %pad_maximum_fusion.refs_1_) | copy-start | bytes 2764804
  99.1 46.7 %collective-permute-start.19 = (bf16[3,240,640]{2,1,0:T(8,128)(2,1)S(1)}, bf16[3,240,640]{2,1,0:T(8,128)(2,1)}, u32[]{:S(2)}, u32[]{:S(2)}) collective-permute-start(bf16[3,240,640]{2,1,0:T(8,128)(2,1)S(1)} %pad_maximum_fusion.refs_1_), channel_id=1, source_target_pairs={{0,24},{8,16},{16,8},{24,0},{1,25},{9,17},{17,9},{25,1},{2,26},{10... | collective-permute-start | bytes 2764808 | tf_op jit(solution)/shard_map/ppermute | solution.py:258
  100.8 45.0 %collective-permute-start.18 = (bf16[3,240,640]{2,1,0:T(8,128)(2,1)S(1)}, bf16[3,240,640]{2,1,0:T(8,128)(2,1)}, u32[]{:S(2)}, u32[]{:S(2)}) collective-permute-start(bf16[3,240,640]{2,1,0:T(8,128)(2,1)S(1)} %pad_maximum_fusion.refs_1_), channel_id=1, source_target_pairs={{0,16},{8,24},{16,0},{24,8},{1,17},{9,25},{17,1},{25,9},{2,18},{10... | collective-permute-start | bytes 2764808 | tf_op jit(solution)/shard_map/ppermute | solution.py:258
  102.1 43.7 %collective-permute-start.17 = (bf16[3,240,640]{2,1,0:T(8,128)(2,1)S(1)}, bf16[3,240,640]{2,1,0:T(8,128)(2,1)}, u32[]{:S(2)}, u32[]{:S(2)}) collective-permute-start(bf16[3,240,640]{2,1,0:T(8,128)(2,1)S(1)} %pad_maximum_fusion.refs_1_), channel_id=1, source_target_pairs={{0,8},{8,0},{16,24},{24,16},{1,9},{9,1},{17,25},{25,17},{2,10},{10... | collective-permute-start | bytes 2764808 | tf_op jit(solution)/shard_map/ppermute | solution.py:258
  102.6 2.1 collective-permute-start.26
  102.7 15.6 %collective-permute-start.27 = (bf16[3,128,640]{2,1,0:T(8,128)(2,1)}, bf16[3,128,640]{2,1,0:T(8,128)(2,1)S(1)}, u32[]{:S(2)}, u32[]{:S(2)}) collective-permute-start(bf16[3,128,640]{2,1,0:T(8,128)(2,1)} %collective-permute-done.22.refs_4_), channel_id=1, source_target_pairs={{0,1},{1,0},{2,3},{3,2},{4,5},{5,4},{6,7},{7,6},{8,9},{9,8},{10,11... | collective-permute-start | bytes 1474568 | tf_op jit(solution)/shard_map/ppermute | solution.py:255
  104.7 45.2 %collective-permute-start.28 = (bf16[960,640]{1,0:T(8,128)(2,1)S(1)}, bf16[960,640]{1,0:T(8,128)(2,1)}, u32[]{:S(2)}, u32[]{:S(2)}) collective-permute-start(bf16[960,640]{1,0:T(8,128)(2,1)S(1)} %copy-done.11), channel_id=1, source_target_pairs={{0,1},{1,0},{2,3},{3,2},{4,5},{5,4},{6,7},{7,6},{8,9},{9,8},{10,11... | collective-permute-start | bytes 3686408 | tf_op jit(solution)/shard_map/ppermute | solution.py:255
  145.8 4.1 %collective-permute-start.29 = (bf16[3,240,640]{2,1,0:T(8,128)(2,1)S(1)}, bf16[3,240,640]{2,1,0:T(8,128)(2,1)}, u32[]{:S(2)}, u32[]{:S(2)}) collective-permute-start(bf16[3,240,640]{2,1,0:T(8,128)(2,1)S(1)} %pad_maximum_fusion.refs_1_), channel_id=1, source_target_pairs={{0,1},{1,0},{2,3},{3,2},{4,5},{5,4},{6,7},{7,6},{8,9},{9,8},{10,11... | collective-permute-start | bytes 2764808 | tf_op jit(solution)/shard_map/ppermute | solution.py:255
  146.2 3.8 collective-permute-start.30
  146.3 4.9 %collective-permute-start.31 = (bf16[3,240,640]{2,1,0:T(8,128)(2,1)}, bf16[3,240,640]{2,1,0:T(8,128)(2,1)}, u32[]{:S(2)}, u32[]{:S(2)}) collective-permute-start(bf16[3,240,640]{2,1,0:T(8,128)(2,1)} %collective-permute-done.18.refs_3_), channel_id=1, source_target_pairs={{0,1},{1,0},{2,3},{3,2},{4,5},{5,4},{6,7},{7,6},{8,9},{9,8},{10,11... | collective-permute-start | bytes 2764808 | tf_op jit(solution)/shard_map/ppermute | solution.py:255
  146.7 5.9 %collective-permute-start.32 = (bf16[3,240,640]{2,1,0:T(8,128)(2,1)}, bf16[3,240,640]{2,1,0:T(8,128)(2,1)}, u32[]{:S(2)}, u32[]{:S(2)}) collective-permute-start(bf16[3,240,640]{2,1,0:T(8,128)(2,1)} %collective-permute-done.19.refs_4_), channel_id=1, source_target_pairs={{0,1},{1,0},{2,3},{3,2},{4,5},{5,4},{6,7},{7,6},{8,9},{9,8},{10,11... | collective-permute-start | bytes 2764808 | tf_op jit(solution)/shard_map/ppermute | solution.py:255
  179.2 127.8 %reduce-scatter.4.cloned.1.call-start = ((), (), s32[]{:S(2)}) async-start(), calls=%async_computation.3 | async-start | bytes 3686400 | tf_op jit(solution)/shard_map/reduce_scatter | solution.py:864
  207.9 99.1 %reduce-scatter.6.cloned.1.call-start = ((), (), s32[]{:S(2)}) async-start(), calls=%async_computation.4 | async-start | bytes 3686400 | tf_op jit(solution)/shard_map/reduce_scatter | solution.py:864
  208.6 167.5 %all-reduce.7.cloned.1.call-start = ((), (), s32[]{:S(2)}) async-start(), calls=%async_computation.6 | async-start | bytes 2457600 | tf_op jit(solution)/shard_map/psum | solution.py:893
  243.4 5.3 %collective-permute-start.33 = (bf16[4,512,640]{2,1,0:T(8,128)(2,1)}, bf16[4,512,640]{2,1,0:T(8,128)(2,1)S(1)}, u32[]{:S(2)}, u32[]{:S(2)}) collective-permute-start(bf16[4,512,640]{2,1,0:T(8,128)(2,1)} %get-tuple-element.168), channel_id=1, source_target_pairs={{0,1},{1,0},{2,3},{3,2},{4,5},{5,4},{6,7},{7,6},{8,9},{9,8},{10,11... | collective-permute-start | bytes 7864328 | tf_op jit(solution)/shard_map/ppermute | solution.py:255
  254.9 23.0 %collective-permute-start.35 = (bf16[4,2,64,640]{3,2,1,0:T(8,128)(2,1)}, bf16[4,2,64,640]{3,2,1,0:T(8,128)(2,1)S(1)}, u32[]{:S(2)}, u32[]{:S(2)}) collective-permute-start(bf16[4,2,64,640]{3,2,1,0:T(8,128)(2,1)} %get-tuple-element.172), channel_id=1, source_target_pairs={{0,16},{8,24},{16,0},{24,8},{1,17},{9,25},{17,1},{25,9},{2,18},{10... | collective-permute-start | bytes 1966088 | tf_op jit(solution)/shard_map/ppermute | solution.py:258
  256.1 21.8 %collective-permute-start.34 = (bf16[4,2,64,640]{3,2,1,0:T(8,128)(2,1)}, bf16[4,2,64,640]{3,2,1,0:T(8,128)(2,1)S(1)}, u32[]{:S(2)}, u32[]{:S(2)}) collective-permute-start(bf16[4,2,64,640]{3,2,1,0:T(8,128)(2,1)} %get-tuple-element.169), channel_id=1, source_target_pairs={{0,8},{8,0},{16,24},{24,16},{1,9},{9,1},{17,25},{25,17},{2,10},{10... | collective-permute-start | bytes 1966088 | tf_op jit(solution)/shard_map/ppermute | solution.py:258
  291.5 7.4 %collective-permute-start.36 = (bf16[4,512,640]{2,1,0:T(8,128)(2,1)}, bf16[4,512,640]{2,1,0:T(8,128)(2,1)S(1)}, u32[]{:S(2)}, u32[]{:S(2)}) collective-permute-start(bf16[4,512,640]{2,1,0:T(8,128)(2,1)} %get-tuple-element.177), channel_id=1, source_target_pairs={{0,1},{1,0},{2,3},{3,2},{4,5},{5,4},{6,7},{7,6},{8,9},{9,8},{10,11... | collective-permute-start | bytes 7864328 | tf_op jit(solution)/shard_map/ppermute | solution.py:255
  296.8 35.0 %collective-permute-start.39 = (bf16[4,64,640]{2,1,0:T(8,128)(2,1)}, bf16[4,64,640]{2,1,0:T(8,128)(2,1)S(1)}, u32[]{:S(2)}, u32[]{:S(2)}) collective-permute-start(bf16[4,64,640]{2,1,0:T(8,128)(2,1)} %get-tuple-element.197), channel_id=1, source_target_pairs={{0,8},{8,0},{16,24},{24,16},{1,9},{9,1},{17,25},{25,17},{2,10},{10... | collective-permute-start | bytes 983048 | tf_op jit(solution)/shard_map/ppermute | solution.py:258
  298.0 33.7 %collective-permute-start.38 = (bf16[4,64,640]{2,1,0:T(8,128)(2,1)}, bf16[4,64,640]{2,1,0:T(8,128)(2,1)}, u32[]{:S(2)}, u32[]{:S(2)}) collective-permute-start(bf16[4,64,640]{2,1,0:T(8,128)(2,1)} %get-tuple-element.181), channel_id=1, source_target_pairs={{0,16},{8,24},{16,0},{24,8},{1,17},{9,25},{17,1},{25,9},{2,18},{10... | collective-permute-start | bytes 983048 | tf_op jit(solution)/shard_map/ppermute | solution.py:258
  305.0 33.5 %collective-permute-start.40 = (bf16[4,2,64,640]{3,2,1,0:T(8,128)(2,1)}, bf16[4,2,64,640]{3,2,1,0:T(8,128)(2,1)S(1)}, u32[]{:S(2)}, u32[]{:S(2)}) collective-permute-start(bf16[4,2,64,640]{3,2,1,0:T(8,128)(2,1)} %get-tuple-element.201), channel_id=1, source_target_pairs={{0,16},{8,24},{16,0},{24,8},{1,17},{9,25},{17,1},{25,9},{2,18},{10... | collective-permute-start | bytes 1966088 | tf_op jit(solution)/shard_map/ppermute | solution.py:258
  306.2 32.3 %collective-permute-start.37 = (bf16[4,2,64,640]{3,2,1,0:T(8,128)(2,1)}, bf16[4,2,64,640]{3,2,1,0:T(8,128)(2,1)}, u32[]{:S(2)}, u32[]{:S(2)}) collective-permute-start(bf16[4,2,64,640]{3,2,1,0:T(8,128)(2,1)} %get-tuple-element.184), channel_id=1, source_target_pairs={{0,8},{8,0},{16,24},{24,16},{1,9},{9,1},{17,25},{25,17},{2,10},{10... | collective-permute-start | bytes 1966088 | tf_op jit(solution)/shard_map/ppermute | solution.py:258
  311.8 33.5 %slice-start = ((s8[5242880]{0:T(1024)(128)(4,1)}), s8[4194304]{0:T(1024)(128)(4,1)S(1)}, s32[]{:S(2)}) async-start(s8[5242880]{0:T(1024)(128)(4,1)} %bitcast.29), calls=%async_computation.7 | async-start | bytes 8388608
  311.8 33.5 %slice-start.1 = ((s8[5242880]{0:T(1024)(128)(4,1)}), s8[1048576]{0:T(1024)(128)(4,1)S(1)}, s32[]{:S(2)}) async-start(s8[5242880]{0:T(1024)(128)(4,1)} %bitcast.29), calls=%async_computation.8 | async-start | bytes 2097152
  334.6 18.6 %collective-permute-start.41 = (bf16[2,64,640]{2,1,0:T(8,128)(2,1)}, bf16[2,64,640]{2,1,0:T(8,128)(2,1)S(1)}, u32[]{:S(2)}, u32[]{:S(2)}) collective-permute-start(bf16[2,64,640]{2,1,0:T(8,128)(2,1)} %get-tuple-element.204), channel_id=1, source_target_pairs={{0,2},{1,3},{2,4},{3,5},{4,6},{5,7},{6,0},{7,1},{8,10},{9,11},{10,... | collective-permute-start | bytes 491528 | tf_op jit(solution)/shard_map/ppermute | solution.py:252
  334.6 18.6 %collective-permute-start.42 = (bf16[2,64,640]{2,1,0:T(8,128)(2,1)}, bf16[2,64,640]{2,1,0:T(8,128)(2,1)S(1)}, u32[]{:S(2)}, u32[]{:S(2)}) collective-permute-start(bf16[2,64,640]{2,1,0:T(8,128)(2,1)} %get-tuple-element.205), channel_id=1, source_target_pairs={{0,4},{1,5},{2,6},{3,7},{4,0},{5,1},{6,2},{7,3},{8,12},{9,13},{10,... | collective-permute-start | bytes 491528 | tf_op jit(solution)/shard_map/ppermute | solution.py:252
  336.6 16.7 %collective-permute-start.43 = (bf16[2,64,640]{2,1,0:T(8,128)(2,1)}, bf16[2,64,640]{2,1,0:T(8,128)(2,1)}, u32[]{:S(2)}, u32[]{:S(2)}) collective-permute-start(bf16[2,64,640]{2,1,0:T(8,128)(2,1)} %get-tuple-element.206), channel_id=1, source_target_pairs={{0,6},{1,7},{2,0},{3,1},{4,2},{5,3},{6,4},{7,5},{8,14},{9,15},{10,... | collective-permute-start | bytes 491528 | tf_op jit(solution)/shard_map/ppermute | solution.py:252
  343.1 12.7 %collective-permute-start.47 = (bf16[4,64,640]{2,1,0:T(8,128)(2,1)}, bf16[4,64,640]{2,1,0:T(8,128)(2,1)S(1)}, u32[]{:S(2)}, u32[]{:S(2)}) collective-permute-start(bf16[4,64,640]{2,1,0:T(8,128)(2,1)} %get-tuple-element.202), channel_id=1, source_target_pairs={{0,16},{8,24},{16,0},{24,8},{1,17},{9,25},{17,1},{25,9},{2,18},{10... | collective-permute-start | bytes 983048 | tf_op jit(solution)/shard_map/ppermute | solution.py:258
  344.5 11.7 %collective-permute-start.48 = (bf16[4,64,640]{2,1,0:T(8,128)(2,1)}, bf16[4,64,640]{2,1,0:T(8,128)(2,1)S(1)}, u32[]{:S(2)}, u32[]{:S(2)}) collective-permute-start(bf16[4,64,640]{2,1,0:T(8,128)(2,1)} %get-tuple-element.213), channel_id=1, source_target_pairs={{0,8},{8,0},{16,24},{24,16},{1,9},{9,1},{17,25},{25,17},{2,10},{10... | collective-permute-start | bytes 983048 | tf_op jit(solution)/shard_map/ppermute | solution.py:258
  359.0 9.2 %collective-permute-start.49 = (bf16[2,64,640]{2,1,0:T(8,128)(2,1)}, bf16[2,64,640]{2,1,0:T(8,128)(2,1)S(1)}, u32[]{:S(2)}, u32[]{:S(2)}) collective-permute-start(bf16[2,64,640]{2,1,0:T(8,128)(2,1)} %get-tuple-element.215), channel_id=1, source_target_pairs={{0,2},{1,3},{2,4},{3,5},{4,6},{5,7},{6,0},{7,1},{8,10},{9,11},{10,... | collective-permute-start | bytes 491528 | tf_op jit(solution)/shard_map/ppermute | solution.py:252
  359.6 12.6 %collective-permute-start.50 = (bf16[2,64,640]{2,1,0:T(8,128)(2,1)}, bf16[2,64,640]{2,1,0:T(8,128)(2,1)S(1)}, u32[]{:S(2)}, u32[]{:S(2)}) collective-permute-start(bf16[2,64,640]{2,1,0:T(8,128)(2,1)} %get-tuple-element.216), channel_id=1, source_target_pairs={{0,4},{1,5},{2,6},{3,7},{4,0},{5,1},{6,2},{7,3},{8,12},{9,13},{10,... | collective-permute-start | bytes 491528 | tf_op jit(solution)/shard_map/ppermute | solution.py:252
  360.8 11.4 %collective-permute-start.51 = (bf16[2,64,640]{2,1,0:T(8,128)(2,1)}, bf16[2,64,640]{2,1,0:T(8,128)(2,1)S(1)}, u32[]{:S(2)}, u32[]{:S(2)}) collective-permute-start(bf16[2,64,640]{2,1,0:T(8,128)(2,1)} %get-tuple-element.217), channel_id=1, source_target_pairs={{0,6},{1,7},{2,0},{3,1},{4,2},{5,3},{6,4},{7,5},{8,14},{9,15},{10,... | collective-permute-start | bytes 491528 | tf_op jit(solution)/shard_map/ppermute | solution.py:252
  363.7 20.3 %collective-permute-start.46 = (bf16[2,64,640]{2,1,0:T(8,128)(2,1)}, bf16[2,64,640]{2,1,0:T(8,128)(2,1)S(1)}, u32[]{:S(2)}, u32[]{:S(2)}) collective-permute-start(bf16[2,64,640]{2,1,0:T(8,128)(2,1)} %fold_planes.2.refs_0_), channel_id=1, source_target_pairs={{0,24},{8,16},{16,8},{24,0},{1,25},{9,17},{17,9},{25,1},{2,26},{10... | collective-permute-start | bytes 491528 | tf_op jit(solution)/shard_map/ppermute | solution.py:258
  365.1 20.1 %collective-permute-start.45 = (bf16[2,64,640]{2,1,0:T(8,128)(2,1)}, bf16[2,64,640]{2,1,0:T(8,128)(2,1)S(1)}, u32[]{:S(2)}, u32[]{:S(2)}) collective-permute-start(bf16[2,64,640]{2,1,0:T(8,128)(2,1)} %fold_planes.2.refs_0_), channel_id=1, source_target_pairs={{0,16},{8,24},{16,0},{24,8},{1,17},{9,25},{17,1},{25,9},{2,18},{10... | collective-permute-start | bytes 491528 | tf_op jit(solution)/shard_map/ppermute | solution.py:258
  368.2 16.9 %collective-permute-start.44 = (bf16[2,64,640]{2,1,0:T(8,128)(2,1)}, bf16[2,64,640]{2,1,0:T(8,128)(2,1)S(1)}, u32[]{:S(2)}, u32[]{:S(2)}) collective-permute-start(bf16[2,64,640]{2,1,0:T(8,128)(2,1)} %fold_planes.2.refs_0_), channel_id=1, source_target_pairs={{0,8},{8,0},{16,24},{24,16},{1,9},{9,1},{17,25},{25,17},{2,10},{10... | collective-permute-start | bytes 491528 | tf_op jit(solution)/shard_map/ppermute | solution.py:258
  378.1 7.0 %collective-permute-start.54 = (bf16[2,64,640]{2,1,0:T(8,128)(2,1)}, bf16[2,64,640]{2,1,0:T(8,128)(2,1)S(1)}, u32[]{:S(2)}, u32[]{:S(2)}) collective-permute-start(bf16[2,64,640]{2,1,0:T(8,128)(2,1)} %fold_planes.3.refs_4_), channel_id=1, source_target_pairs={{0,24},{8,16},{16,8},{24,0},{1,25},{9,17},{17,9},{25,1},{2,26},{10... | collective-permute-start | bytes 491528 | tf_op jit(solution)/shard_map/ppermute | solution.py:258
  379.8 8.7 %collective-permute-start.53 = (bf16[2,64,640]{2,1,0:T(8,128)(2,1)}, bf16[2,64,640]{2,1,0:T(8,128)(2,1)S(1)}, u32[]{:S(2)}, u32[]{:S(2)}) collective-permute-start(bf16[2,64,640]{2,1,0:T(8,128)(2,1)} %fold_planes.3.refs_4_), channel_id=1, source_target_pairs={{0,16},{8,24},{16,0},{24,8},{1,17},{9,25},{17,1},{25,9},{2,18},{10... | collective-permute-start | bytes 491528 | tf_op jit(solution)/shard_map/ppermute | solution.py:258
  384.0 5.4 %collective-permute-start.52 = (bf16[2,64,640]{2,1,0:T(8,128)(2,1)S(1)}, bf16[2,64,640]{2,1,0:T(8,128)(2,1)S(1)}, u32[]{:S(2)}, u32[]{:S(2)}) collective-permute-start(bf16[2,64,640]{2,1,0:T(8,128)(2,1)S(1)} %copy-done.14), channel_id=1, source_target_pairs={{0,8},{8,0},{16,24},{24,16},{1,9},{9,1},{17,25},{25,17},{2,10},{10... | collective-permute-start | bytes 491528 | tf_op jit(solution)/shard_map/ppermute | solution.py:258
  (50 other events, 416.6 us)
Sparse Core Ops, SparseCore 0:
  179.3 39.7 reduce-scatter.7
  221.5 40.2 reduce-scatter.3
  264.1 40.2 reduce-scatter.5
  311.3 64.8 all-reduce.6
where the time goes:
time: 410 us; the launch traced here: 406 us
  Pallas kernels  227 us (55%)
  waiting for transfers between devices  68 us (17%)
  starting transfers between devices  52.7 us (13%)
  local copies, waits for them, and re-layouts  22 us (5%)
  between operations  15.4 us (4%)
  other arithmetic  12.8 us (3%)
  matrix products  7.93 us (2%)
    pallas_call x17, Pallas kernels, kernel_call(): pl.pallas_call(kernel, out_shape=outs, scratch_shapes=scratch, compiler_p...  161 us
    ppermute x15, waiting for transfers between devices, along_z(): return lax.ppermute(v, 'fsdp', pairs)  45.4 us
    pallas_call x2, Pallas kernels, attend_backward(): pl.pallas_call(functools.partial(backward_kernel, GROUP), grid=(1,), in_s...  40.7 us
    ppermute x23, starting transfers between devices, across(): lax.ppermute(v, 'replica', [(i, i ^ code) for i in range(self.copies)])  28.2 us
    pallas_call x2, Pallas kernels, attend_forward(): pl.pallas_call(kernel, grid=(1,), in_specs=[pl.BlockSpec(memory_space=plt...  25.3 us
    ppermute x15, starting transfers between devices, along_z(): return lax.ppermute(v, 'fsdp', pairs)  20.7 us
    unnamed x112, local copies, waits for them, and re-layouts  11.1 us
    ppermute x17, waiting for transfers between devices, other_core(): return lax.ppermute(v, 'fsdp', [(i, i ^ 1) for i in range(self.owners)])  10 us
  transfers between devices with their start and end apart: 59, of which 19 were waited for; matrix products, arithmetic and copies ran while one was open for 6% of the time, Pallas kernels for 48%

commit v1 on v0

--- a/solution.py
+++ b/solution.py
@@ -495,8 +495,8 @@
 
 def mlp_backward_kernel(gain_ref, *refs):
     grad_ref, down_ref, pre_ref, mlp_in_ref, up_ref, hidden_ref, output_ref, attended_ref = refs[:8]
-    up_grad_ref, grad_hidden_ref, grad_att_ref, output_grad_ref, sums_ref = refs[8:13]
-    grad, down, wide, mlp_in, up, hidden, output, attended, grad_pre, grad_proj, first, second, sem = refs[13:]
+    both_ref, grad_hidden_ref, grad_att_ref, sums_ref = refs[8:12]
+    grad, down, wide, mlp_in, up, hidden, output, attended, grad_pre, grad_proj, first, second, sem = refs[12:]
     loads = {}
     for n, (name, source, target) in enumerate(
         (
@@ -519,7 +519,7 @@
         copy.start()
         written.append(copy)
 
-    for name in ("grad", "down", "pre"):
+    for name in ("down", "grad", "pre"):
         loads[name].wait()
     sums = jnp.zeros((1, D), f32)
     for at in in_blocks():
@@ -534,7 +534,7 @@
     for name in ("mlp_in", "up", "hidden"):
         loads[name].wait()
     first[...] = tn(mlp_in[...], grad_pre[...]).astype(bf16)
-    keep(first, up_grad_ref)
+    keep(first, both_ref.at[:, pl.ds(0, D)])
     for at in in_blocks():
         normed, inverse = rms_parts(hidden[at, :])
         back = rms_back(nt(grad_pre[at, :], up[...]) * gain_ref[0:1, :], normed, inverse)
@@ -548,7 +548,7 @@
         mlp_in[at, :] = nt(grad_proj[at, :], output[...]).astype(bf16)
     keep(mlp_in, grad_att_ref)
     second[...] = tn(attended[...], grad_proj[...]).astype(bf16)
-    keep(second, output_grad_ref)
+    keep(second, both_ref.at[:, pl.ds(D, D)])
     for copy in written:
         copy.wait()
 
@@ -556,11 +556,11 @@
 def mlp_backward(gain, grad_out_low, w_down, pre, mlp_in, w_up, hidden1, w_out, attended):
     hbm = pl.BlockSpec(memory_space=pl.ANY)
     low, high, square = ((SEQ, D), bf16), ((SEQ, D), f32), ((D, D), bf16)
-    up_grad, grad_hidden, grad_att, output_grad, sums = kernel_call(
+    both, grad_hidden, grad_att, sums = kernel_call(
         mlp_backward_kernel,
         "mlp_backward",
         (row_of(gain), grad_out_low, w_down, pre, mlp_in, w_up, hidden1, w_out, attended),
-        [jax.ShapeDtypeStruct(*o) for o in (square, high, low, square, ((8, D), f32))],
+        [jax.ShapeDtypeStruct(*o) for o in (((D, 2 * D), bf16), high, low, ((8, D), f32))],
         scratch=[
             *[pltpu.VMEM(*v) for v in (low, square, high, low, square, high, square, low, low, low, square, square)],
             pltpu.SemaphoreType.DMA((12,)),
@@ -568,9 +568,9 @@
         flops=10 * SEQ * D * D,
         nbytes=10 * D * D + 26 * SEQ * D,
         in_specs=[pl.BlockSpec(memory_space=pltpu.VMEM)] + [hbm] * 8,
-        out_specs=[hbm] * 4 + [pl.BlockSpec(memory_space=pltpu.VMEM)],
-    )
-    return up_grad, output_grad, grad_hidden, grad_att, sums[0], sums[1]
+        out_specs=[hbm] * 3 + [pl.BlockSpec(memory_space=pltpu.VMEM)],
+    )
+    return both, grad_hidden, grad_att, sums[0], sums[1]
 
 
 def weight_grad_kernel(planes, rows, place_ref, left_ref, right_ref, vec_ref, mine, theirs, left, right, stage, sem_in, sem_out):
@@ -864,10 +864,10 @@
         return lax.psum_scatter(grad, "fsdp", scatter_dimension=0, tiled=True)
 
     part_down = scattered(down_grad)
-    up_grad, output_grad, grad_hidden, grad_att, up_bias_grad, down_bias_grad = mlp_backward(
+    both, grad_hidden, grad_att, up_bias_grad, down_bias_grad = mlp_backward(
         gain_m, grad_out_low, w_down, pre, mlp_in, w_up, hidden1, wo, attended
     )
-    part_up, part_o = scattered(up_grad), scattered(output_grad)
+    part_both = scattered(both)
 
     back_a, scale_a = attend_backward(0, fac_row, *kept[0], attended, grad_att)
     if grid.pieced:
@@ -885,13 +885,13 @@
         scale_rows = jnp.broadcast_to(jnp.pad(scale_part, (0, grid.rows - HD))[None], owned)
         mine_b, theirs_b = weight_grads(grid, place, left, after(back_b, *ra1), [scale_rows])
         recv_b = grid.other_core(theirs_b)
-        a2 = fold_first(grid, place, a1[1], after(ra1[0], mine_b), a1[3], ra1[1])
+        late = jnp.concatenate(after([part_both, part_down], mine_b), axis=1)
+        summed = lax.psum(late, "replica").astype(f32)
+        a2 = fold_first(grid, place, a1[1], after(ra1[0], mine_b, late), a1[3], ra1[1])
         ra2 = (grid.across(a2[0], 2), grid.across(a2[2], 1))
         b1 = fold_cores(grid, place, mine_b, after(recv_b, a2[0]))
         rb1 = (grid.across(b1[0], 1), grid.across(b1[2], 2))
-        late = jnp.concatenate(after([part_o, part_up, part_down], b1[0]))
-        summed = lax.psum(late, "replica").astype(f32)
-        input_grad = input_grad_of(tokens, gain_a, after(grad_hidden, b1[0], late), (back_a, back_b), (wa, wb))
+        input_grad = input_grad_of(tokens, gain_a, after(grad_hidden, b1[0]), (back_a, back_b), (wa, wb))
         a3 = fold_second(grid, place, a2[1], after(ra2[0], input_grad), a2[3], ra2[1])
         ra3 = [grid.along_z(a3[s], s) for s in range(1, grid.planes)]
         b2 = fold_first(grid, place, b1[1], after(rb1[0], a3[0]), b1[3], rb1[1])
@@ -900,12 +900,12 @@
         out_f = (hidden1 + nn(act, w_down) + bias_down).astype(bf16)
         a4 = fold_planes(grid, a3[0], *after(ra3, out_f))
         a5 = [a4] + [grid.across(a4, code) for code in (1, 2, 3)]
-        b3 = fold_second(grid, place, b2[1], after(rb2[0], a4), b2[3], rb2[1])
+        b3 = fold_second(grid, place, b2[1], after(rb2[0], a4, summed), b2[3], rb2[1])
         rb3 = [grid.along_z(b3[s], s) for s in range(1, grid.planes)]
-        b4 = fold_planes(grid, b3[0], *after(rb3, summed))
+        b4 = fold_planes(grid, b3[0], *rb3)
         b5 = [b4] + [grid.across(b4, code) for code in (1, 2, 3)]
         g_q, g_k, g_v, tail = finish(grid, place, [a5, b5])
-        g_o, g_up, g_down = (summed[i * grid.rows : (i + 1) * grid.rows] for i in range(3))
+        g_up, g_o, g_down = (summed[:, i * D : (i + 1) * D] for i in range(3))
         g_up_bias, g_down_bias = tail[0, : grid.rows], tail[1, : grid.rows]
         scale_grad = tail[0, HALF : HALF + HD]
     else:
@@ -917,8 +917,8 @@
         g_o, g_up, g_down, g_q, g_k, g_v, g_up_bias, g_down_bias = (
             lax.psum(g.astype(f32), "replica")
             for g in (
-                part_o,
-                part_up,
+                part_both[:, D:],
+                part_both[:, :D],
                 part_down,
                 *[scattered(tn(attn_in, g).astype(bf16)) for g in joined],
                 scattered(up_bias_grad),

time: 410 us -> 426 us (1.039)
  waiting for transfers between devices: 68 us -> 88 us
    psum x1, waiting for transfers between devices: 3.94 us -> 13.4 us  [shards(): summed = lax.psum(late, 'replica').astype(f32)]
    ppermute x23, waiting for transfers between devices: 7.94 us -> 14.1 us  [across(): lax.ppermute(v, 'replica', [(i, i ^ code) for i in range(self.copies)])]
    unnamed x112 -> x107, local copies, waits for them, and re-layouts: 11.1 us -> 8.88 us
  transfers between devices with their start and end apart: 59 -> 58, of which waited for: 19 -> 20; matrix products, arithmetic and copies ran while one was open for 6% -> 5% of each run, Pallas kernels for 48% -> 45%
where the time goes in v1:
time: 426 us; the launch traced here: 422 us
  Pallas kernels  228 us (54%)
  waiting for transfers between devices  88 us (21%)
  starting transfers between devices  52.1 us (12%)
  local copies, waits for them, and re-layouts  19.2 us (5%)
  between operations  15.3 us (4%)
  other arithmetic  11.5 us (3%)
  matrix products  7.78 us (2%)
    pallas_call x17, Pallas kernels, kernel_call(): pl.pallas_call(kernel, out_shape=outs, scratch_shapes=scratch, compiler_p...  162 us
    ppermute x15, waiting for transfers between devices, along_z(): return lax.ppermute(v, 'fsdp', pairs)  49.5 us
    pallas_call x2, Pallas kernels, attend_backward(): pl.pallas_call(functools.partial(backward_kernel, GROUP), grid=(1,), in_s...  40.7 us
    ppermute x23, starting transfers between devices, across(): lax.ppermute(v, 'replica', [(i, i ^ code) for i in range(self.copies)])  27.9 us
    pallas_call x2, Pallas kernels, attend_forward(): pl.pallas_call(kernel, grid=(1,), in_specs=[pl.BlockSpec(memory_space=plt...  25.3 us
    ppermute x15, starting transfers between devices, along_z(): return lax.ppermute(v, 'fsdp', pairs)  20.3 us
    ppermute x23, waiting for transfers between devices, across(): lax.ppermute(v, 'replica', [(i, i ^ code) for i in range(self.copies)])  14.1 us
    psum x1, waiting for transfers between devices, shards(): summed = lax.psum(late, 'replica').astype(f32)  13.4 us
  transfers between devices with their start and end apart: 58, of which 20 were waited for; matrix products, arithmetic and copies ran while one was open for 5% of the time, Pallas kernels for 45%

profile of v1, /device:TPU:0, one launch (start us, length us, event | category | flops | bytes accessed | tf_op | source)
XLA Modules:
  0.0 421.5 jit_solution(14156200762889143378)
XLA Ops:
  9.3 3.4 cut.1
  12.7 5.0 %collective-permute-start.2 = (bf16[128,640]{1,0:T(8,128)(2,1)}, bf16[128,640]{1,0:T(8,128)(2,1)S(1)}, u32[]{:S(2)}, u32[]{:S(2)}) collective-permute-start(bf16[128,640]{1,0:T(8,128)(2,1)} %get-tuple-element.115), channel_id=1, source_target_pairs={{0,6},{1,7},{2,0},{3,1},{4,2},{5,3},{6,4},{7,5},{8,14},{9,15},{10,... | collective-permute-start | bytes 491528 | tf_op jit(solution)/shard_map/ppermute | solution.py:252
  18.7 3.9 collective-permute-done.2
  22.7 9.1 %collective-permute-done.1 = bf16[128,640]{1,0:T(8,128)(2,1)S(1)} collective-permute-done((bf16[128,640]{1,0:T(8,128)(2,1)}, bf16[128,640]{1,0:T(8,128)(2,1)S(1)}, u32[]{:S(2)}, u32[]{:S(2)}) %collective-permute-start.1) | collective-permute-done | bytes 163872 | tf_op jit(solution)/shard_map/ppermute | solution.py:252
  32.9 1.7 collective-permute-start.12
  34.6 2.0 collective-permute-start.11
  36.7 2.5 collective-permute-start.5
  39.2 9.7 %collective-permute-done.12 = bf16[128,640]{1,0:T(8,128)(2,1)S(1)} collective-permute-done((bf16[128,640]{1,0:T(8,128)(2,1)}, bf16[128,640]{1,0:T(8,128)(2,1)S(1)}, u32[]{:S(2)}, u32[]{:S(2)}) %collective-permute-start.12) | collective-permute-done | bytes 163872 | tf_op jit(solution)/shard_map/ppermute | solution.py:252
  48.9 1.5 collective-permute-start.4
  50.5 1.5 collective-permute-start.3
  52.8 4.1 collective-permute-done.16
  57.0 13.7 %collective-permute-done.15 = bf16[240,640]{1,0:T(8,128)(2,1)S(1)} collective-permute-done((bf16[240,640]{1,0:T(8,128)(2,1)}, bf16[240,640]{1,0:T(8,128)(2,1)S(1)}, u32[]{:S(2)}, u32[]{:S(2)}) %collective-permute-start.15) | collective-permute-done | bytes 307232 | tf_op jit(solution)/shard_map/ppermute | solution.py:252
  72.5 2.4 collective-permute-start.22
  77.7 16.3 %project.2 = (bf16[1024,1920]{1,0:T(8,128)(2,1)}, bf16[1280,1920]{1,0:T(8,128)(2,1)}, bf16[8,16,640]{2,1,0:T(8,128)(2,1)}, bf16[1024,1280]{1,0:T(8,128)(2,1)}, bf16[1280,1024]{1,0:T(8,128)(2,1)}) custom-call(s32[4]{0:T(128)} %pad_add_fusion.place_ref, f32[8,640]{1,0:T(8,128)} %broadcast_in_dim.23.scale_ref, bf16[1024,1280]{1,0:T(8,128)(2,1)} %x_ref.3, ...), custom_call_target="tpu_custom_call" | custom-call | flops 125829120 | bytes 409600 | tf_op jit(solution)/shard_map/project/pallas_call | solution.py:262
  94.0 3.3 collective-permute-done.21.refs_3_
  99.0 1.7 collective-permute-start.19
  100.8 1.3 collective-permute-start.18
  103.1 1.6 collective-permute-done.26.refs_8_
  105.5 12.7 %attend_forward.2 = (bf16[1024,1280]{1,0:T(8,128)(2,1)}, bf16[8,1024,128]{2,1,0:T(8,128)(2,1)}, bf16[8,1024,128]{2,1,0:T(8,128)(2,1)}, bf16[8,1024,128]{2,1,0:T(8,128)(2,1)}) custom-call(s32[1]{0:T(128)} %copy.33.len_ref, bf16[1024,1920]{1,0:T(8,128)(2,1)} %get-tuple-element.128.qkv_ref), custom_call_target="tpu_custom_call" | custom-call | flops 251658240 | tf_op jit(solution)/shard_map/attend_forward/pallas_call | solution.py:138
  119.0 14.1 %project.3 = (bf16[1024,1920]{1,0:T(8,128)(2,1)}, bf16[1280,1920]{1,0:T(8,128)(2,1)}) custom-call(s32[4]{0:T(128)} %pad_add_fusion.place_ref, f32[8,640]{1,0:T(8,128)} %broadcast_in_dim.23.scale_ref, bf16[1024,1280]{1,0:T(8,128)(2,1)} %get-tuple-element.130.x_ref, bf16[512,640]{1,0:T(8,128)(2,1)} %get-tuple-element.131.refs_0_, ...), custom_call_target="tpu_custom_call" | custom-call | flops 125829120 | bytes 409600 | tf_op jit(solution)/shard_map/project/pallas_call | solution.py:262
  133.2 12.5 %attend_forward.3 = (bf16[1024,1280]{1,0:T(8,128)(2,1)}, bf16[8,1024,128]{2,1,0:T(8,128)(2,1)}, bf16[8,1024,128]{2,1,0:T(8,128)(2,1)}, bf16[8,1024,128]{2,1,0:T(8,128)(2,1)}) custom-call(s32[1]{0:T(128)} %copy.33.len_ref, bf16[1024,1920]{1,0:T(8,128)(2,1)} %get-tuple-element.139.qkv_ref, ...), custom_call_target="tpu_custom_call", output_to_operand_aliasing={{0}: (2, {})} | custom-call | flops 251658240 | tf_op jit(solution)/shard_map/attend_forward/pallas_call | solution.py:138
  146.8 1.7 broadcast_select_fusion.refs_12_.refs_0_
  149.9 1.3 collective-permute-done.31.refs_8_
  151.3 1.3 collective-permute-done.32.refs_9_
  153.8 25.2 %mlp_forward.1 = (bf16[1280,1280]{1,0:T(8,128)(2,1)}, bf16[1280,1280]{1,0:T(8,128)(2,1)}, bf16[1280,1280]{1,0:T(8,128)(2,1)}, f32[1024,1280]{1,0:T(8,128)}, bf16...) custom-call(s32[4]{0:T(128)} %pad_add_fusion.place_ref, ...), custom_call_target="tpu_custom_call" | custom-call | flops 251658240 | bytes 1376256 | tf_op jit(solution)/shard_map/mlp_forward/pallas_call | solution.py:262
  179.1 28.6 %mlp_backward.1 = (bf16[1280,2560]{1,0:T(8,128)(2,1)}, f32[1024,1280]{1,0:T(8,128)}, bf16[1024,1280]{1,0:T(8,128)(2,1)}, f32[8,1280]{1,0:T(8,128)}) custom-call(f32[8,1280]{1,0:T(8,128)} %broadcast_in_dim.24.gain_ref, bf16[1024,1280]{1,0:T(8,128)(2,1)} %broadcast_select_fusion.refs_12_.refs_0_, bf16[1280,1280]{1,0:T(8,128)(2,1)} %get-tuple-element.151.refs_1_, ...), custom_call_target="tpu_custom_call" | custom-call | flops 419430400 | bytes 1261568 | tf_op jit(solution)/shard_map/mlp_backward/pallas_call | solution.py:262
  209.4 20.5 %attend_backward.2 = (bf16[1024,1920]{1,0:T(8,128)(2,1)}, f32[8,128]{1,0:T(8,128)}) custom-call(f32[8,128]{1,0:T(8,128)} %broadcast_in_dim.28.fac_ref, bf16[8,1024,128]{2,1,0:T(8,128)(2,1)} %get-tuple-element.157.qa_ref, bf16[8,1024,128]{2,1,0:T(8,128)(2,1)} %get-tuple-element.158.ka_ref, bf16[8,1024,128]{2,1,0:T(8,128)(2,1)} %get-tuple-element.159.va_ref, ...), custom_call_target="tpu_custom_call" | custom-call | flops 503316480 | tf_op jit(solution)/shard_map/attend_backward/pallas_call | solution.py:220
  230.6 12.7 %weight_grads.2 = (bf16[4,512,640]{2,1,0:T(8,128)(2,1)}, bf16[4,512,640]{2,1,0:T(8,128)(2,1)}) custom-call(s32[4]{0:T(128)} %pad_add_fusion.place_ref, bf16[1280,1024]{1,0:T(8,128)(2,1)} %get-tuple-element.147.left_ref, bf16[1024,1920]{1,0:T(8,128)(2,1)} %get-tuple-element.160.right_ref.grad_a, bf16[8,32,640]{2,1,0:T(8,128)(2,1)} %fusion.5.vec_ref), custom_call_target="tpu_custom_call" | custom-call | flops 125829120 | bytes 286720 | tf_op jit(solution)/shard_map/weight_grads/pallas_call | solution.py:262
  243.7 4.8 %collective-permute-done.33 = bf16[4,512,640]{2,1,0:T(8,128)(2,1)S(1)} collective-permute-done((bf16[4,512,640]{2,1,0:T(8,128)(2,1)}, bf16[4,512,640]{2,1,0:T(8,128)(2,1)S(1)}, u32[]{:S(2)}, u32[]{:S(2)}) %collective-permute-start.33) | collective-permute-done | bytes 2621472 | tf_op jit(solution)/shard_map/ppermute | solution.py:255
  248.5 1.5 copy-done.4
  249.9 4.8 %fold_cores.2 = (bf16[4,2,64,640]{3,2,1,0:T(8,128)(2,1)}, bf16[4,2,64,640]{3,2,1,0:T(8,128)(2,1)}, bf16[4,2,64,640]{3,2,1,0:T(8,128)(2,1)}, bf16[4,2,64,640]{3,2,1,0:T(8,128)(2,1)}) custom-call(s32[4]{0:T(128)} %pad_add_fusion.place_ref, bf16[4,2,2,2,64,640]{5,4,3,2,1,0:T(8,128)(2,1)} %bitcast.32, bf16[4,2,2,2,64,640]{5,4,3,2,1,0:T(8,128)(2,1)} %bitcast.33), custom_call_target="tpu_custom_call" | custom-call | bytes 196608 | tf_op jit(solution)/shard_map/fold_cores/pallas_call | solution.py:262
  254.7 1.4 collective-permute-start.35
  256.6 20.3 %attend_backward.3 = (bf16[1024,1920]{1,0:T(8,128)(2,1)}, f32[8,128]{1,0:T(8,128)}) custom-call(f32[8,128]{1,0:T(8,128)} %broadcast_in_dim.28.fac_ref, bf16[8,1024,128]{2,1,0:T(8,128)(2,1)} %get-tuple-element.148.qa_ref, bf16[8,1024,128]{2,1,0:T(8,128)(2,1)} %get-tuple-element.149.ka_ref, bf16[8,1024,128]{2,1,0:T(8,128)(2,1)} %get-tuple-element.150.va_ref, ...), custom_call_target="tpu_custom_call" | custom-call | flops 503316480 | tf_op jit(solution)/shard_map/attend_backward/pallas_call | solution.py:220
  278.5 12.6 %weight_grads.3 = (bf16[4,512,640]{2,1,0:T(8,128)(2,1)}, bf16[4,512,640]{2,1,0:T(8,128)(2,1)}) custom-call(s32[4]{0:T(128)} %pad_add_fusion.place_ref, bf16[1280,1024]{1,0:T(8,128)(2,1)} %get-tuple-element.147.left_ref, bf16[1024,1920]{1,0:T(8,128)(2,1)} %get-tuple-element.168.right_ref.grad_b, bf16[8,32,640]{2,1,0:T(8,128)(2,1)} %pad.28.vec_ref), custom_call_target="tpu_custom_call" | custom-call | flops 125829120 | bytes 286720 | tf_op jit(solution)/shard_map/weight_grads/pallas_call | solution.py:262
  291.3 1.3 reduce-scatter.3.cloned.1.call-done
  294.8 4.2 fold_first.2
  299.0 4.6 %fold_cores.3 = (bf16[4,2,64,640]{3,2,1,0:T(8,128)(2,1)}, bf16[4,2,64,640]{3,2,1,0:T(8,128)(2,1)}, bf16[4,2,64,640]{3,2,1,0:T(8,128)(2,1)}, bf16[4,2,64,640]{3,2,1,0:T(8,128)(2,1)}) custom-call(s32[4]{0:T(128)} %pad_add_fusion.place_ref, bf16[4,2,2,2,64,640]{5,4,3,2,1,0:T(8,128)(2,1)} %bitcast.31, bf16[4,2,2,2,64,640]{5,4,3,2,1,0:T(8,128)(2,1)} %bitcast.18.b_ref), custom_call_target="tpu_custom_call" | custom-call | bytes 196608 | tf_op jit(solution)/shard_map/fold_cores/pallas_call | solution.py:262
  303.6 1.5 collective-permute-start.37
  305.1 1.5 collective-permute-start.40
  309.1 19.9 %input_grad.1 = bf16[1024,1280]{1,0:T(8,128)(2,1)} custom-call(bf16[1024,1280]{1,0:T(8,128)(2,1)} %x_ref.3, f32[8,1280]{1,0:T(8,128)} %broadcast_in_dim.29.gain_ref, f32[1024,1280]{1,0:T(8,128)} %get-tuple-element.186.hidden_ref, bf16[1024,1920]{1,0:T(8,128)(2,1)} %get-tuple-element.160.right_ref.grad_a, ...), custom_call_target="tpu_custom_call" | custom-call | flops 251658240 | bytes 704512 | tf_op jit(solution)/shard_map/input_grad/pallas_call | solution.py:262
  329.0 5.6 %collective-permute-done.38.low_b = bf16[4,64,640]{2,1,0:T(8,128)(2,1)S(1)} collective-permute-done((bf16[4,64,640]{2,1,0:T(8,128)(2,1)}, bf16[4,64,640]{2,1,0:T(8,128)(2,1)S(1)}, u32[]{:S(2)}, u32[]{:S(2)}) %collective-permute-start.38) | collective-permute-done | bytes 327712 | tf_op jit(solution)/shard_map/ppermute | solution.py:258
  335.3 2.2 fold_second.2
  338.1 1.4 collective-permute-start.42
  339.5 2.3 collective-permute-start.43
  342.6 3.8 fold_first.3
  346.4 1.3 collective-permute-start.47
  348.5 7.8 %add_convert_fusion = bf16[1024,1280]{1,0:T(8,128)(2,1)} fusion(f32[1024,1280]{1,0:T(8,128)S(1)} %bitcast.30, bf16[1024,1280]{1,0:T(8,128)(2,1)} %get-tuple-element.196, bf16[1280,1280]{1,0:T(8,128)(2,1)} %get-tuple-element.151.refs_1_, f32[1280]{0:T(1024)S(1)} %copy-done.46), kind=kOutput, calls=%fused_computation | convolution fusion | flops 3359375360 | bytes 13767680 | tf_op jit(solution)/shard_map/dot_general | solution.py:45
  356.9 1.9 fold_planes.2.refs_0_
  358.8 1.6 collective-permute-start.46
  361.6 13.4 %all-reduce.7.cloned.1.call-done = bf16[160,3840]{1,0:T(8,128)(2,1)} async-done(((bf16[160,3840]{1,0:T(8,128)(2,1)}), bf16[160,3840]{1,0:T(8,128)(2,1)}) %all-reduce.7.cloned.1.call-update) | async-done | bytes 1228816 | tf_op jit(solution)/shard_map/psum | solution.py:889
  375.0 2.2 fold_second.3
  377.2 1.3 collective-permute-start.50
  378.5 2.6 collective-permute-start.51
  381.1 1.5 multiply_reduce_fusion
  382.7 3.8 collective-permute-done.49.refs_1_
  387.4 5.1 %collective-permute-done.50.refs_2_ = bf16[2,64,640]{2,1,0:T(8,128)(2,1)S(1)} collective-permute-done((bf16[2,64,640]{2,1,0:T(8,128)(2,1)}, bf16[2,64,640]{2,1,0:T(8,128)(2,1)S(1)}, u32[]{:S(2)}, u32[]{:S(2)}) %collective-permute-start.50) | collective-permute-done | bytes 163872 | tf_op jit(solution)/shard_map/ppermute | solution.py:252
  393.2 1.9 fold_planes.3.refs_4_
  395.1 1.5 collective-permute-start.54
  399.2 3.3 collective-permute-done.54.refs_7_
  402.5 1.6 collective-permute-done.53.refs_6_
  405.5 3.2 finish.1
  409.9 1.3 fusion.11
  411.2 1.3 multiply_reduce_fusion.3
  412.5 1.6 multiply_reduce_fusion.1
  (229 shorter events, 38.7 us)
Async XLA Ops:
  7.2 69.4 %copy-start.50 = (bf16[80]{0:T(256)(128)(2,1)S(1)}, bf16[80]{0:T(256)(128)(2,1)}, u32[]{:S(2)}) copy-start(bf16[80]{0:T(256)(128)(2,1)} %param.27) | copy-start | bytes 484
  7.2 284.1 %reduce-scatter.5.cloned.1.call-start = ((), (), s32[]{:S(2)}) async-start(), calls=%async_computation.3 | async-start | bytes 3686400 | tf_op jit(solution)/shard_map/reduce_scatter | solution.py:864
  12.7 10.0 %collective-permute-start.2 = (bf16[128,640]{1,0:T(8,128)(2,1)}, bf16[128,640]{1,0:T(8,128)(2,1)S(1)}, u32[]{:S(2)}, u32[]{:S(2)}) collective-permute-start(bf16[128,640]{1,0:T(8,128)(2,1)} %get-tuple-element.115), channel_id=1, source_target_pairs={{0,6},{1,7},{2,0},{3,1},{4,2},{5,3},{6,4},{7,5},{8,14},{9,15},{10,... | collective-permute-start | bytes 491528 | tf_op jit(solution)/shard_map/ppermute | solution.py:252
  17.7 14.1 %collective-permute-start.1 = (bf16[128,640]{1,0:T(8,128)(2,1)}, bf16[128,640]{1,0:T(8,128)(2,1)S(1)}, u32[]{:S(2)}, u32[]{:S(2)}) collective-permute-start(bf16[128,640]{1,0:T(8,128)(2,1)} %get-tuple-element.115), channel_id=1, source_target_pairs={{0,4},{1,5},{2,6},{3,7},{4,0},{5,1},{6,2},{7,3},{8,12},{9,13},{10,... | collective-permute-start | bytes 491528 | tf_op jit(solution)/shard_map/ppermute | solution.py:252
  17.7 14.1 %collective-permute-start = (bf16[128,640]{1,0:T(8,128)(2,1)}, bf16[128,640]{1,0:T(8,128)(2,1)S(1)}, u32[]{:S(2)}, u32[]{:S(2)}) collective-permute-start(bf16[128,640]{1,0:T(8,128)(2,1)} %get-tuple-element.115), channel_id=1, source_target_pairs={{0,2},{1,3},{2,4},{3,5},{4,6},{5,7},{6,0},{7,1},{8,10},{9,11},{10,... | collective-permute-start | bytes 491528 | tf_op jit(solution)/shard_map/ppermute | solution.py:252
  31.8 7.4 %collective-permute-start.13 = (bf16[128,640]{1,0:T(8,128)(2,1)}, bf16[128,640]{1,0:T(8,128)(2,1)S(1)}, u32[]{:S(2)}, u32[]{:S(2)}) collective-permute-start(bf16[128,640]{1,0:T(8,128)(2,1)} %get-tuple-element.121), channel_id=1, source_target_pairs={{0,6},{1,7},{2,0},{3,1},{4,2},{5,3},{6,4},{7,5},{8,14},{9,15},{10,... | collective-permute-start | bytes 491528 | tf_op jit(solution)/shard_map/ppermute | solution.py:252
  32.9 16.1 %collective-permute-start.12 = (bf16[128,640]{1,0:T(8,128)(2,1)}, bf16[128,640]{1,0:T(8,128)(2,1)S(1)}, u32[]{:S(2)}, u32[]{:S(2)}) collective-permute-start(bf16[128,640]{1,0:T(8,128)(2,1)} %get-tuple-element.121), channel_id=1, source_target_pairs={{0,4},{1,5},{2,6},{3,7},{4,0},{5,1},{6,2},{7,3},{8,12},{9,13},{10,... | collective-permute-start | bytes 491528 | tf_op jit(solution)/shard_map/ppermute | solution.py:252
  34.6 14.3 %collective-permute-start.11 = (bf16[128,640]{1,0:T(8,128)(2,1)}, bf16[128,640]{1,0:T(8,128)(2,1)S(1)}, u32[]{:S(2)}, u32[]{:S(2)}) collective-permute-start(bf16[128,640]{1,0:T(8,128)(2,1)} %get-tuple-element.121), channel_id=1, source_target_pairs={{0,2},{1,3},{2,4},{3,5},{4,6},{5,7},{6,0},{7,1},{8,10},{9,11},{10,... | collective-permute-start | bytes 491528 | tf_op jit(solution)/shard_map/ppermute | solution.py:252
  36.7 41.0 %copy-start.6 = (bf16[3,128,640]{2,1,0:T(8,128)(2,1)}, bf16[3,128,640]{2,1,0:T(8,128)(2,1)S(1)}, u32[]{:S(2)}) copy-start(bf16[3,128,640]{2,1,0:T(8,128)(2,1)S(1)} %pad_maximum_fusion.1.refs_1_) | copy-start | bytes 1474564
  36.7 34.0 %collective-permute-start.5 = (bf16[3,128,640]{2,1,0:T(8,128)(2,1)S(1)}, bf16[3,128,640]{2,1,0:T(8,128)(2,1)S(1)}, u32[]{:S(2)}, u32[]{:S(2)}) collective-permute-start(bf16[3,128,640]{2,1,0:T(8,128)(2,1)S(1)} %pad_maximum_fusion.1.refs_1_), channel_id=1, source_target_pairs={{0,24},{8,16},{16,8},{24,0},{1,25},{9,17},{17,9},{25,1},{2,26},{10... | collective-permute-start | bytes 1474568 | tf_op jit(solution)/shard_map/ppermute | solution.py:258
  48.9 8.0 %collective-permute-start.16 = (bf16[240,640]{1,0:T(8,128)(2,1)}, bf16[240,640]{1,0:T(8,128)(2,1)S(1)}, u32[]{:S(2)}, u32[]{:S(2)}) collective-permute-start(bf16[240,640]{1,0:T(8,128)(2,1)} %get-tuple-element.122), channel_id=1, source_target_pairs={{0,6},{1,7},{2,0},{3,1},{4,2},{5,3},{6,4},{7,5},{8,14},{9,15},{10,... | collective-permute-start | bytes 921608 | tf_op jit(solution)/shard_map/ppermute | solution.py:252
  48.9 22.2 %collective-permute-start.4 = (bf16[3,128,640]{2,1,0:T(8,128)(2,1)S(1)}, bf16[3,128,640]{2,1,0:T(8,128)(2,1)S(1)}, u32[]{:S(2)}, u32[]{:S(2)}) collective-permute-start(bf16[3,128,640]{2,1,0:T(8,128)(2,1)S(1)} %pad_maximum_fusion.1.refs_1_), channel_id=1, source_target_pairs={{0,16},{8,24},{16,0},{24,8},{1,17},{9,25},{17,1},{25,9},{2,18},{10... | collective-permute-start | bytes 1474568 | tf_op jit(solution)/shard_map/ppermute | solution.py:258
  50.5 20.8 %collective-permute-start.3 = (bf16[3,128,640]{2,1,0:T(8,128)(2,1)S(1)}, bf16[3,128,640]{2,1,0:T(8,128)(2,1)S(1)}, u32[]{:S(2)}, u32[]{:S(2)}) collective-permute-start(bf16[3,128,640]{2,1,0:T(8,128)(2,1)S(1)} %pad_maximum_fusion.1.refs_1_), channel_id=1, source_target_pairs={{0,8},{8,0},{16,24},{24,16},{1,9},{9,1},{17,25},{25,17},{2,10},{10... | collective-permute-start | bytes 1474568 | tf_op jit(solution)/shard_map/ppermute | solution.py:258
  52.0 18.7 %collective-permute-start.15 = (bf16[240,640]{1,0:T(8,128)(2,1)}, bf16[240,640]{1,0:T(8,128)(2,1)S(1)}, u32[]{:S(2)}, u32[]{:S(2)}) collective-permute-start(bf16[240,640]{1,0:T(8,128)(2,1)} %get-tuple-element.122), channel_id=1, source_target_pairs={{0,4},{1,5},{2,6},{3,7},{4,0},{5,1},{6,2},{7,3},{8,12},{9,13},{10,... | collective-permute-start | bytes 921608 | tf_op jit(solution)/shard_map/ppermute | solution.py:252
  57.0 18.0 %collective-permute-start.6 = (bf16[512,640]{1,0:T(8,128)(2,1)}, bf16[512,640]{1,0:T(8,128)(2,1)S(1)}, u32[]{:S(2)}, u32[]{:S(2)}) collective-permute-start(bf16[512,640]{1,0:T(8,128)(2,1)} %get-tuple-element.114.refs_0_), channel_id=1, source_target_pairs={{0,1},{1,0},{2,3},{3,2},{4,5},{5,4},{6,7},{7,6},{8,9},{9,8},{10,11... | collective-permute-start | bytes 1966088 | tf_op jit(solution)/shard_map/ppermute | solution.py:255
  70.7 1.9 collective-permute-start.7
  70.7 4.8 %collective-permute-start.10 = (bf16[3,128,640]{2,1,0:T(8,128)(2,1)S(1)}, bf16[3,128,640]{2,1,0:T(8,128)(2,1)S(1)}, u32[]{:S(2)}, u32[]{:S(2)}) collective-permute-start(bf16[3,128,640]{2,1,0:T(8,128)(2,1)S(1)} %collective-permute-done.5.refs_4_), channel_id=1, source_target_pairs={{0,1},{1,0},{2,3},{3,2},{4,5},{5,4},{6,7},{7,6},{8,9},{9,8},{10,11... | collective-permute-start | bytes 1474568 | tf_op jit(solution)/shard_map/ppermute | solution.py:255
  71.2 4.8 %collective-permute-start.9 = (bf16[3,128,640]{2,1,0:T(8,128)(2,1)S(1)}, bf16[3,128,640]{2,1,0:T(8,128)(2,1)S(1)}, u32[]{:S(2)}, u32[]{:S(2)}) collective-permute-start(bf16[3,128,640]{2,1,0:T(8,128)(2,1)S(1)} %collective-permute-done.4.refs_3_), channel_id=1, source_target_pairs={{0,1},{1,0},{2,3},{3,2},{4,5},{5,4},{6,7},{7,6},{8,9},{9,8},{10,11... | collective-permute-start | bytes 1474568 | tf_op jit(solution)/shard_map/ppermute | solution.py:255
  71.3 4.9 %collective-permute-start.8 = (bf16[3,128,640]{2,1,0:T(8,128)(2,1)S(1)}, bf16[3,128,640]{2,1,0:T(8,128)(2,1)S(1)}, u32[]{:S(2)}, u32[]{:S(2)}) collective-permute-start(bf16[3,128,640]{2,1,0:T(8,128)(2,1)S(1)} %collective-permute-done.3.refs_2_), channel_id=1, source_target_pairs={{0,1},{1,0},{2,3},{3,2},{4,5},{5,4},{6,7},{7,6},{8,9},{9,8},{10,11... | collective-permute-start | bytes 1474568 | tf_op jit(solution)/shard_map/ppermute | solution.py:255
  72.5 21.5 %collective-permute-start.22 = (bf16[3,128,640]{2,1,0:T(8,128)(2,1)S(1)}, bf16[3,128,640]{2,1,0:T(8,128)(2,1)}, u32[]{:S(2)}, u32[]{:S(2)}) collective-permute-start(bf16[3,128,640]{2,1,0:T(8,128)(2,1)S(1)} %pad_maximum_fusion.2.refs_1_), channel_id=1, source_target_pairs={{0,24},{8,16},{16,8},{24,0},{1,25},{9,17},{17,9},{25,1},{2,26},{10... | collective-permute-start | bytes 1474568 | tf_op jit(solution)/shard_map/ppermute | solution.py:258
  75.0 22.3 %collective-permute-start.21 = (bf16[3,128,640]{2,1,0:T(8,128)(2,1)S(1)}, bf16[3,128,640]{2,1,0:T(8,128)(2,1)}, u32[]{:S(2)}, u32[]{:S(2)}) collective-permute-start(bf16[3,128,640]{2,1,0:T(8,128)(2,1)S(1)} %pad_maximum_fusion.2.refs_1_), channel_id=1, source_target_pairs={{0,16},{8,24},{16,0},{24,8},{1,17},{9,25},{17,1},{25,9},{2,18},{10... | collective-permute-start | bytes 1474568 | tf_op jit(solution)/shard_map/ppermute | solution.py:258
  75.5 21.9 %collective-permute-start.20 = (bf16[3,128,640]{2,1,0:T(8,128)(2,1)S(1)}, bf16[3,128,640]{2,1,0:T(8,128)(2,1)}, u32[]{:S(2)}, u32[]{:S(2)}) collective-permute-start(bf16[3,128,640]{2,1,0:T(8,128)(2,1)S(1)} %pad_maximum_fusion.2.refs_1_), channel_id=1, source_target_pairs={{0,8},{8,0},{16,24},{24,16},{1,9},{9,1},{17,25},{25,17},{2,10},{10... | collective-permute-start | bytes 1474568 | tf_op jit(solution)/shard_map/ppermute | solution.py:258
  76.0 26.0 %collective-permute-start.23 = (bf16[512,640]{1,0:T(8,128)(2,1)}, bf16[512,640]{1,0:T(8,128)(2,1)S(1)}, u32[]{:S(2)}, u32[]{:S(2)}) collective-permute-start(bf16[512,640]{1,0:T(8,128)(2,1)} %get-tuple-element.131.refs_0_), channel_id=1, source_target_pairs={{0,1},{1,0},{2,3},{3,2},{4,5},{5,4},{6,7},{7,6},{8,9},{9,8},{10,11... | collective-permute-start | bytes 1966088 | tf_op jit(solution)/shard_map/ppermute | solution.py:255
  76.2 17.8 %collective-permute-start.14 = (bf16[240,640]{1,0:T(8,128)(2,1)}, bf16[240,640]{1,0:T(8,128)(2,1)}, u32[]{:S(2)}, u32[]{:S(2)}) collective-permute-start(bf16[240,640]{1,0:T(8,128)(2,1)} %get-tuple-element.122), channel_id=1, source_target_pairs={{0,2},{1,3},{2,4},{3,5},{4,6},{5,7},{6,0},{7,1},{8,10},{9,11},{10,... | collective-permute-start | bytes 921608 | tf_op jit(solution)/shard_map/ppermute | solution.py:252
  97.4 5.2 %collective-permute-start.24 = (bf16[3,128,640]{2,1,0:T(8,128)(2,1)S(1)}, bf16[3,128,640]{2,1,0:T(8,128)(2,1)S(1)}, u32[]{:S(2)}, u32[]{:S(2)}) collective-permute-start(bf16[3,128,640]{2,1,0:T(8,128)(2,1)S(1)} %pad_maximum_fusion.2.refs_1_), channel_id=1, source_target_pairs={{0,1},{1,0},{2,3},{3,2},{4,5},{5,4},{6,7},{7,6},{8,9},{9,8},{10,11... | collective-permute-start | bytes 1474568 | tf_op jit(solution)/shard_map/ppermute | solution.py:255
  97.4 5.2 %collective-permute-start.25 = (bf16[3,128,640]{2,1,0:T(8,128)(2,1)}, bf16[3,128,640]{2,1,0:T(8,128)(2,1)S(1)}, u32[]{:S(2)}, u32[]{:S(2)}) collective-permute-start(bf16[3,128,640]{2,1,0:T(8,128)(2,1)} %collective-permute-done.20.refs_2_), channel_id=1, source_target_pairs={{0,1},{1,0},{2,3},{3,2},{4,5},{5,4},{6,7},{7,6},{8,9},{9,8},{10,11... | collective-permute-start | bytes 1474568 | tf_op jit(solution)/shard_map/ppermute | solution.py:255
  99.0 46.7 %copy-start.1 = (bf16[3,240,640]{2,1,0:T(8,128)(2,1)}, bf16[3,240,640]{2,1,0:T(8,128)(2,1)S(1)}, u32[]{:S(2)}) copy-start(bf16[3,240,640]{2,1,0:T(8,128)(2,1)S(1)} %pad_maximum_fusion.refs_1_) | copy-start | bytes 2764804
  99.0 46.7 %collective-permute-start.19 = (bf16[3,240,640]{2,1,0:T(8,128)(2,1)S(1)}, bf16[3,240,640]{2,1,0:T(8,128)(2,1)}, u32[]{:S(2)}, u32[]{:S(2)}) collective-permute-start(bf16[3,240,640]{2,1,0:T(8,128)(2,1)S(1)} %pad_maximum_fusion.refs_1_), channel_id=1, source_target_pairs={{0,24},{8,16},{16,8},{24,0},{1,25},{9,17},{17,9},{25,1},{2,26},{10... | collective-permute-start | bytes 2764808 | tf_op jit(solution)/shard_map/ppermute | solution.py:258
  100.8 44.9 %collective-permute-start.18 = (bf16[3,240,640]{2,1,0:T(8,128)(2,1)S(1)}, bf16[3,240,640]{2,1,0:T(8,128)(2,1)}, u32[]{:S(2)}, u32[]{:S(2)}) collective-permute-start(bf16[3,240,640]{2,1,0:T(8,128)(2,1)S(1)} %pad_maximum_fusion.refs_1_), channel_id=1, source_target_pairs={{0,16},{8,24},{16,0},{24,8},{1,17},{9,25},{17,1},{25,9},{2,18},{10... | collective-permute-start | bytes 2764808 | tf_op jit(solution)/shard_map/ppermute | solution.py:258
  102.1 43.6 %collective-permute-start.17 = (bf16[3,240,640]{2,1,0:T(8,128)(2,1)S(1)}, bf16[3,240,640]{2,1,0:T(8,128)(2,1)}, u32[]{:S(2)}, u32[]{:S(2)}) collective-permute-start(bf16[3,240,640]{2,1,0:T(8,128)(2,1)S(1)} %pad_maximum_fusion.refs_1_), channel_id=1, source_target_pairs={{0,8},{8,0},{16,24},{24,16},{1,9},{9,1},{17,25},{25,17},{2,10},{10... | collective-permute-start | bytes 2764808 | tf_op jit(solution)/shard_map/ppermute | solution.py:258
  102.6 2.1 collective-permute-start.26
  102.6 15.6 %collective-permute-start.27 = (bf16[3,128,640]{2,1,0:T(8,128)(2,1)}, bf16[3,128,640]{2,1,0:T(8,128)(2,1)S(1)}, u32[]{:S(2)}, u32[]{:S(2)}) collective-permute-start(bf16[3,128,640]{2,1,0:T(8,128)(2,1)} %collective-permute-done.22.refs_4_), channel_id=1, source_target_pairs={{0,1},{1,0},{2,3},{3,2},{4,5},{5,4},{6,7},{7,6},{8,9},{9,8},{10,11... | collective-permute-start | bytes 1474568 | tf_op jit(solution)/shard_map/ppermute | solution.py:255
  104.7 45.2 %collective-permute-start.28 = (bf16[960,640]{1,0:T(8,128)(2,1)S(1)}, bf16[960,640]{1,0:T(8,128)(2,1)}, u32[]{:S(2)}, u32[]{:S(2)}) collective-permute-start(bf16[960,640]{1,0:T(8,128)(2,1)S(1)} %copy-done.11), channel_id=1, source_target_pairs={{0,1},{1,0},{2,3},{3,2},{4,5},{5,4},{6,7},{7,6},{8,9},{9,8},{10,11... | collective-permute-start | bytes 3686408 | tf_op jit(solution)/shard_map/ppermute | solution.py:255
  145.7 4.1 collective-permute-start.29
  146.1 3.8 collective-permute-start.30
  146.3 4.9 %collective-permute-start.31 = (bf16[3,240,640]{2,1,0:T(8,128)(2,1)}, bf16[3,240,640]{2,1,0:T(8,128)(2,1)}, u32[]{:S(2)}, u32[]{:S(2)}) collective-permute-start(bf16[3,240,640]{2,1,0:T(8,128)(2,1)} %collective-permute-done.18.refs_3_), channel_id=1, source_target_pairs={{0,1},{1,0},{2,3},{3,2},{4,5},{5,4},{6,7},{7,6},{8,9},{9,8},{10,11... | collective-permute-start | bytes 2764808 | tf_op jit(solution)/shard_map/ppermute | solution.py:255
  146.6 5.9 %collective-permute-start.32 = (bf16[3,240,640]{2,1,0:T(8,128)(2,1)}, bf16[3,240,640]{2,1,0:T(8,128)(2,1)}, u32[]{:S(2)}, u32[]{:S(2)}) collective-permute-start(bf16[3,240,640]{2,1,0:T(8,128)(2,1)} %collective-permute-done.19.refs_4_), channel_id=1, source_target_pairs={{0,1},{1,0},{2,3},{3,2},{4,5},{5,4},{6,7},{7,6},{8,9},{9,8},{10,11... | collective-permute-start | bytes 2764808 | tf_op jit(solution)/shard_map/ppermute | solution.py:255
  179.1 113.5 %reduce-scatter.3.cloned.1.call-start = ((), (), s32[]{:S(2)}) async-start(), calls=%async_computation.2 | async-start | bytes 7372800 | tf_op jit(solution)/shard_map/reduce_scatter | solution.py:864
  207.8 167.1 %all-reduce.7.cloned.1.call-start = ((), (), s32[]{:S(2)}) async-start(), calls=%async_computation.4 | async-start | bytes 2457600 | tf_op jit(solution)/shard_map/psum | solution.py:889
  243.3 5.2 %collective-permute-start.33 = (bf16[4,512,640]{2,1,0:T(8,128)(2,1)}, bf16[4,512,640]{2,1,0:T(8,128)(2,1)S(1)}, u32[]{:S(2)}, u32[]{:S(2)}) collective-permute-start(bf16[4,512,640]{2,1,0:T(8,128)(2,1)} %get-tuple-element.163), channel_id=1, source_target_pairs={{0,1},{1,0},{2,3},{3,2},{4,5},{5,4},{6,7},{7,6},{8,9},{9,8},{10,11... | collective-permute-start | bytes 7864328 | tf_op jit(solution)/shard_map/ppermute | solution.py:255
  254.7 23.0 %collective-permute-start.35 = (bf16[4,2,64,640]{3,2,1,0:T(8,128)(2,1)}, bf16[4,2,64,640]{3,2,1,0:T(8,128)(2,1)S(1)}, u32[]{:S(2)}, u32[]{:S(2)}) collective-permute-start(bf16[4,2,64,640]{3,2,1,0:T(8,128)(2,1)} %get-tuple-element.167), channel_id=1, source_target_pairs={{0,16},{8,24},{16,0},{24,8},{1,17},{9,25},{17,1},{25,9},{2,18},{10... | collective-permute-start | bytes 1966088 | tf_op jit(solution)/shard_map/ppermute | solution.py:258
  256.0 21.6 %collective-permute-start.34 = (bf16[4,2,64,640]{3,2,1,0:T(8,128)(2,1)}, bf16[4,2,64,640]{3,2,1,0:T(8,128)(2,1)S(1)}, u32[]{:S(2)}, u32[]{:S(2)}) collective-permute-start(bf16[4,2,64,640]{3,2,1,0:T(8,128)(2,1)} %get-tuple-element.164), channel_id=1, source_target_pairs={{0,8},{8,0},{16,24},{24,16},{1,9},{9,1},{17,25},{25,17},{2,10},{10... | collective-permute-start | bytes 1966088 | tf_op jit(solution)/shard_map/ppermute | solution.py:258
  291.2 7.8 %collective-permute-start.36 = (bf16[4,512,640]{2,1,0:T(8,128)(2,1)}, bf16[4,512,640]{2,1,0:T(8,128)(2,1)}, u32[]{:S(2)}, u32[]{:S(2)}) collective-permute-start(bf16[4,512,640]{2,1,0:T(8,128)(2,1)} %get-tuple-element.172), channel_id=1, source_target_pairs={{0,1},{1,0},{2,3},{3,2},{4,5},{5,4},{6,7},{7,6},{8,9},{9,8},{10,11... | collective-permute-start | bytes 7864328 | tf_op jit(solution)/shard_map/ppermute | solution.py:255
  303.6 38.2 %collective-permute-start.37 = (bf16[4,2,64,640]{3,2,1,0:T(8,128)(2,1)}, bf16[4,2,64,640]{3,2,1,0:T(8,128)(2,1)S(1)}, u32[]{:S(2)}, u32[]{:S(2)}) collective-permute-start(bf16[4,2,64,640]{3,2,1,0:T(8,128)(2,1)} %get-tuple-element.183), channel_id=1, source_target_pairs={{0,8},{8,0},{16,24},{24,16},{1,9},{9,1},{17,25},{25,17},{2,10},{10... | collective-permute-start | bytes 1966088 | tf_op jit(solution)/shard_map/ppermute | solution.py:258
  305.1 36.7 %collective-permute-start.40 = (bf16[4,2,64,640]{3,2,1,0:T(8,128)(2,1)}, bf16[4,2,64,640]{3,2,1,0:T(8,128)(2,1)}, u32[]{:S(2)}, u32[]{:S(2)}) collective-permute-start(bf16[4,2,64,640]{3,2,1,0:T(8,128)(2,1)} %get-tuple-element.194), channel_id=1, source_target_pairs={{0,16},{8,24},{16,0},{24,8},{1,17},{9,25},{17,1},{25,9},{2,18},{10... | collective-permute-start | bytes 1966088 | tf_op jit(solution)/shard_map/ppermute | solution.py:258
  306.6 28.0 %collective-permute-start.38 = (bf16[4,64,640]{2,1,0:T(8,128)(2,1)}, bf16[4,64,640]{2,1,0:T(8,128)(2,1)S(1)}, u32[]{:S(2)}, u32[]{:S(2)}) collective-permute-start(bf16[4,64,640]{2,1,0:T(8,128)(2,1)} %get-tuple-element.180), channel_id=1, source_target_pairs={{0,16},{8,24},{16,0},{24,8},{1,17},{9,25},{17,1},{25,9},{2,18},{10... | collective-permute-start | bytes 983048 | tf_op jit(solution)/shard_map/ppermute | solution.py:258
  307.1 27.5 %collective-permute-start.39 = (bf16[4,64,640]{2,1,0:T(8,128)(2,1)}, bf16[4,64,640]{2,1,0:T(8,128)(2,1)}, u32[]{:S(2)}, u32[]{:S(2)}) collective-permute-start(bf16[4,64,640]{2,1,0:T(8,128)(2,1)} %get-tuple-element.190), channel_id=1, source_target_pairs={{0,8},{8,0},{16,24},{24,16},{1,9},{9,1},{17,25},{25,17},{2,10},{10... | collective-permute-start | bytes 983048 | tf_op jit(solution)/shard_map/ppermute | solution.py:258
  309.1 39.4 %slice-start = ((s8[5242880]{0:T(1024)(128)(4,1)}), s8[4194304]{0:T(1024)(128)(4,1)S(1)}, s32[]{:S(2)}) async-start(s8[5242880]{0:T(1024)(128)(4,1)} %bitcast.29), calls=%async_computation.5 | async-start | bytes 8388608
  309.1 39.4 %slice-start.1 = ((s8[5242880]{0:T(1024)(128)(4,1)}), s8[1048576]{0:T(1024)(128)(4,1)S(1)}, s32[]{:S(2)}) async-start(s8[5242880]{0:T(1024)(128)(4,1)} %bitcast.29), calls=%async_computation.6 | async-start | bytes 2097152
  337.5 18.8 %collective-permute-start.41 = (bf16[2,64,640]{2,1,0:T(8,128)(2,1)}, bf16[2,64,640]{2,1,0:T(8,128)(2,1)S(1)}, u32[]{:S(2)}, u32[]{:S(2)}) collective-permute-start(bf16[2,64,640]{2,1,0:T(8,128)(2,1)} %get-tuple-element.197), channel_id=1, source_target_pairs={{0,2},{1,3},{2,4},{3,5},{4,6},{5,7},{6,0},{7,1},{8,10},{9,11},{10,... | collective-permute-start | bytes 491528 | tf_op jit(solution)/shard_map/ppermute | solution.py:252
  338.1 18.2 %collective-permute-start.42 = (bf16[2,64,640]{2,1,0:T(8,128)(2,1)}, bf16[2,64,640]{2,1,0:T(8,128)(2,1)}, u32[]{:S(2)}, u32[]{:S(2)}) collective-permute-start(bf16[2,64,640]{2,1,0:T(8,128)(2,1)} %get-tuple-element.198), channel_id=1, source_target_pairs={{0,4},{1,5},{2,6},{3,7},{4,0},{5,1},{6,2},{7,3},{8,12},{9,13},{10,... | collective-permute-start | bytes 491528 | tf_op jit(solution)/shard_map/ppermute | solution.py:252
  339.5 16.8 %collective-permute-start.43 = (bf16[2,64,640]{2,1,0:T(8,128)(2,1)}, bf16[2,64,640]{2,1,0:T(8,128)(2,1)}, u32[]{:S(2)}, u32[]{:S(2)}) collective-permute-start(bf16[2,64,640]{2,1,0:T(8,128)(2,1)} %get-tuple-element.199), channel_id=1, source_target_pairs={{0,6},{1,7},{2,0},{3,1},{4,2},{5,3},{6,4},{7,5},{8,14},{9,15},{10,... | collective-permute-start | bytes 491528 | tf_op jit(solution)/shard_map/ppermute | solution.py:252
  346.4 15.2 %collective-permute-start.47 = (bf16[4,64,640]{2,1,0:T(8,128)(2,1)}, bf16[4,64,640]{2,1,0:T(8,128)(2,1)S(1)}, u32[]{:S(2)}, u32[]{:S(2)}) collective-permute-start(bf16[4,64,640]{2,1,0:T(8,128)(2,1)} %get-tuple-element.195), channel_id=1, source_target_pairs={{0,16},{8,24},{16,0},{24,8},{1,17},{9,25},{17,1},{25,9},{2,18},{10... | collective-permute-start | bytes 983048 | tf_op jit(solution)/shard_map/ppermute | solution.py:258
  347.7 33.4 %copy-start.7 = (bf16[160,1280]{1,0:T(8,128)(2,1)S(1)}, bf16[160,1280]{1,0:T(8,128)(2,1)}, u32[]{:S(2)}) copy-start(bf16[160,1280]{1,0:T(8,128)(2,1)} %refs_4_.1) | copy-start | bytes 1228804
  347.7 27.2 %collective-permute-start.48 = (bf16[4,64,640]{2,1,0:T(8,128)(2,1)}, bf16[4,64,640]{2,1,0:T(8,128)(2,1)}, u32[]{:S(2)}, u32[]{:S(2)}) collective-permute-start(bf16[4,64,640]{2,1,0:T(8,128)(2,1)} %get-tuple-element.206), channel_id=1, source_target_pairs={{0,8},{8,0},{16,24},{24,16},{1,9},{9,1},{17,25},{25,17},{2,10},{10... | collective-permute-start | bytes 983048 | tf_op jit(solution)/shard_map/ppermute | solution.py:258
  358.8 38.7 %collective-permute-start.46 = (bf16[2,64,640]{2,1,0:T(8,128)(2,1)}, bf16[2,64,640]{2,1,0:T(8,128)(2,1)S(1)}, u32[]{:S(2)}, u32[]{:S(2)}) collective-permute-start(bf16[2,64,640]{2,1,0:T(8,128)(2,1)} %fold_planes.2.refs_0_), channel_id=1, source_target_pairs={{0,24},{8,16},{16,8},{24,0},{1,25},{9,17},{17,9},{25,1},{2,26},{10... | collective-permute-start | bytes 491528 | tf_op jit(solution)/shard_map/ppermute | solution.py:258
  360.4 38.8 %collective-permute-start.45 = (bf16[2,64,640]{2,1,0:T(8,128)(2,1)}, bf16[2,64,640]{2,1,0:T(8,128)(2,1)S(1)}, u32[]{:S(2)}, u32[]{:S(2)}) collective-permute-start(bf16[2,64,640]{2,1,0:T(8,128)(2,1)} %fold_planes.2.refs_0_), channel_id=1, source_target_pairs={{0,16},{8,24},{16,0},{24,8},{1,17},{9,25},{17,1},{25,9},{2,18},{10... | collective-permute-start | bytes 491528 | tf_op jit(solution)/shard_map/ppermute | solution.py:258
  377.2 9.2 %collective-permute-start.49 = (bf16[2,64,640]{2,1,0:T(8,128)(2,1)}, bf16[2,64,640]{2,1,0:T(8,128)(2,1)S(1)}, u32[]{:S(2)}, u32[]{:S(2)}) collective-permute-start(bf16[2,64,640]{2,1,0:T(8,128)(2,1)} %get-tuple-element.208), channel_id=1, source_target_pairs={{0,2},{1,3},{2,4},{3,5},{4,6},{5,7},{6,0},{7,1},{8,10},{9,11},{10,... | collective-permute-start | bytes 491528 | tf_op jit(solution)/shard_map/ppermute | solution.py:252
  377.2 15.2 %collective-permute-start.50 = (bf16[2,64,640]{2,1,0:T(8,128)(2,1)}, bf16[2,64,640]{2,1,0:T(8,128)(2,1)S(1)}, u32[]{:S(2)}, u32[]{:S(2)}) collective-permute-start(bf16[2,64,640]{2,1,0:T(8,128)(2,1)} %get-tuple-element.209), channel_id=1, source_target_pairs={{0,4},{1,5},{2,6},{3,7},{4,0},{5,1},{6,2},{7,3},{8,12},{9,13},{10,... | collective-permute-start | bytes 491528 | tf_op jit(solution)/shard_map/ppermute | solution.py:252
  378.5 14.0 %collective-permute-start.51 = (bf16[2,64,640]{2,1,0:T(8,128)(2,1)}, bf16[2,64,640]{2,1,0:T(8,128)(2,1)S(1)}, u32[]{:S(2)}, u32[]{:S(2)}) collective-permute-start(bf16[2,64,640]{2,1,0:T(8,128)(2,1)} %get-tuple-element.210), channel_id=1, source_target_pairs={{0,6},{1,7},{2,0},{3,1},{4,2},{5,3},{6,4},{7,5},{8,14},{9,15},{10,... | collective-permute-start | bytes 491528 | tf_op jit(solution)/shard_map/ppermute | solution.py:252
  386.4 12.7 %collective-permute-start.44 = (bf16[2,64,640]{2,1,0:T(8,128)(2,1)S(1)}, bf16[2,64,640]{2,1,0:T(8,128)(2,1)S(1)}, u32[]{:S(2)}, u32[]{:S(2)}) collective-permute-start(bf16[2,64,640]{2,1,0:T(8,128)(2,1)S(1)} %copy-done.14), channel_id=1, source_target_pairs={{0,8},{8,0},{16,24},{24,16},{1,9},{9,1},{17,25},{25,17},{2,10},{10... | collective-permute-start | bytes 491528 | tf_op jit(solution)/shard_map/ppermute | solution.py:258
  395.1 7.4 %collective-permute-start.54 = (bf16[2,64,640]{2,1,0:T(8,128)(2,1)}, bf16[2,64,640]{2,1,0:T(8,128)(2,1)S(1)}, u32[]{:S(2)}, u32[]{:S(2)}) collective-permute-start(bf16[2,64,640]{2,1,0:T(8,128)(2,1)} %fold_planes.3.refs_4_), channel_id=1, source_target_pairs={{0,24},{8,16},{16,8},{24,0},{1,25},{9,17},{17,9},{25,1},{2,26},{10... | collective-permute-start | bytes 491528 | tf_op jit(solution)/shard_map/ppermute | solution.py:258
  396.6 7.5 %collective-permute-start.53 = (bf16[2,64,640]{2,1,0:T(8,128)(2,1)}, bf16[2,64,640]{2,1,0:T(8,128)(2,1)S(1)}, u32[]{:S(2)}, u32[]{:S(2)}) collective-permute-start(bf16[2,64,640]{2,1,0:T(8,128)(2,1)} %fold_planes.3.refs_4_), channel_id=1, source_target_pairs={{0,16},{8,24},{16,0},{24,8},{1,17},{9,25},{17,1},{25,9},{2,18},{10... | collective-permute-start | bytes 491528 | tf_op jit(solution)/shard_map/ppermute | solution.py:258
  397.5 6.7 %collective-permute-start.52 = (bf16[2,64,640]{2,1,0:T(8,128)(2,1)}, bf16[2,64,640]{2,1,0:T(8,128)(2,1)S(1)}, u32[]{:S(2)}, u32[]{:S(2)}) collective-permute-start(bf16[2,64,640]{2,1,0:T(8,128)(2,1)} %fold_planes.3.refs_4_), channel_id=1, source_target_pairs={{0,8},{8,0},{16,24},{24,16},{1,9},{9,1},{17,25},{25,17},{2,10},{10... | collective-permute-start | bytes 491528 | tf_op jit(solution)/shard_map/ppermute | solution.py:258
  (47 other events, 465.2 us)
Sparse Core Ops, SparseCore 0:
  179.2 39.7 reduce-scatter.4
  221.4 71.0 reduce-scatter.2
  307.8 67.0 all-reduce.6

commit v2 on v0

--- a/solution.py
+++ b/solution.py
@@ -440,7 +440,7 @@
             )
             copy.start()
             written.append(copy)
-    for load in loads:
+    for load in loads[:2]:
         load.wait()
 
     def tile(t):
@@ -459,6 +459,7 @@
         act[:, across] = (value * jax.nn.sigmoid(value)).astype(bf16)
     keep(pre, pre_ref, 5)
     keep(act, act_ref, 6)
+    loads[2].wait()
     down_grad[...] = tn(act[...], grad[...]).astype(bf16)
     keep(down_grad, down_grad_ref, 7)
     for copy in written:
@@ -502,7 +503,7 @@
         (
             ("grad", grad_ref, grad),
             ("down", down_ref, down),
-            ("pre", pre_ref, wide),
+            *[(f"pre{at.start}", pre_ref.at[at, :], wide.at[at, :]) for at in in_blocks()],
             ("mlp_in", mlp_in_ref, mlp_in),
             ("up", up_ref, up),
             ("hidden", hidden_ref, hidden),
@@ -515,14 +516,15 @@
     written = []
 
     def keep(source, target):
-        copy = pltpu.make_async_copy(source, target, sem.at[8 + len(written)])
+        copy = pltpu.make_async_copy(source, target, sem.at[7 + SEQ // BLOCK + len(written)])
         copy.start()
         written.append(copy)
 
-    for name in ("grad", "down", "pre"):
+    for name in ("grad", "down"):
         loads[name].wait()
     sums = jnp.zeros((1, D), f32)
     for at in in_blocks():
+        loads[f"pre{at.start}"].wait()
         pre = wide[at, :]
         sigma = jax.nn.sigmoid(pre)
         value = (nt(grad[at, :], down[...]) * (sigma * (1.0 + pre * (1.0 - sigma)))).astype(bf16)
@@ -563,7 +565,7 @@
         [jax.ShapeDtypeStruct(*o) for o in (square, high, low, square, ((8, D), f32))],
         scratch=[
             *[pltpu.VMEM(*v) for v in (low, square, high, low, square, high, square, low, low, low, square, square)],
-            pltpu.SemaphoreType.DMA((12,)),
+            pltpu.SemaphoreType.DMA((11 + SEQ // BLOCK,)),
         ],
         flops=10 * SEQ * D * D,
         nbytes=10 * D * D + 26 * SEQ * D,

time: 410 us -> 409 us (level)
  no operation moved by 1% of the time
where the time goes in v2:
time: 409 us; the launch traced here: 405 us
  Pallas kernels  226 us (55%)
  waiting for transfers between devices  68.6 us (17%)
  starting transfers between devices  52.6 us (13%)
  local copies, waits for them, and re-layouts  22 us (5%)
  between operations  15.4 us (4%)
  other arithmetic  12.8 us (3%)
  matrix products  7.91 us (2%)
    pallas_call x17, Pallas kernels, kernel_call(): pl.pallas_call(kernel, out_shape=outs, scratch_shapes=scratch, compiler_p...  160 us
    ppermute x15, waiting for transfers between devices, along_z(): return lax.ppermute(v, 'fsdp', pairs)  45.2 us
    pallas_call x2, Pallas kernels, attend_backward(): pl.pallas_call(functools.partial(backward_kernel, GROUP), grid=(1,), in_s...  40.7 us
    ppermute x23, starting transfers between devices, across(): lax.ppermute(v, 'replica', [(i, i ^ code) for i in range(self.copies)])  28.1 us
    pallas_call x2, Pallas kernels, attend_forward(): pl.pallas_call(kernel, grid=(1,), in_specs=[pl.BlockSpec(memory_space=plt...  25.3 us
    ppermute x15, starting transfers between devices, along_z(): return lax.ppermute(v, 'fsdp', pairs)  20.6 us
    unnamed x112, local copies, waits for them, and re-layouts  11.1 us
    ppermute x17, waiting for transfers between devices, other_core(): return lax.ppermute(v, 'fsdp', [(i, i ^ 1) for i in range(self.owners)])  9.81 us
  transfers between devices with their start and end apart: 59, of which 19 were waited for; matrix products, arithmetic and copies ran while one was open for 6% of the time, Pallas kernels for 48%

profile of v2, /device:TPU:0, one launch (start us, length us, event | category | flops | bytes accessed | tf_op | source)
XLA Modules:
  0.0 405.2 jit_solution(14035422141185274758)
XLA Ops:
  9.3 3.4 cut.1
  12.7 5.0 %collective-permute-start.2 = (bf16[128,640]{1,0:T(8,128)(2,1)}, bf16[128,640]{1,0:T(8,128)(2,1)S(1)}, u32[]{:S(2)}, u32[]{:S(2)}) collective-permute-start(bf16[128,640]{1,0:T(8,128)(2,1)} %get-tuple-element.120), channel_id=1, source_target_pairs={{0,6},{1,7},{2,0},{3,1},{4,2},{5,3},{6,4},{7,5},{8,14},{9,15},{10,... | collective-permute-start | bytes 491528 | tf_op jit(solution)/shard_map/ppermute | solution.py:252
  18.7 3.9 collective-permute-done.2
  22.7 9.1 %collective-permute-done.1 = bf16[128,640]{1,0:T(8,128)(2,1)S(1)} collective-permute-done((bf16[128,640]{1,0:T(8,128)(2,1)}, bf16[128,640]{1,0:T(8,128)(2,1)S(1)}, u32[]{:S(2)}, u32[]{:S(2)}) %collective-permute-start.1) | collective-permute-done | bytes 163872 | tf_op jit(solution)/shard_map/ppermute | solution.py:252
  32.9 1.7 collective-permute-start.12
  34.6 2.0 collective-permute-start.11
  36.7 2.5 collective-permute-start.5
  39.2 9.7 %collective-permute-done.12 = bf16[128,640]{1,0:T(8,128)(2,1)S(1)} collective-permute-done((bf16[128,640]{1,0:T(8,128)(2,1)}, bf16[128,640]{1,0:T(8,128)(2,1)S(1)}, u32[]{:S(2)}, u32[]{:S(2)}) %collective-permute-start.12) | collective-permute-done | bytes 163872 | tf_op jit(solution)/shard_map/ppermute | solution.py:252
  49.0 1.5 collective-permute-start.4
  50.5 1.5 collective-permute-start.3
  52.9 4.1 %collective-permute-done.16 = bf16[240,640]{1,0:T(8,128)(2,1)S(1)} collective-permute-done((bf16[240,640]{1,0:T(8,128)(2,1)}, bf16[240,640]{1,0:T(8,128)(2,1)S(1)}, u32[]{:S(2)}, u32[]{:S(2)}) %collective-permute-start.16) | collective-permute-done | bytes 307232 | tf_op jit(solution)/shard_map/ppermute | solution.py:252
  57.0 13.7 %collective-permute-done.15 = bf16[240,640]{1,0:T(8,128)(2,1)S(1)} collective-permute-done((bf16[240,640]{1,0:T(8,128)(2,1)}, bf16[240,640]{1,0:T(8,128)(2,1)S(1)}, u32[]{:S(2)}, u32[]{:S(2)}) %collective-permute-start.15) | collective-permute-done | bytes 307232 | tf_op jit(solution)/shard_map/ppermute | solution.py:252
  72.5 2.4 collective-permute-start.22
  77.7 16.3 %project.2 = (bf16[1024,1920]{1,0:T(8,128)(2,1)}, bf16[1280,1920]{1,0:T(8,128)(2,1)}, bf16[8,16,640]{2,1,0:T(8,128)(2,1)}, bf16[1024,1280]{1,0:T(8,128)(2,1)}, bf16[1280,1024]{1,0:T(8,128)(2,1)}) custom-call(s32[4]{0:T(128)} %pad_add_fusion.place_ref, f32[8,640]{1,0:T(8,128)} %broadcast_in_dim.23.scale_ref, bf16[1024,1280]{1,0:T(8,128)(2,1)} %x_ref.3, ...), custom_call_target="tpu_custom_call" | custom-call | flops 125829120 | bytes 409600 | tf_op jit(solution)/shard_map/project/pallas_call | solution.py:262
  94.1 3.3 collective-permute-done.21.refs_3_
  99.1 1.7 collective-permute-start.19
  100.8 1.3 collective-permute-start.18
  103.1 1.6 collective-permute-done.26.refs_8_
  105.5 12.7 %attend_forward.2 = (bf16[1024,1280]{1,0:T(8,128)(2,1)}, bf16[8,1024,128]{2,1,0:T(8,128)(2,1)}, bf16[8,1024,128]{2,1,0:T(8,128)(2,1)}, bf16[8,1024,128]{2,1,0:T(8,128)(2,1)}) custom-call(s32[1]{0:T(128)} %copy.34.len_ref, bf16[1024,1920]{1,0:T(8,128)(2,1)} %get-tuple-element.133.qkv_ref), custom_call_target="tpu_custom_call" | custom-call | flops 251658240 | tf_op jit(solution)/shard_map/attend_forward/pallas_call | solution.py:138
  119.1 14.1 %project.3 = (bf16[1024,1920]{1,0:T(8,128)(2,1)}, bf16[1280,1920]{1,0:T(8,128)(2,1)}) custom-call(s32[4]{0:T(128)} %pad_add_fusion.place_ref, f32[8,640]{1,0:T(8,128)} %broadcast_in_dim.23.scale_ref, bf16[1024,1280]{1,0:T(8,128)(2,1)} %get-tuple-element.135.x_ref, bf16[512,640]{1,0:T(8,128)(2,1)} %get-tuple-element.136.refs_0_, ...), custom_call_target="tpu_custom_call" | custom-call | flops 125829120 | bytes 409600 | tf_op jit(solution)/shard_map/project/pallas_call | solution.py:262
  133.2 12.5 %attend_forward.3 = (bf16[1024,1280]{1,0:T(8,128)(2,1)}, bf16[8,1024,128]{2,1,0:T(8,128)(2,1)}, bf16[8,1024,128]{2,1,0:T(8,128)(2,1)}, bf16[8,1024,128]{2,1,0:T(8,128)(2,1)}) custom-call(s32[1]{0:T(128)} %copy.34.len_ref, bf16[1024,1920]{1,0:T(8,128)(2,1)} %get-tuple-element.144.qkv_ref, ...), custom_call_target="tpu_custom_call", output_to_operand_aliasing={{0}: (2, {})} | custom-call | flops 251658240 | tf_op jit(solution)/shard_map/attend_forward/pallas_call | solution.py:138
  146.9 1.7 broadcast_select_fusion.refs_12_.refs_0_
  150.0 1.3 collective-permute-done.31.refs_8_
  151.3 1.3 collective-permute-done.32.refs_9_
  153.8 24.3 %mlp_forward.1 = (bf16[1280,1280]{1,0:T(8,128)(2,1)}, bf16[1280,1280]{1,0:T(8,128)(2,1)}, bf16[1280,1280]{1,0:T(8,128)(2,1)}, f32[1024,1280]{1,0:T(8,128)}, bf16...) custom-call(s32[4]{0:T(128)} %pad_add_fusion.place_ref, ...), custom_call_target="tpu_custom_call" | custom-call | flops 251658240 | bytes 1376256 | tf_op jit(solution)/shard_map/mlp_forward/pallas_call | solution.py:262
  178.2 28.3 %mlp_backward.1 = (bf16[1280,1280]{1,0:T(8,128)(2,1)}, f32[1024,1280]{1,0:T(8,128)}, bf16[1024,1280]{1,0:T(8,128)(2,1)}, bf16[1280,1280]{1,0:T(8,128)(2,1)}, f32[8,1280]{1,0:T(8,128)}) custom-call(f32[8,1280]{1,0:T(8,128)} %broadcast_in_dim.24.gain_ref, bf16[1024,1280]{1,0:T(8,128)(2,1)} %broadcast_select_fusion.refs_12_.refs_0_, ...), custom_call_target="tpu_custom_call" | custom-call | flops 419430400 | bytes 1261568 | tf_op jit(solution)/shard_map/mlp_backward/pallas_call | solution.py:262
  208.2 20.4 %attend_backward.2 = (bf16[1024,1920]{1,0:T(8,128)(2,1)}, f32[8,128]{1,0:T(8,128)}) custom-call(f32[8,128]{1,0:T(8,128)} %broadcast_in_dim.28.fac_ref, bf16[8,1024,128]{2,1,0:T(8,128)(2,1)} %get-tuple-element.162.qa_ref, bf16[8,1024,128]{2,1,0:T(8,128)(2,1)} %get-tuple-element.163.ka_ref, bf16[8,1024,128]{2,1,0:T(8,128)(2,1)} %get-tuple-element.164.va_ref, ...), custom_call_target="tpu_custom_call" | custom-call | flops 503316480 | tf_op jit(solution)/shard_map/attend_backward/pallas_call | solution.py:220
  229.4 12.7 %weight_grads.2 = (bf16[4,512,640]{2,1,0:T(8,128)(2,1)}, bf16[4,512,640]{2,1,0:T(8,128)(2,1)}) custom-call(s32[4]{0:T(128)} %pad_add_fusion.place_ref, bf16[1280,1024]{1,0:T(8,128)(2,1)} %get-tuple-element.152.left_ref, bf16[1024,1920]{1,0:T(8,128)(2,1)} %get-tuple-element.165.right_ref.grad_a, bf16[8,32,640]{2,1,0:T(8,128)(2,1)} %fusion.5.vec_ref), custom_call_target="tpu_custom_call" | custom-call | flops 125829120 | bytes 286720 | tf_op jit(solution)/shard_map/weight_grads/pallas_call | solution.py:262
  242.5 4.8 %collective-permute-done.33 = bf16[4,512,640]{2,1,0:T(8,128)(2,1)S(1)} collective-permute-done((bf16[4,512,640]{2,1,0:T(8,128)(2,1)}, bf16[4,512,640]{2,1,0:T(8,128)(2,1)S(1)}, u32[]{:S(2)}, u32[]{:S(2)}) %collective-permute-start.33) | collective-permute-done | bytes 2621472 | tf_op jit(solution)/shard_map/ppermute | solution.py:255
  247.3 1.4 copy-done.3
  248.7 4.7 %fold_cores.2 = (bf16[4,2,64,640]{3,2,1,0:T(8,128)(2,1)}, bf16[4,2,64,640]{3,2,1,0:T(8,128)(2,1)}, bf16[4,2,64,640]{3,2,1,0:T(8,128)(2,1)}, bf16[4,2,64,640]{3,2,1,0:T(8,128)(2,1)}) custom-call(s32[4]{0:T(128)} %pad_add_fusion.place_ref, bf16[4,2,2,2,64,640]{5,4,3,2,1,0:T(8,128)(2,1)} %bitcast.33, bf16[4,2,2,2,64,640]{5,4,3,2,1,0:T(8,128)(2,1)} %bitcast.34), custom_call_target="tpu_custom_call" | custom-call | bytes 196608 | tf_op jit(solution)/shard_map/fold_cores/pallas_call | solution.py:262
  253.5 1.5 collective-permute-start.35
  255.9 20.3 %attend_backward.3 = (bf16[1024,1920]{1,0:T(8,128)(2,1)}, f32[8,128]{1,0:T(8,128)}) custom-call(f32[8,128]{1,0:T(8,128)} %broadcast_in_dim.28.fac_ref, bf16[8,1024,128]{2,1,0:T(8,128)(2,1)} %get-tuple-element.153.qa_ref, bf16[8,1024,128]{2,1,0:T(8,128)(2,1)} %get-tuple-element.154.ka_ref, bf16[8,1024,128]{2,1,0:T(8,128)(2,1)} %get-tuple-element.155.va_ref, ...), custom_call_target="tpu_custom_call" | custom-call | flops 503316480 | tf_op jit(solution)/shard_map/attend_backward/pallas_call | solution.py:220
  277.8 12.7 %weight_grads.3 = (bf16[4,512,640]{2,1,0:T(8,128)(2,1)}, bf16[4,512,640]{2,1,0:T(8,128)(2,1)}) custom-call(s32[4]{0:T(128)} %pad_add_fusion.place_ref, bf16[1280,1024]{1,0:T(8,128)(2,1)} %get-tuple-element.152.left_ref, bf16[1024,1920]{1,0:T(8,128)(2,1)} %get-tuple-element.173.right_ref.grad_b, bf16[8,32,640]{2,1,0:T(8,128)(2,1)} %pad.28.vec_ref), custom_call_target="tpu_custom_call" | custom-call | flops 125829120 | bytes 286720 | tf_op jit(solution)/shard_map/weight_grads/pallas_call | solution.py:262
  291.9 3.8 fold_first.2
  297.4 1.5 copy-done.2
  298.9 4.6 %fold_cores.3 = (bf16[4,2,64,640]{3,2,1,0:T(8,128)(2,1)}, bf16[4,2,64,640]{3,2,1,0:T(8,128)(2,1)}, bf16[4,2,64,640]{3,2,1,0:T(8,128)(2,1)}, bf16[4,2,64,640]{3,2,1,0:T(8,128)(2,1)}) custom-call(s32[4]{0:T(128)} %pad_add_fusion.place_ref, bf16[4,2,2,2,64,640]{5,4,3,2,1,0:T(8,128)(2,1)} %bitcast.31, bf16[4,2,2,2,64,640]{5,4,3,2,1,0:T(8,128)(2,1)} %bitcast.32), custom_call_target="tpu_custom_call" | custom-call | bytes 196608 | tf_op jit(solution)/shard_map/fold_cores/pallas_call | solution.py:262
  303.5 1.5 collective-permute-start.40
  310.8 19.9 %input_grad.1 = bf16[1024,1280]{1,0:T(8,128)(2,1)} custom-call(bf16[1024,1280]{1,0:T(8,128)(2,1)} %x_ref.3, f32[8,1280]{1,0:T(8,128)} %broadcast_in_dim.29.gain_ref, f32[1024,1280]{1,0:T(8,128)} %get-tuple-element.193.hidden_ref, bf16[1024,1920]{1,0:T(8,128)(2,1)} %get-tuple-element.165.right_ref.grad_a, ...), custom_call_target="tpu_custom_call" | custom-call | flops 251658240 | bytes 704512 | tf_op jit(solution)/shard_map/input_grad/pallas_call | solution.py:262
  331.4 2.2 fold_second.2
  333.6 1.9 collective-permute-start.42
  335.6 1.9 collective-permute-start.43
  338.3 3.8 fold_first.3
  342.1 1.2 collective-permute-start.47
  343.8 7.9 %add_convert_fusion = bf16[1024,1280]{1,0:T(8,128)(2,1)} fusion(f32[1024,1280]{1,0:T(8,128)S(1)} %bitcast.30, bf16[1024,1280]{1,0:T(8,128)(2,1)} %get-tuple-element.203, bf16[1280,1280]{1,0:T(8,128)(2,1)} %get-tuple-element.156.refs_1_, f32[1280]{0:T(1024)} %reshape.89), kind=kOutput, calls=%fused_computation | convolution fusion | flops 3359375360 | bytes 13767680 | tf_op jit(solution)/shard_map/dot_general | solution.py:45
  352.4 1.9 fold_planes.2.refs_0_
  355.7 2.2 fold_second.3
  358.4 1.2 collective-permute-start.50
  359.6 2.9 collective-permute-start.51
  362.5 1.5 collective-permute-start.46
  364.0 1.2 collective-permute-start.45
  365.2 1.9 collective-permute-done.49.refs_1_
  368.0 2.7 collective-permute-done.50.refs_2_
  370.7 4.5 %all-reduce.7.cloned.1.call-done = bf16[480,1280]{1,0:T(8,128)(2,1)} async-done(((bf16[480,1280]{1,0:T(8,128)(2,1)}), bf16[480,1280]{1,0:T(8,128)(2,1)}) %all-reduce.7.cloned.1.call-update) | async-done | bytes 1228816 | tf_op jit(solution)/shard_map/psum | solution.py:895
  375.2 1.9 fold_planes.3.refs_4_
  377.2 1.7 collective-permute-start.54
  378.9 1.3 collective-permute-start.53
  380.3 2.8 multiply_reduce_fusion
  384.2 3.4 collective-permute-done.53.refs_6_
  389.2 3.2 finish.1
  392.3 1.2 slice_bitcast_fusion
  393.5 1.3 fusion.11
  394.9 1.3 multiply_reduce_fusion.3
  396.2 1.6 multiply_reduce_fusion.1
  (237 shorter events, 40.1 us)
Async XLA Ops:
  7.2 69.4 %copy-start.52 = (bf16[80]{0:T(256)(128)(2,1)S(1)}, bf16[80]{0:T(256)(128)(2,1)}, u32[]{:S(2)}) copy-start(bf16[80]{0:T(256)(128)(2,1)} %param.27) | copy-start | bytes 484
  7.2 298.8 %reduce-scatter.8.cloned.1.call-start = ((), (), s32[]{:S(2)}) async-start(), calls=%async_computation.5 | async-start | bytes 3686400 | tf_op jit(solution)/shard_map/reduce_scatter | solution.py:866
  12.7 10.0 %collective-permute-start.2 = (bf16[128,640]{1,0:T(8,128)(2,1)}, bf16[128,640]{1,0:T(8,128)(2,1)S(1)}, u32[]{:S(2)}, u32[]{:S(2)}) collective-permute-start(bf16[128,640]{1,0:T(8,128)(2,1)} %get-tuple-element.120), channel_id=1, source_target_pairs={{0,6},{1,7},{2,0},{3,1},{4,2},{5,3},{6,4},{7,5},{8,14},{9,15},{10,... | collective-permute-start | bytes 491528 | tf_op jit(solution)/shard_map/ppermute | solution.py:252
  17.7 14.1 %collective-permute-start.1 = (bf16[128,640]{1,0:T(8,128)(2,1)}, bf16[128,640]{1,0:T(8,128)(2,1)S(1)}, u32[]{:S(2)}, u32[]{:S(2)}) collective-permute-start(bf16[128,640]{1,0:T(8,128)(2,1)} %get-tuple-element.120), channel_id=1, source_target_pairs={{0,4},{1,5},{2,6},{3,7},{4,0},{5,1},{6,2},{7,3},{8,12},{9,13},{10,... | collective-permute-start | bytes 491528 | tf_op jit(solution)/shard_map/ppermute | solution.py:252
  17.7 14.1 %collective-permute-start = (bf16[128,640]{1,0:T(8,128)(2,1)}, bf16[128,640]{1,0:T(8,128)(2,1)S(1)}, u32[]{:S(2)}, u32[]{:S(2)}) collective-permute-start(bf16[128,640]{1,0:T(8,128)(2,1)} %get-tuple-element.120), channel_id=1, source_target_pairs={{0,2},{1,3},{2,4},{3,5},{4,6},{5,7},{6,0},{7,1},{8,10},{9,11},{10,... | collective-permute-start | bytes 491528 | tf_op jit(solution)/shard_map/ppermute | solution.py:252
  31.8 7.4 %collective-permute-start.13 = (bf16[128,640]{1,0:T(8,128)(2,1)}, bf16[128,640]{1,0:T(8,128)(2,1)S(1)}, u32[]{:S(2)}, u32[]{:S(2)}) collective-permute-start(bf16[128,640]{1,0:T(8,128)(2,1)} %get-tuple-element.126), channel_id=1, source_target_pairs={{0,6},{1,7},{2,0},{3,1},{4,2},{5,3},{6,4},{7,5},{8,14},{9,15},{10,... | collective-permute-start | bytes 491528 | tf_op jit(solution)/shard_map/ppermute | solution.py:252
  32.9 16.1 %collective-permute-start.12 = (bf16[128,640]{1,0:T(8,128)(2,1)}, bf16[128,640]{1,0:T(8,128)(2,1)S(1)}, u32[]{:S(2)}, u32[]{:S(2)}) collective-permute-start(bf16[128,640]{1,0:T(8,128)(2,1)} %get-tuple-element.126), channel_id=1, source_target_pairs={{0,4},{1,5},{2,6},{3,7},{4,0},{5,1},{6,2},{7,3},{8,12},{9,13},{10,... | collective-permute-start | bytes 491528 | tf_op jit(solution)/shard_map/ppermute | solution.py:252
  34.6 14.3 %collective-permute-start.11 = (bf16[128,640]{1,0:T(8,128)(2,1)}, bf16[128,640]{1,0:T(8,128)(2,1)S(1)}, u32[]{:S(2)}, u32[]{:S(2)}) collective-permute-start(bf16[128,640]{1,0:T(8,128)(2,1)} %get-tuple-element.126), channel_id=1, source_target_pairs={{0,2},{1,3},{2,4},{3,5},{4,6},{5,7},{6,0},{7,1},{8,10},{9,11},{10,... | collective-permute-start | bytes 491528 | tf_op jit(solution)/shard_map/ppermute | solution.py:252
  36.7 41.0 %copy-start.6 = (bf16[3,128,640]{2,1,0:T(8,128)(2,1)}, bf16[3,128,640]{2,1,0:T(8,128)(2,1)S(1)}, u32[]{:S(2)}) copy-start(bf16[3,128,640]{2,1,0:T(8,128)(2,1)S(1)} %pad_maximum_fusion.1.refs_1_) | copy-start | bytes 1474564
  36.7 34.0 %collective-permute-start.5 = (bf16[3,128,640]{2,1,0:T(8,128)(2,1)S(1)}, bf16[3,128,640]{2,1,0:T(8,128)(2,1)S(1)}, u32[]{:S(2)}, u32[]{:S(2)}) collective-permute-start(bf16[3,128,640]{2,1,0:T(8,128)(2,1)S(1)} %pad_maximum_fusion.1.refs_1_), channel_id=1, source_target_pairs={{0,24},{8,16},{16,8},{24,0},{1,25},{9,17},{17,9},{25,1},{2,26},{10... | collective-permute-start | bytes 1474568 | tf_op jit(solution)/shard_map/ppermute | solution.py:258
  49.0 8.0 %collective-permute-start.16 = (bf16[240,640]{1,0:T(8,128)(2,1)}, bf16[240,640]{1,0:T(8,128)(2,1)S(1)}, u32[]{:S(2)}, u32[]{:S(2)}) collective-permute-start(bf16[240,640]{1,0:T(8,128)(2,1)} %get-tuple-element.127), channel_id=1, source_target_pairs={{0,6},{1,7},{2,0},{3,1},{4,2},{5,3},{6,4},{7,5},{8,14},{9,15},{10,... | collective-permute-start | bytes 921608 | tf_op jit(solution)/shard_map/ppermute | solution.py:252
  49.0 22.2 %collective-permute-start.4 = (bf16[3,128,640]{2,1,0:T(8,128)(2,1)S(1)}, bf16[3,128,640]{2,1,0:T(8,128)(2,1)S(1)}, u32[]{:S(2)}, u32[]{:S(2)}) collective-permute-start(bf16[3,128,640]{2,1,0:T(8,128)(2,1)S(1)} %pad_maximum_fusion.1.refs_1_), channel_id=1, source_target_pairs={{0,16},{8,24},{16,0},{24,8},{1,17},{9,25},{17,1},{25,9},{2,18},{10... | collective-permute-start | bytes 1474568 | tf_op jit(solution)/shard_map/ppermute | solution.py:258
  50.5 20.8 %collective-permute-start.3 = (bf16[3,128,640]{2,1,0:T(8,128)(2,1)S(1)}, bf16[3,128,640]{2,1,0:T(8,128)(2,1)S(1)}, u32[]{:S(2)}, u32[]{:S(2)}) collective-permute-start(bf16[3,128,640]{2,1,0:T(8,128)(2,1)S(1)} %pad_maximum_fusion.1.refs_1_), channel_id=1, source_target_pairs={{0,8},{8,0},{16,24},{24,16},{1,9},{9,1},{17,25},{25,17},{2,10},{10... | collective-permute-start | bytes 1474568 | tf_op jit(solution)/shard_map/ppermute | solution.py:258
  52.0 18.7 %collective-permute-start.15 = (bf16[240,640]{1,0:T(8,128)(2,1)}, bf16[240,640]{1,0:T(8,128)(2,1)S(1)}, u32[]{:S(2)}, u32[]{:S(2)}) collective-permute-start(bf16[240,640]{1,0:T(8,128)(2,1)} %get-tuple-element.127), channel_id=1, source_target_pairs={{0,4},{1,5},{2,6},{3,7},{4,0},{5,1},{6,2},{7,3},{8,12},{9,13},{10,... | collective-permute-start | bytes 921608 | tf_op jit(solution)/shard_map/ppermute | solution.py:252
  57.0 18.0 %collective-permute-start.6 = (bf16[512,640]{1,0:T(8,128)(2,1)}, bf16[512,640]{1,0:T(8,128)(2,1)S(1)}, u32[]{:S(2)}, u32[]{:S(2)}) collective-permute-start(bf16[512,640]{1,0:T(8,128)(2,1)} %get-tuple-element.119.refs_0_), channel_id=1, source_target_pairs={{0,1},{1,0},{2,3},{3,2},{4,5},{5,4},{6,7},{7,6},{8,9},{9,8},{10,11... | collective-permute-start | bytes 1966088 | tf_op jit(solution)/shard_map/ppermute | solution.py:255
  70.7 1.9 collective-permute-start.7
  70.7 4.8 %collective-permute-start.10 = (bf16[3,128,640]{2,1,0:T(8,128)(2,1)S(1)}, bf16[3,128,640]{2,1,0:T(8,128)(2,1)S(1)}, u32[]{:S(2)}, u32[]{:S(2)}) collective-permute-start(bf16[3,128,640]{2,1,0:T(8,128)(2,1)S(1)} %collective-permute-done.5.refs_4_), channel_id=1, source_target_pairs={{0,1},{1,0},{2,3},{3,2},{4,5},{5,4},{6,7},{7,6},{8,9},{9,8},{10,11... | collective-permute-start | bytes 1474568 | tf_op jit(solution)/shard_map/ppermute | solution.py:255
  71.2 4.8 %collective-permute-start.9 = (bf16[3,128,640]{2,1,0:T(8,128)(2,1)S(1)}, bf16[3,128,640]{2,1,0:T(8,128)(2,1)S(1)}, u32[]{:S(2)}, u32[]{:S(2)}) collective-permute-start(bf16[3,128,640]{2,1,0:T(8,128)(2,1)S(1)} %collective-permute-done.4.refs_3_), channel_id=1, source_target_pairs={{0,1},{1,0},{2,3},{3,2},{4,5},{5,4},{6,7},{7,6},{8,9},{9,8},{10,11... | collective-permute-start | bytes 1474568 | tf_op jit(solution)/shard_map/ppermute | solution.py:255
  71.3 4.9 %collective-permute-start.8 = (bf16[3,128,640]{2,1,0:T(8,128)(2,1)S(1)}, bf16[3,128,640]{2,1,0:T(8,128)(2,1)S(1)}, u32[]{:S(2)}, u32[]{:S(2)}) collective-permute-start(bf16[3,128,640]{2,1,0:T(8,128)(2,1)S(1)} %collective-permute-done.3.refs_2_), channel_id=1, source_target_pairs={{0,1},{1,0},{2,3},{3,2},{4,5},{5,4},{6,7},{7,6},{8,9},{9,8},{10,11... | collective-permute-start | bytes 1474568 | tf_op jit(solution)/shard_map/ppermute | solution.py:255
  72.5 21.5 %collective-permute-start.22 = (bf16[3,128,640]{2,1,0:T(8,128)(2,1)S(1)}, bf16[3,128,640]{2,1,0:T(8,128)(2,1)}, u32[]{:S(2)}, u32[]{:S(2)}) collective-permute-start(bf16[3,128,640]{2,1,0:T(8,128)(2,1)S(1)} %pad_maximum_fusion.2.refs_1_), channel_id=1, source_target_pairs={{0,24},{8,16},{16,8},{24,0},{1,25},{9,17},{17,9},{25,1},{2,26},{10... | collective-permute-start | bytes 1474568 | tf_op jit(solution)/shard_map/ppermute | solution.py:258
  75.0 22.3 %collective-permute-start.21 = (bf16[3,128,640]{2,1,0:T(8,128)(2,1)S(1)}, bf16[3,128,640]{2,1,0:T(8,128)(2,1)}, u32[]{:S(2)}, u32[]{:S(2)}) collective-permute-start(bf16[3,128,640]{2,1,0:T(8,128)(2,1)S(1)} %pad_maximum_fusion.2.refs_1_), channel_id=1, source_target_pairs={{0,16},{8,24},{16,0},{24,8},{1,17},{9,25},{17,1},{25,9},{2,18},{10... | collective-permute-start | bytes 1474568 | tf_op jit(solution)/shard_map/ppermute | solution.py:258
  75.5 21.9 %collective-permute-start.20 = (bf16[3,128,640]{2,1,0:T(8,128)(2,1)S(1)}, bf16[3,128,640]{2,1,0:T(8,128)(2,1)}, u32[]{:S(2)}, u32[]{:S(2)}) collective-permute-start(bf16[3,128,640]{2,1,0:T(8,128)(2,1)S(1)} %pad_maximum_fusion.2.refs_1_), channel_id=1, source_target_pairs={{0,8},{8,0},{16,24},{24,16},{1,9},{9,1},{17,25},{25,17},{2,10},{10... | collective-permute-start | bytes 1474568 | tf_op jit(solution)/shard_map/ppermute | solution.py:258
  76.1 26.0 %collective-permute-start.23 = (bf16[512,640]{1,0:T(8,128)(2,1)}, bf16[512,640]{1,0:T(8,128)(2,1)S(1)}, u32[]{:S(2)}, u32[]{:S(2)}) collective-permute-start(bf16[512,640]{1,0:T(8,128)(2,1)} %get-tuple-element.136.refs_0_), channel_id=1, source_target_pairs={{0,1},{1,0},{2,3},{3,2},{4,5},{5,4},{6,7},{7,6},{8,9},{9,8},{10,11... | collective-permute-start | bytes 1966088 | tf_op jit(solution)/shard_map/ppermute | solution.py:255
  76.2 17.9 %collective-permute-start.14 = (bf16[240,640]{1,0:T(8,128)(2,1)}, bf16[240,640]{1,0:T(8,128)(2,1)}, u32[]{:S(2)}, u32[]{:S(2)}) collective-permute-start(bf16[240,640]{1,0:T(8,128)(2,1)} %get-tuple-element.127), channel_id=1, source_target_pairs={{0,2},{1,3},{2,4},{3,5},{4,6},{5,7},{6,0},{7,1},{8,10},{9,11},{10,... | collective-permute-start | bytes 921608 | tf_op jit(solution)/shard_map/ppermute | solution.py:252
  97.4 5.2 %collective-permute-start.24 = (bf16[3,128,640]{2,1,0:T(8,128)(2,1)S(1)}, bf16[3,128,640]{2,1,0:T(8,128)(2,1)S(1)}, u32[]{:S(2)}, u32[]{:S(2)}) collective-permute-start(bf16[3,128,640]{2,1,0:T(8,128)(2,1)S(1)} %pad_maximum_fusion.2.refs_1_), channel_id=1, source_target_pairs={{0,1},{1,0},{2,3},{3,2},{4,5},{5,4},{6,7},{7,6},{8,9},{9,8},{10,11... | collective-permute-start | bytes 1474568 | tf_op jit(solution)/shard_map/ppermute | solution.py:255
  97.4 5.2 %collective-permute-start.25 = (bf16[3,128,640]{2,1,0:T(8,128)(2,1)}, bf16[3,128,640]{2,1,0:T(8,128)(2,1)S(1)}, u32[]{:S(2)}, u32[]{:S(2)}) collective-permute-start(bf16[3,128,640]{2,1,0:T(8,128)(2,1)} %collective-permute-done.20.refs_2_), channel_id=1, source_target_pairs={{0,1},{1,0},{2,3},{3,2},{4,5},{5,4},{6,7},{7,6},{8,9},{9,8},{10,11... | collective-permute-start | bytes 1474568 | tf_op jit(solution)/shard_map/ppermute | solution.py:255
  99.0 46.7 %copy-start = (bf16[3,240,640]{2,1,0:T(8,128)(2,1)}, bf16[3,240,640]{2,1,0:T(8,128)(2,1)S(1)}, u32[]{:S(2)}) copy-start(bf16[3,240,640]{2,1,0:T(8,128)(2,1)S(1)} %pad_maximum_fusion.refs_1_) | copy-start | bytes 2764804
  99.1 46.7 %collective-permute-start.19 = (bf16[3,240,640]{2,1,0:T(8,128)(2,1)S(1)}, bf16[3,240,640]{2,1,0:T(8,128)(2,1)}, u32[]{:S(2)}, u32[]{:S(2)}) collective-permute-start(bf16[3,240,640]{2,1,0:T(8,128)(2,1)S(1)} %pad_maximum_fusion.refs_1_), channel_id=1, source_target_pairs={{0,24},{8,16},{16,8},{24,0},{1,25},{9,17},{17,9},{25,1},{2,26},{10... | collective-permute-start | bytes 2764808 | tf_op jit(solution)/shard_map/ppermute | solution.py:258
  100.8 45.0 %collective-permute-start.18 = (bf16[3,240,640]{2,1,0:T(8,128)(2,1)S(1)}, bf16[3,240,640]{2,1,0:T(8,128)(2,1)}, u32[]{:S(2)}, u32[]{:S(2)}) collective-permute-start(bf16[3,240,640]{2,1,0:T(8,128)(2,1)S(1)} %pad_maximum_fusion.refs_1_), channel_id=1, source_target_pairs={{0,16},{8,24},{16,0},{24,8},{1,17},{9,25},{17,1},{25,9},{2,18},{10... | collective-permute-start | bytes 2764808 | tf_op jit(solution)/shard_map/ppermute | solution.py:258
  102.1 43.7 %collective-permute-start.17 = (bf16[3,240,640]{2,1,0:T(8,128)(2,1)S(1)}, bf16[3,240,640]{2,1,0:T(8,128)(2,1)}, u32[]{:S(2)}, u32[]{:S(2)}) collective-permute-start(bf16[3,240,640]{2,1,0:T(8,128)(2,1)S(1)} %pad_maximum_fusion.refs_1_), channel_id=1, source_target_pairs={{0,8},{8,0},{16,24},{24,16},{1,9},{9,1},{17,25},{25,17},{2,10},{10... | collective-permute-start | bytes 2764808 | tf_op jit(solution)/shard_map/ppermute | solution.py:258
  102.6 2.1 collective-permute-start.26
  102.7 15.6 %collective-permute-start.27 = (bf16[3,128,640]{2,1,0:T(8,128)(2,1)}, bf16[3,128,640]{2,1,0:T(8,128)(2,1)S(1)}, u32[]{:S(2)}, u32[]{:S(2)}) collective-permute-start(bf16[3,128,640]{2,1,0:T(8,128)(2,1)} %collective-permute-done.22.refs_4_), channel_id=1, source_target_pairs={{0,1},{1,0},{2,3},{3,2},{4,5},{5,4},{6,7},{7,6},{8,9},{9,8},{10,11... | collective-permute-start | bytes 1474568 | tf_op jit(solution)/shard_map/ppermute | solution.py:255
  104.7 45.2 %collective-permute-start.28 = (bf16[960,640]{1,0:T(8,128)(2,1)S(1)}, bf16[960,640]{1,0:T(8,128)(2,1)}, u32[]{:S(2)}, u32[]{:S(2)}) collective-permute-start(bf16[960,640]{1,0:T(8,128)(2,1)S(1)} %copy-done.11), channel_id=1, source_target_pairs={{0,1},{1,0},{2,3},{3,2},{4,5},{5,4},{6,7},{7,6},{8,9},{9,8},{10,11... | collective-permute-start | bytes 3686408 | tf_op jit(solution)/shard_map/ppermute | solution.py:255
  145.8 4.1 %collective-permute-start.29 = (bf16[3,240,640]{2,1,0:T(8,128)(2,1)S(1)}, bf16[3,240,640]{2,1,0:T(8,128)(2,1)}, u32[]{:S(2)}, u32[]{:S(2)}) collective-permute-start(bf16[3,240,640]{2,1,0:T(8,128)(2,1)S(1)} %pad_maximum_fusion.refs_1_), channel_id=1, source_target_pairs={{0,1},{1,0},{2,3},{3,2},{4,5},{5,4},{6,7},{7,6},{8,9},{9,8},{10,11... | collective-permute-start | bytes 2764808 | tf_op jit(solution)/shard_map/ppermute | solution.py:255
  146.2 3.8 collective-permute-start.30
  146.3 4.9 %collective-permute-start.31 = (bf16[3,240,640]{2,1,0:T(8,128)(2,1)}, bf16[3,240,640]{2,1,0:T(8,128)(2,1)}, u32[]{:S(2)}, u32[]{:S(2)}) collective-permute-start(bf16[3,240,640]{2,1,0:T(8,128)(2,1)} %collective-permute-done.18.refs_3_), channel_id=1, source_target_pairs={{0,1},{1,0},{2,3},{3,2},{4,5},{5,4},{6,7},{7,6},{8,9},{9,8},{10,11... | collective-permute-start | bytes 2764808 | tf_op jit(solution)/shard_map/ppermute | solution.py:255
  146.7 5.9 %collective-permute-start.32 = (bf16[3,240,640]{2,1,0:T(8,128)(2,1)}, bf16[3,240,640]{2,1,0:T(8,128)(2,1)}, u32[]{:S(2)}, u32[]{:S(2)}) collective-permute-start(bf16[3,240,640]{2,1,0:T(8,128)(2,1)} %collective-permute-done.19.refs_4_), channel_id=1, source_target_pairs={{0,1},{1,0},{2,3},{3,2},{4,5},{5,4},{6,7},{7,6},{8,9},{9,8},{10,11... | collective-permute-start | bytes 2764808 | tf_op jit(solution)/shard_map/ppermute | solution.py:255
  178.2 127.8 %reduce-scatter.4.cloned.1.call-start = ((), (), s32[]{:S(2)}) async-start(), calls=%async_computation.3 | async-start | bytes 3686400 | tf_op jit(solution)/shard_map/reduce_scatter | solution.py:866
  206.6 99.4 %reduce-scatter.6.cloned.1.call-start = ((), (), s32[]{:S(2)}) async-start(), calls=%async_computation.4 | async-start | bytes 3686400 | tf_op jit(solution)/shard_map/reduce_scatter | solution.py:866
  207.4 167.9 %all-reduce.7.cloned.1.call-start = ((), (), s32[]{:S(2)}) async-start(), calls=%async_computation.6 | async-start | bytes 2457600 | tf_op jit(solution)/shard_map/psum | solution.py:895
  242.1 5.2 %collective-permute-start.33 = (bf16[4,512,640]{2,1,0:T(8,128)(2,1)}, bf16[4,512,640]{2,1,0:T(8,128)(2,1)S(1)}, u32[]{:S(2)}, u32[]{:S(2)}) collective-permute-start(bf16[4,512,640]{2,1,0:T(8,128)(2,1)} %get-tuple-element.168), channel_id=1, source_target_pairs={{0,1},{1,0},{2,3},{3,2},{4,5},{5,4},{6,7},{7,6},{8,9},{9,8},{10,11... | collective-permute-start | bytes 7864328 | tf_op jit(solution)/shard_map/ppermute | solution.py:255
  253.5 23.5 %collective-permute-start.35 = (bf16[4,2,64,640]{3,2,1,0:T(8,128)(2,1)}, bf16[4,2,64,640]{3,2,1,0:T(8,128)(2,1)S(1)}, u32[]{:S(2)}, u32[]{:S(2)}) collective-permute-start(bf16[4,2,64,640]{3,2,1,0:T(8,128)(2,1)} %get-tuple-element.172), channel_id=1, source_target_pairs={{0,16},{8,24},{16,0},{24,8},{1,17},{9,25},{17,1},{25,9},{2,18},{10... | collective-permute-start | bytes 1966088 | tf_op jit(solution)/shard_map/ppermute | solution.py:258
  255.0 22.0 %collective-permute-start.34 = (bf16[4,2,64,640]{3,2,1,0:T(8,128)(2,1)}, bf16[4,2,64,640]{3,2,1,0:T(8,128)(2,1)S(1)}, u32[]{:S(2)}, u32[]{:S(2)}) collective-permute-start(bf16[4,2,64,640]{3,2,1,0:T(8,128)(2,1)} %get-tuple-element.169), channel_id=1, source_target_pairs={{0,8},{8,0},{16,24},{24,16},{1,9},{9,1},{17,25},{25,17},{2,10},{10... | collective-permute-start | bytes 1966088 | tf_op jit(solution)/shard_map/ppermute | solution.py:258
  290.5 6.9 %collective-permute-start.36 = (bf16[4,512,640]{2,1,0:T(8,128)(2,1)}, bf16[4,512,640]{2,1,0:T(8,128)(2,1)S(1)}, u32[]{:S(2)}, u32[]{:S(2)}) collective-permute-start(bf16[4,512,640]{2,1,0:T(8,128)(2,1)} %get-tuple-element.177), channel_id=1, source_target_pairs={{0,1},{1,0},{2,3},{3,2},{4,5},{5,4},{6,7},{7,6},{8,9},{9,8},{10,11... | collective-permute-start | bytes 7864328 | tf_op jit(solution)/shard_map/ppermute | solution.py:255
  295.7 35.0 %collective-permute-start.39 = (bf16[4,64,640]{2,1,0:T(8,128)(2,1)}, bf16[4,64,640]{2,1,0:T(8,128)(2,1)S(1)}, u32[]{:S(2)}, u32[]{:S(2)}) collective-permute-start(bf16[4,64,640]{2,1,0:T(8,128)(2,1)} %get-tuple-element.197), channel_id=1, source_target_pairs={{0,8},{8,0},{16,24},{24,16},{1,9},{9,1},{17,25},{25,17},{2,10},{10... | collective-permute-start | bytes 983048 | tf_op jit(solution)/shard_map/ppermute | solution.py:258
  296.8 33.9 %collective-permute-start.38 = (bf16[4,64,640]{2,1,0:T(8,128)(2,1)}, bf16[4,64,640]{2,1,0:T(8,128)(2,1)}, u32[]{:S(2)}, u32[]{:S(2)}) collective-permute-start(bf16[4,64,640]{2,1,0:T(8,128)(2,1)} %get-tuple-element.181), channel_id=1, source_target_pairs={{0,16},{8,24},{16,0},{24,8},{1,17},{9,25},{17,1},{25,9},{2,18},{10... | collective-permute-start | bytes 983048 | tf_op jit(solution)/shard_map/ppermute | solution.py:258
  303.5 33.9 %collective-permute-start.40 = (bf16[4,2,64,640]{3,2,1,0:T(8,128)(2,1)}, bf16[4,2,64,640]{3,2,1,0:T(8,128)(2,1)S(1)}, u32[]{:S(2)}, u32[]{:S(2)}) collective-permute-start(bf16[4,2,64,640]{3,2,1,0:T(8,128)(2,1)} %get-tuple-element.201), channel_id=1, source_target_pairs={{0,16},{8,24},{16,0},{24,8},{1,17},{9,25},{17,1},{25,9},{2,18},{10... | collective-permute-start | bytes 1966088 | tf_op jit(solution)/shard_map/ppermute | solution.py:258
  305.0 32.5 %collective-permute-start.37 = (bf16[4,2,64,640]{3,2,1,0:T(8,128)(2,1)}, bf16[4,2,64,640]{3,2,1,0:T(8,128)(2,1)}, u32[]{:S(2)}, u32[]{:S(2)}) collective-permute-start(bf16[4,2,64,640]{3,2,1,0:T(8,128)(2,1)} %get-tuple-element.184), channel_id=1, source_target_pairs={{0,8},{8,0},{16,24},{24,16},{1,9},{9,1},{17,25},{25,17},{2,10},{10... | collective-permute-start | bytes 1966088 | tf_op jit(solution)/shard_map/ppermute | solution.py:258
  310.8 33.0 %slice-start = ((s8[5242880]{0:T(1024)(128)(4,1)}), s8[4194304]{0:T(1024)(128)(4,1)S(1)}, s32[]{:S(2)}) async-start(s8[5242880]{0:T(1024)(128)(4,1)} %bitcast.29), calls=%async_computation.7 | async-start | bytes 8388608
  310.8 33.0 %slice-start.1 = ((s8[5242880]{0:T(1024)(128)(4,1)}), s8[1048576]{0:T(1024)(128)(4,1)S(1)}, s32[]{:S(2)}) async-start(s8[5242880]{0:T(1024)(128)(4,1)} %bitcast.29), calls=%async_computation.8 | async-start | bytes 2097152
  333.6 18.1 %collective-permute-start.41 = (bf16[2,64,640]{2,1,0:T(8,128)(2,1)}, bf16[2,64,640]{2,1,0:T(8,128)(2,1)S(1)}, u32[]{:S(2)}, u32[]{:S(2)}) collective-permute-start(bf16[2,64,640]{2,1,0:T(8,128)(2,1)} %get-tuple-element.204), channel_id=1, source_target_pairs={{0,2},{1,3},{2,4},{3,5},{4,6},{5,7},{6,0},{7,1},{8,10},{9,11},{10,... | collective-permute-start | bytes 491528 | tf_op jit(solution)/shard_map/ppermute | solution.py:252
  333.6 18.1 %collective-permute-start.42 = (bf16[2,64,640]{2,1,0:T(8,128)(2,1)}, bf16[2,64,640]{2,1,0:T(8,128)(2,1)S(1)}, u32[]{:S(2)}, u32[]{:S(2)}) collective-permute-start(bf16[2,64,640]{2,1,0:T(8,128)(2,1)} %get-tuple-element.205), channel_id=1, source_target_pairs={{0,4},{1,5},{2,6},{3,7},{4,0},{5,1},{6,2},{7,3},{8,12},{9,13},{10,... | collective-permute-start | bytes 491528 | tf_op jit(solution)/shard_map/ppermute | solution.py:252
  335.6 16.2 %collective-permute-start.43 = (bf16[2,64,640]{2,1,0:T(8,128)(2,1)}, bf16[2,64,640]{2,1,0:T(8,128)(2,1)}, u32[]{:S(2)}, u32[]{:S(2)}) collective-permute-start(bf16[2,64,640]{2,1,0:T(8,128)(2,1)} %get-tuple-element.206), channel_id=1, source_target_pairs={{0,6},{1,7},{2,0},{3,1},{4,2},{5,3},{6,4},{7,5},{8,14},{9,15},{10,... | collective-permute-start | bytes 491528 | tf_op jit(solution)/shard_map/ppermute | solution.py:252
  342.1 12.2 %collective-permute-start.47 = (bf16[4,64,640]{2,1,0:T(8,128)(2,1)}, bf16[4,64,640]{2,1,0:T(8,128)(2,1)S(1)}, u32[]{:S(2)}, u32[]{:S(2)}) collective-permute-start(bf16[4,64,640]{2,1,0:T(8,128)(2,1)} %get-tuple-element.202), channel_id=1, source_target_pairs={{0,16},{8,24},{16,0},{24,8},{1,17},{9,25},{17,1},{25,9},{2,18},{10... | collective-permute-start | bytes 983048 | tf_op jit(solution)/shard_map/ppermute | solution.py:258
  343.2 11.7 %collective-permute-start.48 = (bf16[4,64,640]{2,1,0:T(8,128)(2,1)}, bf16[4,64,640]{2,1,0:T(8,128)(2,1)S(1)}, u32[]{:S(2)}, u32[]{:S(2)}) collective-permute-start(bf16[4,64,640]{2,1,0:T(8,128)(2,1)} %get-tuple-element.213), channel_id=1, source_target_pairs={{0,8},{8,0},{16,24},{24,16},{1,9},{9,1},{17,25},{25,17},{2,10},{10... | collective-permute-start | bytes 983048 | tf_op jit(solution)/shard_map/ppermute | solution.py:258
  357.8 9.2 %collective-permute-start.49 = (bf16[2,64,640]{2,1,0:T(8,128)(2,1)}, bf16[2,64,640]{2,1,0:T(8,128)(2,1)S(1)}, u32[]{:S(2)}, u32[]{:S(2)}) collective-permute-start(bf16[2,64,640]{2,1,0:T(8,128)(2,1)} %get-tuple-element.215), channel_id=1, source_target_pairs={{0,2},{1,3},{2,4},{3,5},{4,6},{5,7},{6,0},{7,1},{8,10},{9,11},{10,... | collective-permute-start | bytes 491528 | tf_op jit(solution)/shard_map/ppermute | solution.py:252
  358.4 12.3 %collective-permute-start.50 = (bf16[2,64,640]{2,1,0:T(8,128)(2,1)}, bf16[2,64,640]{2,1,0:T(8,128)(2,1)S(1)}, u32[]{:S(2)}, u32[]{:S(2)}) collective-permute-start(bf16[2,64,640]{2,1,0:T(8,128)(2,1)} %get-tuple-element.216), channel_id=1, source_target_pairs={{0,4},{1,5},{2,6},{3,7},{4,0},{5,1},{6,2},{7,3},{8,12},{9,13},{10,... | collective-permute-start | bytes 491528 | tf_op jit(solution)/shard_map/ppermute | solution.py:252
  359.6 11.1 %collective-permute-start.51 = (bf16[2,64,640]{2,1,0:T(8,128)(2,1)}, bf16[2,64,640]{2,1,0:T(8,128)(2,1)S(1)}, u32[]{:S(2)}, u32[]{:S(2)}) collective-permute-start(bf16[2,64,640]{2,1,0:T(8,128)(2,1)} %get-tuple-element.217), channel_id=1, source_target_pairs={{0,6},{1,7},{2,0},{3,1},{4,2},{5,3},{6,4},{7,5},{8,14},{9,15},{10,... | collective-permute-start | bytes 491528 | tf_op jit(solution)/shard_map/ppermute | solution.py:252
  362.5 20.6 %collective-permute-start.46 = (bf16[2,64,640]{2,1,0:T(8,128)(2,1)}, bf16[2,64,640]{2,1,0:T(8,128)(2,1)S(1)}, u32[]{:S(2)}, u32[]{:S(2)}) collective-permute-start(bf16[2,64,640]{2,1,0:T(8,128)(2,1)} %fold_planes.2.refs_0_), channel_id=1, source_target_pairs={{0,24},{8,16},{16,8},{24,0},{1,25},{9,17},{17,9},{25,1},{2,26},{10... | collective-permute-start | bytes 491528 | tf_op jit(solution)/shard_map/ppermute | solution.py:258
  364.0 20.2 %collective-permute-start.45 = (bf16[2,64,640]{2,1,0:T(8,128)(2,1)}, bf16[2,64,640]{2,1,0:T(8,128)(2,1)S(1)}, u32[]{:S(2)}, u32[]{:S(2)}) collective-permute-start(bf16[2,64,640]{2,1,0:T(8,128)(2,1)} %fold_planes.2.refs_0_), channel_id=1, source_target_pairs={{0,16},{8,24},{16,0},{24,8},{1,17},{9,25},{17,1},{25,9},{2,18},{10... | collective-permute-start | bytes 491528 | tf_op jit(solution)/shard_map/ppermute | solution.py:258
  367.0 17.2 %collective-permute-start.44 = (bf16[2,64,640]{2,1,0:T(8,128)(2,1)}, bf16[2,64,640]{2,1,0:T(8,128)(2,1)S(1)}, u32[]{:S(2)}, u32[]{:S(2)}) collective-permute-start(bf16[2,64,640]{2,1,0:T(8,128)(2,1)} %fold_planes.2.refs_0_), channel_id=1, source_target_pairs={{0,8},{8,0},{16,24},{24,16},{1,9},{9,1},{17,25},{25,17},{2,10},{10... | collective-permute-start | bytes 491528 | tf_op jit(solution)/shard_map/ppermute | solution.py:258
  377.2 7.0 %collective-permute-start.54 = (bf16[2,64,640]{2,1,0:T(8,128)(2,1)}, bf16[2,64,640]{2,1,0:T(8,128)(2,1)S(1)}, u32[]{:S(2)}, u32[]{:S(2)}) collective-permute-start(bf16[2,64,640]{2,1,0:T(8,128)(2,1)} %fold_planes.3.refs_4_), channel_id=1, source_target_pairs={{0,24},{8,16},{16,8},{24,0},{1,25},{9,17},{17,9},{25,1},{2,26},{10... | collective-permute-start | bytes 491528 | tf_op jit(solution)/shard_map/ppermute | solution.py:258
  378.9 8.7 %collective-permute-start.53 = (bf16[2,64,640]{2,1,0:T(8,128)(2,1)}, bf16[2,64,640]{2,1,0:T(8,128)(2,1)S(1)}, u32[]{:S(2)}, u32[]{:S(2)}) collective-permute-start(bf16[2,64,640]{2,1,0:T(8,128)(2,1)} %fold_planes.3.refs_4_), channel_id=1, source_target_pairs={{0,16},{8,24},{16,0},{24,8},{1,17},{9,25},{17,1},{25,9},{2,18},{10... | collective-permute-start | bytes 491528 | tf_op jit(solution)/shard_map/ppermute | solution.py:258
  383.1 5.4 %collective-permute-start.52 = (bf16[2,64,640]{2,1,0:T(8,128)(2,1)S(1)}, bf16[2,64,640]{2,1,0:T(8,128)(2,1)S(1)}, u32[]{:S(2)}, u32[]{:S(2)}) collective-permute-start(bf16[2,64,640]{2,1,0:T(8,128)(2,1)S(1)} %copy-done.14), channel_id=1, source_target_pairs={{0,8},{8,0},{16,24},{24,16},{1,9},{9,1},{17,25},{25,17},{2,10},{10... | collective-permute-start | bytes 491528 | tf_op jit(solution)/shard_map/ppermute | solution.py:258
  (50 other events, 419.1 us)
Sparse Core Ops, SparseCore 0:
  178.3 39.7 reduce-scatter.7
  220.5 40.1 reduce-scatter.3
  263.0 40.2 reduce-scatter.5
  310.3 64.9 all-reduce.6
